TPU v7x, 32 devices: a whole 2x2x4 slice. The times are simulated.
32 devices in a mesh: leaf: 32 (over z, y, x, core).
Axes of the slice: x: 2, y: 2, z: 4, core: 2. Of those that a mesh axis runs over, the one named last changes fastest.
Arguments:
- solution: float32 [32, 98304], P(None, 'leaf'), may hold values from -6 to 6
- residual: float32 [32, 98304], P(None, 'leaf')
- direction: float32 [32, 98304], P(None, 'leaf')
- coordinates: float32 [3, 98304], P(None, 'leaf'), may hold values from 0 to 1
- cluster_order: int32 [98304], P('leaf'), may hold values from 0 to 3071, as said below
- leaf_sizes: int32 [32, 4], P('leaf'), may hold values from 1 to 1024, 3072 in all within a row
- leaf_basis: bfloat16 [128, 98304], P(None, 'leaf'), may hold values from -0.1875 to 0.1875
- node_transfer: bfloat16 [32, 7, 128, 128], P('leaf'), may hold values from -0.375 to 0.375
- node_coupling: bfloat16 [32, 7, 128, 128], P('leaf')
- upper_transfer: bfloat16 [32, 3, 128, 128], P('leaf'), as said below
- upper_coupling: bfloat16 [32, 4, 128, 128], P('leaf'), as said below
- lengthscale: float32 [1], replicated, may hold values from 0.15 to 0.4
- outputscale: float32 [1], replicated, may hold values from 0.05 to 0.2
- noise_variance: float32 [1], replicated, may hold values from 0.5 to 2
Outputs:
- new_solution: float32 [32, 98304], P(None, 'leaf')
- new_residual: float32 [32, 98304], P(None, 'leaf')
- new_direction: float32 [32, 98304], P(None, 'leaf')
Inputs may be any that keep to these rules, and one draw needn't show every extreme that they name: `cluster_order`: each device's block of 3072 entries holds every number of 0 to 3071 once. `leaf_sizes`: each row sums to 3072 and its largest entry is 1024. `upper_transfer`: entry (d, j - 1) is the same for all devices d whose index divided by 2 to the power j is the same. `upper_coupling`: entry (d, j - 1) is the same for all devices d whose index divided by 2 to the power j is the same.
All inputs are finite; a program needn't handle non-finite values.
Results may differ from a plain program's by a relative error of at most 0.0003.
Values sent between devices are 32-bit elements; how exact they have to be, the bound alone decides.
No kernel may reach another device: no remote copies, remote signals or barrier semaphores. Data moves between devices by JAX's collectives and lax.ppermute only.
A program may use at most 64 MiB of HBM per device.

v0:
```python
import jax
import jax.numpy as jnp
from jax import lax
from jax.sharding import PartitionSpec as P

LEAF = 1024


def swapped(array, axis, stride):
    return lax.ppermute(array, axis, [(i, i ^ 1 << stride) for i in range(lax.axis_size(axis))])


def exact_product(form, left, right):
    return jnp.einsum(form, left, right, precision=lax.Precision.HIGHEST)


def matern_block(points, lengthscale, outputscale):
    point_count = points.shape[1]
    squared = jnp.zeros((point_count, point_count), jnp.float32)
    for axis_index in range(3):
        gap_row = points[axis_index][:, None] - points[axis_index][None, :]
        squared = squared + gap_row * gap_row
    scaled = jnp.sqrt(5.0) * jnp.sqrt(squared) / lengthscale
    return outputscale * (1.0 + scaled + scaled * scaled / 3.0) * jnp.exp(-scaled)


def leaf_layout(sizes_row, points_dev):
    leaf_ends = jnp.cumsum(sizes_row)
    starts = leaf_ends - sizes_row
    first_rows = jnp.clip(starts, 0, points_dev - LEAF)
    positions = jnp.arange(points_dev, dtype=jnp.int32)
    leaf_of = jnp.sum((positions[None, :] >= leaf_ends[:, None]).astype(jnp.int32), axis=0)
    return (first_rows, leaf_of)


def near_pass(direction, ordered, basis, first_rows, leaf_of, lengthscale, outputscale):
    leaf_count = first_rows.shape[0]

    def near_one_leaf(leaf_index, carry):
        near_sum, coeffs = carry
        first_row = first_rows[leaf_index]
        member = (lax.dynamic_slice_in_dim(leaf_of, first_row, LEAF, 0) == leaf_index).astype(
            jnp.float32
        )
        masked = lax.dynamic_slice_in_dim(direction, first_row, LEAF, 1) * member[None, :]
        kernel = matern_block(
            lax.dynamic_slice_in_dim(ordered, first_row, LEAF, 1), lengthscale, outputscale
        )
        applied = exact_product("pa,ab->pb", masked, kernel) * member[None, :]
        current = lax.dynamic_slice_in_dim(near_sum, first_row, LEAF, 1)
        near_sum = lax.dynamic_update_slice_in_dim(near_sum, current + applied, first_row, 1)
        window = lax.dynamic_slice_in_dim(basis, first_row, LEAF, 1).astype(jnp.float32)
        coeffs = coeffs.at[leaf_index].set(exact_product("pa,ra->pr", masked, window))
        return (near_sum, coeffs)

    initial = (
        jnp.zeros_like(direction),
        jnp.zeros((leaf_count, direction.shape[0], basis.shape[0]), jnp.float32),
    )
    return lax.fori_loop(0, leaf_count, near_one_leaf, initial)


def far_pass(leaf_terms, basis, first_rows, leaf_of, template):

    def far_one_leaf(leaf_index, far_sum):
        first_row = first_rows[leaf_index]
        member = (lax.dynamic_slice_in_dim(leaf_of, first_row, LEAF, 0) == leaf_index).astype(
            jnp.float32
        )
        window = lax.dynamic_slice_in_dim(basis, first_row, LEAF, 1).astype(jnp.float32)
        added = exact_product("pr,ra->pa", leaf_terms[leaf_index], window) * member[None, :]
        current = lax.dynamic_slice_in_dim(far_sum, first_row, LEAF, 1)
        return lax.dynamic_update_slice_in_dim(far_sum, current + added, first_row, 1)

    return lax.fori_loop(0, leaf_terms.shape[0], far_one_leaf, jnp.zeros_like(template))


def climb_local(leaf_coeffs, transfers, couplings):
    current = leaf_coeffs
    parent_sums = []
    for depth_index in range(leaf_coeffs.shape[0].bit_length() - 1, 0, -1):
        first_node = 2**depth_index - 1
        node_count = 2**depth_index
        raised = exact_product(
            "npa,nab->npb", current, transfers[first_node : first_node + node_count]
        )
        sided = exact_product(
            "npa,nab->npb", current, couplings[first_node : first_node + node_count]
        )
        current = raised[0::2] + raised[1::2]
        parent_sums.insert(0, sided[0::2] + sided[1::2])
    return (current[0], parent_sums)


def descend_local(device_term, parent_sums, transfers, couplings):
    current = device_term[None]
    for depth_index in range(1, len(parent_sums) + 1):
        first_node = 2**depth_index - 1
        node_count = 2**depth_index
        inherited = jnp.repeat(current, 2, axis=0)
        sums_here = jnp.repeat(parent_sums[depth_index - 1], 2, axis=0)
        current = exact_product(
            "npb,nab->npa", inherited, transfers[first_node : first_node + node_count]
        ) + exact_product(
            "npb,nab->npa", sums_here, couplings[first_node : first_node + node_count]
        )
    return current


def shards(
    solution,
    residual,
    direction,
    coordinates,
    cluster_order,
    leaf_sizes,
    leaf_basis,
    node_transfer,
    node_coupling,
    upper_transfer,
    upper_coupling,
    lengthscale,
    outputscale,
    noise_variance,
):
    noise_level = noise_variance[0]
    points_dev = direction.shape[1]
    ordered = jnp.take(coordinates, cluster_order, axis=1)
    first_rows, leaf_of = leaf_layout(leaf_sizes[0], points_dev)
    near_sum, leaf_coeffs = near_pass(
        direction, ordered, leaf_basis, first_rows, leaf_of, lengthscale[0], outputscale[0]
    )
    transfers = node_transfer[0].astype(jnp.float32)
    couplings = node_coupling[0].astype(jnp.float32)
    device_coeff, local_sums = climb_local(leaf_coeffs, transfers, couplings)
    levels = lax.axis_size("leaf").bit_length() - 1
    chain_transfer = [transfers[0]] + [
        upper_transfer[0, level_index].astype(jnp.float32) for level_index in range(levels - 2)
    ]
    chain_coupling = [couplings[0]] + [
        upper_coupling[0, level_index].astype(jnp.float32) for level_index in range(levels - 1)
    ]
    curvature_part = jnp.sum(direction * (noise_level * direction + near_sum), axis=1)
    for sums_here in local_sums:
        curvature_part = curvature_part + jnp.sum(sums_here * sums_here, axis=(0, 2))
    parent_sums = []
    coefficient = device_coeff
    for level_index in range(levels):
        side_term = exact_product("pa,ab->pb", coefficient, chain_coupling[level_index])
        if level_index + 1 < levels:
            outgoing = jnp.stack(
                [side_term, exact_product("pa,ab->pb", coefficient, chain_transfer[level_index])]
            )
        else:
            outgoing = side_term[None]
        combined = outgoing + swapped(outgoing, "leaf", level_index)
        parent_sums.append(combined[0])
        if level_index + 1 < levels:
            coefficient = combined[1]
    downward = device_coeff
    for level_index in range(levels - 1, -1, -1):
        coupled = exact_product("pb,ab->pa", parent_sums[level_index], chain_coupling[level_index])
        if level_index == levels - 1:
            downward = coupled
        else:
            downward = exact_product("pb,ab->pa", downward, chain_transfer[level_index]) + coupled
    leaf_terms = descend_local(downward, local_sums, transfers, couplings)
    far_sum = far_pass(leaf_terms, leaf_basis, first_rows, leaf_of, direction)
    applied = noise_level * direction + near_sum + far_sum
    curvature, norm_old = lax.psum(
        (jnp.sum(direction * applied, axis=1), jnp.sum(residual * residual, axis=1)), "leaf"
    )
    step_size = norm_old / curvature
    new_solution = solution + step_size[:, None] * direction
    new_residual = residual - step_size[:, None] * applied
    norm_new = lax.psum(jnp.sum(new_residual * new_residual, axis=1), "leaf")
    new_direction = new_residual + (norm_new / norm_old)[:, None] * direction
    return (new_solution, new_residual, new_direction)


def solution(mesh):
    in_specs = (
        P(None, "leaf"),
        P(None, "leaf"),
        P(None, "leaf"),
        P(None, "leaf"),
        P("leaf"),
        P("leaf", None),
        P(None, "leaf"),
        P("leaf", None, None, None),
        P("leaf", None, None, None),
        P("leaf", None, None, None),
        P("leaf", None, None, None),
        P(),
        P(),
        P(),
    )
    out_specs = (P(None, "leaf"), P(None, "leaf"), P(None, "leaf"))
    return jax.shard_map(shards, mesh=mesh, in_specs=in_specs, out_specs=out_specs, check_vma=False)
```

profile of v0, /device:TPU:0, one launch (start us, length us, event | category | flops | bytes accessed | tf_op | source)
XLA Modules:
  0.0 194.3 jit_solution(9857469103438305342)
XLA Ops:
  0.6 0.7 fusion.112
  1.3 0.7 compare_and_fusion
  2.1 0.8 reduce-window.8
  2.9 0.7 fusion.115
  3.6 1.3 copy.19
  5.0 10.8 %gather_fusion = f32[3072,3]{1,0:T(8,128)} fusion(f32[3,3072]{0,1:T(8,128)S(1)} %copy.19, s32[3072]{0:T(1024)S(1)} %fusion.112), kind=kCustom, calls=%fused_computation | custom fusion | bytes 86016 | tf_op jit(solution)/shard_map/jit(_take)/gather | solution.py:128
  15.8 2.7 %select_bitcast_fusion = f32[3,3072]{0,1:T(8,128)S(1)} fusion(f32[3072,3]{1,0:T(8,128)} %gather_fusion, pred[3072]{0:T(1024)(128)(4,1)S(1)} %compare_and_fusion), kind=kLoop, calls=%fused_computation.48 | loop fusion | flops 9216 | bytes 76800 | tf_op jit(solution)/shard_map/jit(_take)/select_n | solution.py:128
  18.5 0.5 copy.20
  19.1 0.6 copy-done
  19.8 51.0 %while.29 = (s32[]{:T(128)}, f32[32,3072]{1,0:T(8,128)S(1)}, f32[4,32,128]{2,1,0:T(8,128)S(1)}, s32[4]{0:T(128)S(1)}, f32[32,3072]{1,0:T(8,128)S(1)}, /*index=5*...) while((s32[]{:T(128)}, f32[32,3072]{1,0:T(8,128)S(1)}, ...), condition=%wide.region_6.7_spmd, body=%wide.region_4.6_spmd.sunk | while | flops 470947872 | bytes 1153309 | solution.py:60
  19.8 0.6 dynamic_slice.112
  22.5 7.2 %fusion.140 = f32[32,1024]{1,0:T(8,128)S(1)} fusion(f32[]{:T(128)} %get-tuple-element.515, f32[1024]{0:T(1024)S(1)} %bitcast.178, f32[1024]{0:T(1024)S(1)} %bitcast.177, f32[1024]{0:T(1024)S(1)} %bitcast.176, f32[]{:T(128)} %get-tuple-element.513, f32[32,3072]{1,0:T(8,128)S(1)} %get-tuple-element.491, s32[]{:T(128)S(6)} %select_n.56, ...), kind=kOutput, calls=%fused_computation.23.clone.1 | convolution fusion | flops 420577280 | bytes 427016 | tf_op jit(solution)/shard_map/while/body/eval_jaxpr/pa,ab->pb/dot_general | solution.py:14
  29.7 1.1 dynamic_update_slice.16
  30.8 0.7 and_reduce_fusion.2
  31.5 1.1 fusion.141
  32.6 0.6 dynamic_slice.112
  35.4 7.2 %fusion.140 = f32[32,1024]{1,0:T(8,128)S(1)} fusion(f32[]{:T(128)} %get-tuple-element.515, f32[1024]{0:T(1024)S(1)} %bitcast.178, f32[1024]{0:T(1024)S(1)} %bitcast.177, f32[1024]{0:T(1024)S(1)} %bitcast.176, f32[]{:T(128)} %get-tuple-element.513, f32[32,3072]{1,0:T(8,128)S(1)} %get-tuple-element.491, s32[]{:T(128)S(6)} %select_n.56, ...), kind=kOutput, calls=%fused_computation.23.clone.1 | convolution fusion | flops 420577280 | bytes 427016 | tf_op jit(solution)/shard_map/while/body/eval_jaxpr/pa,ab->pb/dot_general | solution.py:14
  42.6 1.1 dynamic_update_slice.16
  43.7 0.7 and_reduce_fusion.2
  44.4 1.1 fusion.141
  45.5 0.6 dynamic_slice.112
  48.2 7.2 %fusion.140 = f32[32,1024]{1,0:T(8,128)S(1)} fusion(f32[]{:T(128)} %get-tuple-element.515, f32[1024]{0:T(1024)S(1)} %bitcast.178, f32[1024]{0:T(1024)S(1)} %bitcast.177, f32[1024]{0:T(1024)S(1)} %bitcast.176, f32[]{:T(128)} %get-tuple-element.513, f32[32,3072]{1,0:T(8,128)S(1)} %get-tuple-element.491, s32[]{:T(128)S(6)} %select_n.56, ...), kind=kOutput, calls=%fused_computation.23.clone.1 | convolution fusion | flops 420577280 | bytes 427016 | tf_op jit(solution)/shard_map/while/body/eval_jaxpr/pa,ab->pb/dot_general | solution.py:14
  55.5 1.1 dynamic_update_slice.16
  56.5 0.7 and_reduce_fusion.2
  57.2 1.1 fusion.141
  58.3 0.6 dynamic_slice.112
  61.0 7.2 %fusion.140 = f32[32,1024]{1,0:T(8,128)S(1)} fusion(f32[]{:T(128)} %get-tuple-element.515, f32[1024]{0:T(1024)S(1)} %bitcast.178, f32[1024]{0:T(1024)S(1)} %bitcast.177, f32[1024]{0:T(1024)S(1)} %bitcast.176, f32[]{:T(128)} %get-tuple-element.513, f32[32,3072]{1,0:T(8,128)S(1)} %get-tuple-element.491, s32[]{:T(128)S(6)} %select_n.56, ...), kind=kOutput, calls=%fused_computation.23.clone.1 | convolution fusion | flops 420577280 | bytes 427016 | tf_op jit(solution)/shard_map/while/body/eval_jaxpr/pa,ab->pb/dot_general | solution.py:14
  68.3 0.7 dynamic_update_slice.16
  69.0 0.7 and_reduce_fusion.2
  69.7 1.1 fusion.141
  70.8 0.2 fusion.48
  71.5 0.5 collective-permute-start
  72.0 0.9 collective-permute-done
  73.1 3.4 %collective-permute-start.1 = (f32[2,32,128]{2,1,0:T(8,128)S(1)}, f32[2,32,128]{2,1,0:T(8,128)S(1)}, u32[]{:S(2)}, u32[]{:S(2)}) collective-permute-start(f32[2,32,128]{2,1,0:T(8,128)S(1)} %pad_maximum_fusion.1), channel_id=1, source_target_pairs={{0,2},{1,3},{2,0},{3,1},{4,6},{5,7},{6,4},{7,5},{8,10},{9,11},{10,... | collective-permute-start | bytes 98312 | tf_op jit(solution)/shard_map/ppermute | solution.py:10
  76.5 0.2 fusion.44
  76.7 1.7 collective-permute-done.1
  78.7 1.6 collective-permute-start.2
  80.5 2.2 %collective-permute-done.2 = f32[2,32,128]{2,1,0:T(8,128)S(1)} collective-permute-done((f32[2,32,128]{2,1,0:T(8,128)S(1)}, f32[2,32,128]{2,1,0:T(8,128)S(1)}, u32[]{:S(2)}, u32[]{:S(2)}) %collective-permute-start.2) | collective-permute-done | bytes 32800 | tf_op jit(solution)/shard_map/ppermute | solution.py:10
  83.0 2.2 %collective-permute-start.3 = (f32[2,32,128]{2,1,0:T(8,128)S(1)}, f32[2,32,128]{2,1,0:T(8,128)S(1)}, u32[]{:S(2)}, u32[]{:S(2)}) collective-permute-start(f32[2,32,128]{2,1,0:T(8,128)S(1)} %pad_maximum_fusion.3), channel_id=1, source_target_pairs={{0,8},{1,9},{2,10},{3,11},{4,12},{5,13},{6,14},{7,15},{8,0},{9,1},... | collective-permute-start | bytes 98312 | tf_op jit(solution)/shard_map/ppermute | solution.py:10
  85.2 1.9 collective-permute-done.3
  87.2 2.9 %collective-permute-start.4 = (f32[1,32,128]{2,1,0:T(8,128)S(1)}, f32[1,32,128]{2,1,0:T(8,128)S(1)}, u32[]{:S(2)}, u32[]{:S(2)}) collective-permute-start(f32[1,32,128]{2,1,0:T(8,128)S(1)} %convolution_bitcast_fusion.1), channel_id=1, source_target_pairs={{0,16},{1,17},{2,18},{3,19},{4,20},{5,21},{6,22},{7,23},{8,24},{9,... | collective-permute-start | bytes 49160 | tf_op jit(solution)/shard_map/ppermute | solution.py:10
  90.8 1.1 collective-permute-done.4
  93.5 0.3 fusion.57
  93.8 0.2 convolution_add_fusion.1
  94.0 0.3 fusion.46
  94.4 0.3 convolution_add_fusion
  94.7 15.9 %while.30 = (s32[]{:T(128)}, f32[32,3072]{1,0:T(8,128)S(1)}, s32[4]{0:T(128)S(1)}, f32[4,32,128]{2,1,0:T(8,128)S(1)}, bf16[128,3072]{1,0:T(8,128)(2,1)S(1)}, /*i...) while((s32[]{:T(128)}, f32[32,3072]{1,0:T(8,128)S(1)}, s32[4]{0:T(128)S(1)}, ...), condition=%wide.region_8.9_spmd, body=%wide.region_7.8_spmd.sunk | while | flops 50399236 | bytes 816283 | solution.py:75
  94.8 0.6 dynamic_slice.117
  97.4 0.4 fusion.145
  97.7 1.1 dynamic_update_slice.17
  98.9 0.6 dynamic_slice.117
  101.5 0.4 fusion.145
  101.8 1.1 dynamic_update_slice.17
  103.0 0.6 dynamic_slice.117
  105.6 0.4 fusion.145
  105.9 1.1 dynamic_update_slice.17
  107.0 0.6 dynamic_slice.117
  109.6 0.3 fusion.145
  110.0 0.7 dynamic_update_slice.17
  110.7 0.2 multiply_reduce_fusion.1
  110.9 41.0 %all-reduce = (f32[32]{0:T(128)S(1)}, f32[32]{0:T(128)S(1)}) all-reduce(f32[32]{0:T(128)S(1)} %get-tuple-element.368, f32[32]{0:T(128)S(1)} %get-tuple-element.367), channel_id=1, replica_groups=mesh['leaf'=32] {'leaf'}, use_global_device_ids=true, to_apply=%region_1.2 | all-reduce | flops 64 | bytes 512 | tf_op jit(solution)/shard_map/psum | solution.py:170
  151.9 1.0 multiply_reduce_fusion
  152.9 40.5 %psum.23 = f32[32]{0:T(128)S(1)} all-reduce(f32[32]{0:T(128)S(1)} %get-tuple-element.361), channel_id=1, replica_groups=mesh['leaf'=32] {'leaf'}, use_global_device_ids=true, to_apply=%region_12.13 | all-reduce | flops 32 | bytes 256 | tf_op jit(solution)/shard_map/psum | solution.py:176
  193.4 0.9 multiply_add_fusion
  (69 shorter events, 4.7 us)
Async XLA Ops:
  18.5 1.1 copy-start
  18.5 1.2 copy-start.1
  18.5 1.2 copy-start.9
  19.7 51.0 %copy-start.4 = (bf16[1,7,128,128]{3,2,1,0:T(8,128)(2,1)S(1)}, bf16[1,7,128,128]{3,2,1,0:T(8,128)(2,1)}, u32[]{:S(2)}) copy-start(bf16[1,7,128,128]{3,2,1,0:T(8,128)(2,1)} %param.27) | copy-start | bytes 688132
  19.7 51.6 %copy-start.5 = (bf16[1,7,128,128]{3,2,1,0:T(8,128)(2,1)S(1)}, bf16[1,7,128,128]{3,2,1,0:T(8,128)(2,1)}, u32[]{:S(2)}) copy-start(bf16[1,7,128,128]{3,2,1,0:T(8,128)(2,1)} %param.28) | copy-start | bytes 688132
  19.7 53.1 %copy-start.7 = (bf16[1,3,128,128]{3,2,1,0:T(8,128)(2,1)S(1)}, bf16[1,3,128,128]{3,2,1,0:T(8,128)(2,1)}, u32[]{:S(2)}) copy-start(bf16[1,3,128,128]{3,2,1,0:T(8,128)(2,1)} %param.29) | copy-start | bytes 294916
  19.7 53.2 %copy-start.6 = (bf16[1,4,128,128]{3,2,1,0:T(8,128)(2,1)S(1)}, bf16[1,4,128,128]{3,2,1,0:T(8,128)(2,1)}, u32[]{:S(2)}) copy-start(bf16[1,4,128,128]{3,2,1,0:T(8,128)(2,1)} %param.30) | copy-start | bytes 393220
  71.5 1.3 collective-permute-start
  73.1 5.3 %collective-permute-start.1 = (f32[2,32,128]{2,1,0:T(8,128)S(1)}, f32[2,32,128]{2,1,0:T(8,128)S(1)}, u32[]{:S(2)}, u32[]{:S(2)}) collective-permute-start(f32[2,32,128]{2,1,0:T(8,128)S(1)} %pad_maximum_fusion.1), channel_id=1, source_target_pairs={{0,2},{1,3},{2,0},{3,1},{4,6},{5,7},{6,4},{7,5},{8,10},{9,11},{10,... | collective-permute-start | bytes 98312 | tf_op jit(solution)/shard_map/ppermute | solution.py:10
  78.7 4.0 %collective-permute-start.2 = (f32[2,32,128]{2,1,0:T(8,128)S(1)}, f32[2,32,128]{2,1,0:T(8,128)S(1)}, u32[]{:S(2)}, u32[]{:S(2)}) collective-permute-start(f32[2,32,128]{2,1,0:T(8,128)S(1)} %pad_maximum_fusion.2), channel_id=1, source_target_pairs={{0,4},{1,5},{2,6},{3,7},{4,0},{5,1},{6,2},{7,3},{8,12},{9,13},{10,... | collective-permute-start | bytes 98312 | tf_op jit(solution)/shard_map/ppermute | solution.py:10
  83.0 4.1 %collective-permute-start.3 = (f32[2,32,128]{2,1,0:T(8,128)S(1)}, f32[2,32,128]{2,1,0:T(8,128)S(1)}, u32[]{:S(2)}, u32[]{:S(2)}) collective-permute-start(f32[2,32,128]{2,1,0:T(8,128)S(1)} %pad_maximum_fusion.3), channel_id=1, source_target_pairs={{0,8},{1,9},{2,10},{3,11},{4,12},{5,13},{6,14},{7,15},{8,0},{9,1},... | collective-permute-start | bytes 98312 | tf_op jit(solution)/shard_map/ppermute | solution.py:10
  87.2 4.7 %collective-permute-start.4 = (f32[1,32,128]{2,1,0:T(8,128)S(1)}, f32[1,32,128]{2,1,0:T(8,128)S(1)}, u32[]{:S(2)}, u32[]{:S(2)}) collective-permute-start(f32[1,32,128]{2,1,0:T(8,128)S(1)} %convolution_bitcast_fusion.1), channel_id=1, source_target_pairs={{0,16},{1,17},{2,18},{3,19},{4,20},{5,21},{6,22},{7,23},{8,24},{9,... | collective-permute-start | bytes 49160 | tf_op jit(solution)/shard_map/ppermute | solution.py:10
  94.7 16.0 %copy-start.2 = (f32[32,3072]{1,0:T(8,128)S(1)}, f32[32,3072]{1,0:T(8,128)}, u32[]{:S(2)}) copy-start(f32[32,3072]{1,0:T(8,128)} %param.21) | copy-start | bytes 1179652
  110.7 41.2 %copy-start.8 = (f32[32,3072]{1,0:T(8,128)S(1)}, f32[32,3072]{1,0:T(8,128)}, u32[]{:S(2)}) copy-start(f32[32,3072]{1,0:T(8,128)} %param.20) | copy-start | bytes 1179652
  152.9 41.4 %copy-start.3 = (f32[32,3072]{1,0:T(8,128)}, f32[32,3072]{1,0:T(8,128)S(1)}, u32[]{:S(2)}) copy-start(f32[32,3072]{1,0:T(8,128)S(1)} %get-tuple-element.362) | copy-start | bytes 1179652
where the time goes:
time: 195 us; the launch traced here: 194 us
  blocking collectives  81.5 us (42%)
  matrix products  39.3 us (20%)
  local copies, waits for them, and re-layouts  26.4 us (14%)
  loops' own time  15.9 us (8%)
  other arithmetic  11.4 us (6%)
  starting transfers between devices  10.6 us (5%)
  waiting for transfers between devices  7.75 us (4%)
    psum x1, blocking collectives, shards(): lax.psum((jnp.sum(direction * applied, axis=1), jnp.sum(residual * residu...  41 us
    psum x1, blocking collectives, shards(): norm_new = lax.psum(jnp.sum(new_residual * new_residual, axis=1), 'leaf')  40.5 us
    dot_general x38, matrix products, exact_product(): return jnp.einsum(form, left, right, precision=lax.Precision.HIGHEST)  39.3 us
    gather x1, local copies, waits for them, and re-layouts, shards(): ordered = jnp.take(coordinates, cluster_order, axis=1)  10.8 us
    ppermute x5, starting transfers between devices, swapped(): lax.ppermute(array, axis, [(i, i ^ 1 << stride) for i in range(lax.axis_s...  10.6 us
    another operation x1, loops' own time, near_pass(): return lax.fori_loop(0, leaf_count, near_one_leaf, initial)  7.96 us
    another operation x1, loops' own time, far_pass(): lax.fori_loop(0, leaf_terms.shape[0], far_one_leaf, jnp.zeros_like(templa...  7.9 us
    ppermute x5, waiting for transfers between devices, swapped(): lax.ppermute(array, axis, [(i, i ^ 1 << stride) for i in range(lax.axis_s...  7.75 us
  transfers between devices with their start and end apart: 5, of which 5 were waited for; matrix products, arithmetic and copies ran while one was open for 0% of the time, Pallas kernels for 0%

commit v1 on v0

v1 whole, which is shorter than its diff:
```python
import functools
import math

import jax
import jax.numpy as jnp
from jax import lax
from jax.experimental import pallas as pl
from jax.experimental.pallas import tpu as pltpu
from jax.sharding import PartitionSpec as P

F32 = jnp.float32
BF16 = jnp.bfloat16
TILE = 256
FAR_AWAY = 32768.0
LOG2E = 1.0 / math.log(2.0)
POLY = math.log(2.0) ** 2 / 3.0
LINEAR = 3.0 * LOG2E
CONSTANT = 3.0 * LOG2E * LOG2E

VMEM = pl.BlockSpec(memory_space=pltpu.VMEM)
SMEM = pl.BlockSpec(memory_space=pltpu.SMEM)
ANY = pl.BlockSpec(memory_space=pl.ANY)
PARAMS = pltpu.CompilerParams(vmem_limit_bytes=48 * 1024 * 1024)


def halves(x):
    high = x.astype(BF16)
    low = (x - high.astype(F32)).astype(BF16)
    return jnp.concatenate([high, low], axis=0)


def folded(x):
    rows = x.shape[0] // 2
    return x[:rows] + x[rows:]


def times(x, generator):
    return folded(jnp.dot(halves(x), generator, preferred_element_type=F32))


def times_transposed(x, generator):
    return folded(
        lax.dot_general(
            halves(x), generator, (((1,), (1,)), ((), ())), preferred_element_type=F32
        )
    )


def leaf_ends(sizes_ref, leaf_count):
    ends = []
    total = 0
    for leaf in range(leaf_count):
        total = total + sizes_ref[0, leaf]
        ends.append(total)
    return ends


def leaf_row(ends, first, shape):
    positions = lax.broadcasted_iota(jnp.int32, shape, 1) + first
    leaf = jnp.zeros(shape, jnp.int32)
    for end in ends[:-1]:
        leaf = leaf + (positions >= end).astype(jnp.int32)
    return leaf


def up_kernel(
    leaf_count,
    levels,
    sizes_ref,
    d_ref,
    basis_ref,
    nt_ref,
    nc_ref,
    ut_ref,
    uc_ref,
    up_ref,
    local_ref,
):
    probes, points = d_ref.shape
    ends = leaf_ends(sizes_ref, leaf_count)
    split = halves(d_ref[...])
    leaf = leaf_row(ends, 0, (2 * probes, points))
    zero = jnp.zeros_like(split)
    masked = jnp.concatenate(
        [jnp.where(leaf == index, split, zero) for index in range(leaf_count)], axis=0
    )
    raw = lax.dot_general(
        masked, basis_ref[...], (((1,), (1,)), ((), ())), preferred_element_type=F32
    )
    current = [
        folded(raw[2 * probes * index : 2 * probes * (index + 1)]) for index in range(leaf_count)
    ]
    rank = basis_ref.shape[0]
    while len(current) > 1:
        count = len(current)
        raised, sided = [], []
        for index in range(count):
            node = count - 1 + index
            both = jnp.concatenate([nt_ref[0, node], nc_ref[0, node]], axis=1)
            image = times(current[index], both)
            raised.append(image[:, :rank])
            sided.append(image[:, rank:])
        current = [raised[2 * i] + raised[2 * i + 1] for i in range(count // 2)]
        for i in range(count // 2):
            local_ref[count // 2 - 1 + i] = sided[2 * i] + sided[2 * i + 1]
    coefficient = current[0]
    for level in range(levels):
        coupling = nc_ref[0, 0] if level == 0 else uc_ref[0, level - 1]
        if level + 1 < levels:
            transfer = nt_ref[0, 0] if level == 0 else ut_ref[0, level - 1]
            image = times(coefficient, jnp.concatenate([transfer, coupling], axis=1))
            coefficient = image[:, :rank]
            up_ref[level] = image[:, rank:]
        else:
            up_ref[level] = times(coefficient, coupling)


def climb(sizes, direction, basis, node_transfer, node_coupling, upper_transfer, upper_coupling, levels):
    leaf_count = sizes.shape[1]
    probes, rank = direction.shape[0], basis.shape[0]
    return pl.pallas_call(
        functools.partial(up_kernel, leaf_count, levels),
        out_shape=(
            jax.ShapeDtypeStruct((levels, probes, rank), F32),
            jax.ShapeDtypeStruct((leaf_count - 1, probes, rank), F32),
        ),
        in_specs=[SMEM] + [VMEM] * 6,
        out_specs=(VMEM, VMEM),
        compiler_params=PARAMS,
        name="climb",
    )(sizes, direction, basis, node_transfer, node_coupling, upper_transfer, upper_coupling)


def features_kernel(
    leaf_count,
    sizes_ref,
    length_ref,
    coords_ref,
    order_ref,
    d_ref,
    after_ref,
    left_ref,
    right_ref,
    dd_ref,
    ordered_ref,
):
    points = coords_ref.shape[1]
    chunks = points // 128
    ordered_ref[...] = jnp.zeros_like(ordered_ref)
    for group in range(chunks // 8):
        order = order_ref[8 * group : 8 * group + 8, :]
        chunk_of = lax.shift_right_logical(order, 7)
        lane_of = lax.bitwise_and(order, 127)
        for axis in range(3):
            found = jnp.zeros((8, 128), F32)
            for chunk in range(chunks):
                source = jnp.broadcast_to(
                    coords_ref[axis : axis + 1, 128 * chunk : 128 * chunk + 128], (8, 128)
                )
                picked = jnp.take_along_axis(source, lane_of, axis=1)
                found = jnp.where(chunk_of == chunk, picked, found)
            for row in range(8):
                place = 128 * (8 * group + row)
                ordered_ref[axis : axis + 1, place : place + 128] = found[row : row + 1, :]
    row8 = lax.broadcasted_iota(jnp.int32, (8, points), 0)
    scale = jnp.full((1, 1), math.sqrt(5.0) * LOG2E, F32) / length_ref[0]
    scaled = jnp.where(row8 < 3, (ordered_ref[...] - 0.5) * scale, 0.0)
    z1 = scaled.astype(BF16).astype(F32)
    z2 = (scaled - z1).astype(BF16).astype(F32)
    kept = z1 + z2
    norm = jnp.broadcast_to(jnp.sum(kept * kept, axis=0, keepdims=True), (8, points))
    n1 = norm.astype(BF16).astype(F32)
    n2 = (norm - n1).astype(BF16).astype(F32)
    n3 = norm - n1 - n2
    ends = leaf_ends(sizes_ref, leaf_count)
    leaf = leaf_row(ends, 0, (8, points))
    parts = jnp.where(row8 % 3 == 0, n1, jnp.where(row8 % 3 == 1, n2, n3))
    norm_left = jnp.where(row8 < 3, parts, jnp.where(row8 < 6, 1.0, 0.0))
    norm_right = jnp.where(row8 < 3, 1.0, jnp.where(row8 < 6, parts, 0.0))
    same = leaf == row8
    leaf_left = jnp.where(same, 1.0, 0.0)
    leaf_right = jnp.where(same, 0.0, FAR_AWAY)
    left = jnp.concatenate(
        [-2.0 * z1, -2.0 * z1, -2.0 * z2, -2.0 * z2, norm_left, leaf_left]
        + [jnp.zeros((80, points), F32)],
        axis=0,
    )
    right = jnp.concatenate(
        [z1, z2, z1, z2, norm_right, leaf_right] + [jnp.zeros((80, points), F32)], axis=0
    )
    right_ref[...] = right.astype(BF16)
    left_ref[...] = left.T.astype(BF16)
    split = halves(d_ref[...]).astype(F32)
    split = jnp.concatenate([split, jnp.zeros((128 - split.shape[0], points), F32)], axis=0)
    dd_ref[...] = split.T.astype(BF16)


def features(sizes, lengthscale, coordinates, order, direction, after):
    leaf_count = sizes.shape[1]
    points = direction.shape[1]
    return pl.pallas_call(
        functools.partial(features_kernel, leaf_count),
        out_shape=(
            jax.ShapeDtypeStruct((points, 128), BF16),
            jax.ShapeDtypeStruct((128, points), BF16),
            jax.ShapeDtypeStruct((points, 128), BF16),
        ),
        in_specs=[SMEM, SMEM, VMEM, VMEM, VMEM, ANY],
        out_specs=(VMEM, VMEM, VMEM),
        scratch_shapes=[pltpu.VMEM((8, points), F32)],
        compiler_params=PARAMS,
        name="features",
    )(sizes, lengthscale, coordinates, order.reshape(-1, 128), direction, after)


def near_kernel(leaf_count, probes, first, sizes_ref, left_ref, right_ref, dd_ref, after_ref, out_ref):
    ends = leaf_ends(sizes_ref, leaf_count)
    count = out_ref.shape[1] // TILE

    def one_tile(step, carry):
        row = first + step
        begin = row * TILE
        last = begin + TILE - 1
        low = 0
        high = ends[-1]
        for end in ends:
            low = jnp.where(end <= begin, end, low)
        for end in ends[::-1]:
            high = jnp.where(end > last, end, high)
        left = left_ref[pl.ds(pl.multiple_of(begin, TILE), TILE), :]

        def one_block(block, total):
            place = pl.multiple_of(block * TILE, TILE)
            squared = jnp.dot(left, right_ref[:, pl.ds(place, TILE)], preferred_element_type=F32)
            squared = jnp.maximum(squared, 1e-12)
            root = squared * lax.rsqrt(squared)
            kernel = (squared + LINEAR * root + CONSTANT) * jnp.exp2(-root)
            high_part = kernel.astype(BF16)
            low_part = (kernel - high_part.astype(F32)).astype(BF16)
            weights = dd_ref[pl.ds(place, TILE), :]
            return (
                total
                + jnp.dot(high_part, weights, preferred_element_type=F32)
                + jnp.dot(low_part, weights, preferred_element_type=F32)
            )

        total = lax.fori_loop(
            lax.shift_right_logical(low, 8),
            lax.shift_right_logical(high - 1, 8) + 1,
            one_block,
            jnp.zeros((TILE, 128), F32),
        )
        flipped = total.T
        out_ref[:, pl.ds(pl.multiple_of(step * TILE, TILE), TILE)] = (
            flipped[:probes] + flipped[probes : 2 * probes]
        )
        return carry

    lax.fori_loop(0, count, one_tile, 0)


def near_part(sizes, left, right, dd, after, probes, first, count):
    leaf_count = sizes.shape[1]
    return pl.pallas_call(
        functools.partial(near_kernel, leaf_count, probes, first),
        out_shape=jax.ShapeDtypeStruct((probes, count * TILE), F32),
        in_specs=[SMEM, VMEM, VMEM, VMEM, ANY],
        out_specs=VMEM,
        compiler_params=PARAMS,
        name="near_part",
    )(sizes, left, right, dd, after)


def down_kernel(
    leaf_count,
    levels,
    parts,
    sizes_ref,
    noise_ref,
    scale_ref,
    d_ref,
    r_ref,
    basis_ref,
    nt_ref,
    nc_ref,
    ut_ref,
    uc_ref,
    local_ref,
    *rest,
):
    side_refs = rest[:levels]
    near_refs = rest[levels : levels + parts]
    a_ref, sums_ref = rest[levels + parts :]
    probes, points = d_ref.shape
    down = None
    for level in range(levels - 1, -1, -1):
        coupling = nc_ref[0, 0] if level == 0 else uc_ref[0, level - 1]
        side = side_refs[level][...]
        if down is None:
            down = times_transposed(side, coupling)
        else:
            transfer = nt_ref[0, 0] if level == 0 else ut_ref[0, level - 1]
            down = times_transposed(
                jnp.concatenate([down, side], axis=1),
                jnp.concatenate([transfer, coupling], axis=1),
            )
    current = [down]
    while len(current) < leaf_count:
        count = len(current)
        following = []
        for index in range(2 * count):
            node = 2 * count - 1 + index
            parent = index // 2
            following.append(
                times_transposed(
                    jnp.concatenate([current[parent], local_ref[count - 1 + parent]], axis=1),
                    jnp.concatenate([nt_ref[0, node], nc_ref[0, node]], axis=1),
                )
            )
        current = following
    stacked = jnp.concatenate([halves(term) for term in current], axis=0)
    ends = leaf_ends(sizes_ref, leaf_count)
    noise = noise_ref[0]
    near_scale = scale_ref[0] * POLY
    width = 512
    peak = jnp.zeros((probes, 128), F32)
    old = jnp.zeros((probes, 128), F32)
    curve = jnp.zeros((probes, 128), F32)
    per_part = near_refs[0].shape[1]

    def lanes(x):
        return sum(x[:, 128 * i : 128 * i + 128] for i in range(width // 128))

    for first in range(0, points, width):
        far_all = jnp.dot(
            stacked, basis_ref[:, first : first + width], preferred_element_type=F32
        )
        leaf = leaf_row(ends, first, (probes, width))
        far = folded(far_all[: 2 * probes])
        for index in range(1, leaf_count):
            term = folded(far_all[2 * probes * index : 2 * probes * (index + 1)])
            far = jnp.where(leaf == index, term, far)
        d = d_ref[:, first : first + width]
        r = r_ref[:, first : first + width]
        at = first % per_part
        near = near_refs[first // per_part][:, at : at + width]
        applied = noise * d + near_scale * near + far
        a_ref[:, first : first + width] = applied
        size = jnp.abs(applied)
        for i in range(width // 128):
            peak = jnp.maximum(peak, size[:, 128 * i : 128 * i + 128])
        old = old + lanes(r * r)
        curve = curve + lanes(d * applied)
    top = jnp.maximum(jnp.max(peak, axis=1, keepdims=True), 1e-30)
    inverse = 1.0 / top
    cross = jnp.zeros((probes, 128), F32)
    square = jnp.zeros((probes, 128), F32)
    for first in range(0, points, width):
        unit = a_ref[:, first : first + width] * inverse
        cross = cross + lanes(r_ref[:, first : first + width] * unit)
        square = square + lanes(unit * unit)
    lane = lax.broadcasted_iota(jnp.int32, (probes, 128), 1)
    sums = jnp.where(lane == 0, jnp.sum(old, axis=1, keepdims=True), 0.0)
    sums = jnp.where(lane == 1, jnp.sum(curve, axis=1, keepdims=True), sums)
    sums = jnp.where(lane == 2, jnp.sum(cross, axis=1, keepdims=True), sums)
    sums = jnp.where(lane == 3, jnp.sum(square, axis=1, keepdims=True), sums)
    sums_ref[...] = jnp.where(lane == 4, top, sums)


def descend(
    sizes, noise, scale, direction, residual, basis, node_transfer, node_coupling,
    upper_transfer, upper_coupling, local, sides, nears,
):
    leaf_count = sizes.shape[1]
    probes, points = direction.shape
    return pl.pallas_call(
        functools.partial(down_kernel, leaf_count, len(sides), len(nears)),
        out_shape=(
            jax.ShapeDtypeStruct((probes, points), F32),
            jax.ShapeDtypeStruct((probes, 128), F32),
        ),
        in_specs=[SMEM, SMEM, SMEM] + [VMEM] * (8 + len(sides) + len(nears)),
        out_specs=(VMEM, VMEM),
        compiler_params=PARAMS,
        name="descend",
    )(
        sizes, noise, scale, direction, residual, basis, node_transfer, node_coupling,
        upper_transfer, upper_coupling, local, *sides, *nears,
    )


def merged(pieces):
    tops = [piece[:, 4:5] for piece in pieces]
    top = functools.reduce(jnp.maximum, tops)
    lane = lax.broadcasted_iota(jnp.int32, pieces[0].shape, 1)
    total = jnp.zeros_like(pieces[0])
    for piece, own in zip(pieces, tops):
        ratio = own / top
        factor = jnp.where(lane < 2, 1.0, jnp.where(lane == 2, ratio, ratio * ratio))
        total = total + piece * factor
    return jnp.where(lane == 4, top, total)


def merge_kernel(*refs):
    refs[-1][...] = merged([ref[...] for ref in refs[:-1]])


def merge(pieces):
    return pl.pallas_call(
        merge_kernel,
        out_shape=jax.ShapeDtypeStruct(pieces[0].shape, F32),
        in_specs=[VMEM] * len(pieces),
        out_specs=VMEM,
        name="merge",
    )(*pieces)


def step_kernel(pieces, *refs):
    sums = merged([ref[...] for ref in refs[:pieces]])
    x_ref, r_ref, d_ref, a_ref, nx_ref, nr_ref, nd_ref = refs[pieces:]
    old, curve, cross, square, top = (sums[:, i : i + 1] for i in range(5))
    step = old / curve
    reach = step * top
    fresh = old - 2.0 * (reach * cross) + (reach * reach) * square
    beta = fresh / old
    d = d_ref[...]
    nx_ref[...] = x_ref[...] + step * d
    remaining = r_ref[...] - step * a_ref[...]
    nr_ref[...] = remaining
    nd_ref[...] = remaining + beta * d


def finish(pieces, solution_block, residual, direction, applied):
    shape = jax.ShapeDtypeStruct(direction.shape, F32)
    return pl.pallas_call(
        functools.partial(step_kernel, len(pieces)),
        out_shape=(shape, shape, shape),
        in_specs=[VMEM] * (len(pieces) + 4),
        out_specs=(VMEM, VMEM, VMEM),
        compiler_params=PARAMS,
        name="finish",
    )(*pieces, solution_block, residual, direction, applied)


def from_partner(array, stride):
    count = lax.axis_size("leaf")
    return lax.ppermute(array, "leaf", [(i, i ^ stride) for i in range(count)])


def level_groups(levels):
    groups = [[0]]
    level = 1
    while level < levels:
        groups.append(list(range(level, min(level + 2, levels))))
        level += 2
    return groups


def shards(
    solution,
    residual,
    direction,
    coordinates,
    cluster_order,
    leaf_sizes,
    leaf_basis,
    node_transfer,
    node_coupling,
    upper_transfer,
    upper_coupling,
    lengthscale,
    outputscale,
    noise_variance,
):
    levels = lax.axis_size("leaf").bit_length() - 1
    probes, points = direction.shape
    up, local = climb(
        leaf_sizes, direction, leaf_basis, node_transfer, node_coupling,
        upper_transfer, upper_coupling, levels,
    )
    left, right, dd = features(leaf_sizes, lengthscale, coordinates, cluster_order, direction, up)
    tiles = points // TILE
    groups = level_groups(levels)
    parts = 3
    per_part = tiles // parts
    sides = [None] * levels
    nears = []
    current = up
    for number, group in enumerate(groups):
        base = group[0]
        strides = [2**level for level in group]
        incoming = {}
        for pick in range(1, 2 ** len(group)):
            stride = sum(s for bit, s in enumerate(strides) if pick >> bit & 1)
            top = pick.bit_length() - 1
            incoming[pick] = from_partner(current[top:], stride)
        if number < parts:
            nears.append(
                near_part(leaf_sizes, left, right, dd, current, probes, number * per_part, per_part)
            )
        for position in range(len(group)):
            total = current[position]
            for pick in range(1, 2 ** (position + 1)):
                top = pick.bit_length() - 1
                total = total + incoming[pick][position - top]
            sides[base + position] = total
        following = current[len(group) :]
        if following.shape[0]:
            for pick in range(1, 2 ** len(group)):
                top = pick.bit_length() - 1
                following = following + incoming[pick][len(group) - top :]
        current = following
    for number in range(len(groups), parts):
        nears.append(
            near_part(leaf_sizes, left, right, dd, up, probes, number * per_part, per_part)
        )
    applied, sums = descend(
        leaf_sizes, noise_variance, outputscale, direction, residual, leaf_basis,
        node_transfer, node_coupling, upper_transfer, upper_coupling, local, sides, nears,
    )
    pieces = [sums]
    for group in groups:
        own = merge(pieces) if len(pieces) > 1 else pieces[0]
        pieces = [own]
        for pick in range(1, 2 ** len(group)):
            stride = sum(2**level for bit, level in enumerate(group) if pick >> bit & 1)
            pieces.append(from_partner(own, stride))
    return finish(pieces, solution, residual, direction, applied)


def solution(mesh):
    in_specs = (
        P(None, "leaf"),
        P(None, "leaf"),
        P(None, "leaf"),
        P(None, "leaf"),
        P("leaf"),
        P("leaf", None),
        P(None, "leaf"),
        P("leaf", None, None, None),
        P("leaf", None, None, None),
        P("leaf", None, None, None),
        P("leaf", None, None, None),
        P(),
        P(),
        P(),
    )
    out_specs = (P(None, "leaf"), P(None, "leaf"), P(None, "leaf"))
    return jax.shard_map(shards, mesh=mesh, in_specs=in_specs, out_specs=out_specs, check_vma=False)
```

time: 195 us -> 73 us (0.37)
  blocking collectives: 81.5 us -> 0 us
  matrix products: 39.3 us -> 0 us
  Pallas kernels: 0 us -> 32.1 us
  local copies, waits for them, and re-layouts: 26.4 us -> 8.44 us
  loops' own time: 15.9 us -> 0 us
  other arithmetic: 11.4 us -> 0.05 us
  starting transfers between devices: 10.6 us -> 21.5 us
    psum x2 -> x0, blocking collectives: 81.5 us -> none  [the longest x1 41 us: shards(): lax.psum((jnp.sum(direction * applied, axis=1), jnp.sum(residual * residu...]
    dot_general x38 -> x0, matrix products: 39.3 us -> none  [exact_product(): return jnp.einsum(form, left, right, precision=lax.Precision.HIGHEST)]
    pallas_call x0 -> x9, Pallas kernels: none -> 32.1 us  [the longest x3 22.2 us: near_part(): pl.pallas_call(functools.partial(near_kernel, leaf_count, probes, first),...]
    another operation x2 -> x0, loops' own time: 15.9 us -> none  [the longest x1 7.96 us: near_pass(): return lax.fori_loop(0, leaf_count, near_one_leaf, initial)]
    ppermute x5 -> x14, starting transfers between devices: 10.6 us -> 21.5 us  [from_partner(): return lax.ppermute(array, 'leaf', [(i, i ^ stride) for i in range(count)])]
    gather x1 -> x0, local copies, waits for them, and re-layouts: 10.8 us -> none  [shards(): ordered = jnp.take(coordinates, cluster_order, axis=1)]
    dynamic_update_slice x8 -> x0, local copies, waits for them, and re-layouts: 7.91 us -> none  [the longest x4 3.96 us: far_one_leaf(): lax.dynamic_update_slice_in_dim(far_sum, current + added, first_row, 1)]
    unnamed x21 -> x42, local copies, waits for them, and re-layouts: 2.04 us -> 8.44 us
  transfers between devices with their start and end apart: 5 -> 14, of which waited for: 5 -> 6; matrix products, arithmetic and copies ran while one was open for 0% -> 0% of each run, Pallas kernels for 0% -> 33%
where the time goes in v1:
time: 73 us; the launch traced here: 71.6 us
  Pallas kernels  32.1 us (44%)
  starting transfers between devices  21.5 us (29%)
  local copies, waits for them, and re-layouts  8.44 us (12%)
  waiting for transfers between devices  6.67 us (9%)
  between operations  2.83 us (4%)
    pallas_call x3, Pallas kernels, near_part(): pl.pallas_call(functools.partial(near_kernel, leaf_count, probes, first),...  22.2 us
    ppermute x14, starting transfers between devices, from_partner(): return lax.ppermute(array, 'leaf', [(i, i ^ stride) for i in range(count)])  21.5 us
    unnamed x42, local copies, waits for them, and re-layouts  8.44 us
    ppermute x14, waiting for transfers between devices, from_partner(): return lax.ppermute(array, 'leaf', [(i, i ^ stride) for i in range(count)])  6.67 us
    pallas_call x2, Pallas kernels, merge(): pl.pallas_call(merge_kernel, out_shape=jax.ShapeDtypeStruct(pieces[0].sha...  2.92 us
    pallas_call x1, Pallas kernels, descend(): pl.pallas_call(functools.partial(down_kernel, leaf_count, len(sides), len...  2.26 us
    pallas_call x1, Pallas kernels, climb(): pl.pallas_call(functools.partial(up_kernel, leaf_count, levels), out_shap...  2.12 us
  transfers between devices with their start and end apart: 14, of which 6 were waited for; matrix products, arithmetic and copies ran while one was open for 0% of the time, Pallas kernels for 33%

profile of v1, /device:TPU:0, one launch (start us, length us, event | category | flops | bytes accessed | tf_op | source)
XLA Modules:
  0.0 71.6 jit_solution(2398278808801056233)
XLA Ops:
  0.6 0.0 copy-start
  0.6 1.0 %copy-done = f32[32,3072]{1,0:T(8,128)S(1)} copy-done((f32[32,3072]{1,0:T(8,128)S(1)}, f32[32,3072]{1,0:T(8,128)}, u32[]{:S(2)}) %copy-start) | copy-done | bytes 393240
  1.6 1.1 %copy-done.2 = bf16[128,3072]{1,0:T(8,128)(2,1)S(1)} copy-done((bf16[128,3072]{1,0:T(8,128)(2,1)S(1)}, bf16[128,3072]{1,0:T(8,128)(2,1)}, u32[]{:S(2)}) %copy-start.2) | copy-done | bytes 786456
  2.8 0.9 %copy-done.5 = bf16[1,7,128,128]{3,2,1,0:T(8,128)(2,1)S(1)} copy-done((bf16[1,7,128,128]{3,2,1,0:T(8,128)(2,1)S(1)}, bf16[1,7,128,128]{3,2,1,0:T(8,128)(2,1)}, u32[]{:S(2)}) %copy-start.5) | copy-done | bytes 229400
  3.7 0.9 %copy-done.7 = bf16[1,7,128,128]{3,2,1,0:T(8,128)(2,1)S(1)} copy-done((bf16[1,7,128,128]{3,2,1,0:T(8,128)(2,1)S(1)}, bf16[1,7,128,128]{3,2,1,0:T(8,128)(2,1)}, u32[]{:S(2)}) %copy-start.7) | copy-done | bytes 229400
  4.6 0.9 %copy-done.8 = bf16[1,4,128,128]{3,2,1,0:T(8,128)(2,1)S(1)} copy-done((bf16[1,4,128,128]{3,2,1,0:T(8,128)(2,1)S(1)}, bf16[1,4,128,128]{3,2,1,0:T(8,128)(2,1)}, u32[]{:S(2)}) %copy-start.8) | copy-done | bytes 131096
  5.5 0.9 %copy-done.9 = bf16[1,3,128,128]{3,2,1,0:T(8,128)(2,1)S(1)} copy-done((bf16[1,3,128,128]{3,2,1,0:T(8,128)(2,1)S(1)}, bf16[1,3,128,128]{3,2,1,0:T(8,128)(2,1)}, u32[]{:S(2)}) %copy-start.9) | copy-done | bytes 98328
  6.4 0.7 copy-done.13
  7.1 2.1 %climb.1 = (f32[5,32,128]{2,1,0:T(8,128)S(1)}, f32[3,32,128]{2,1,0:T(8,128)S(1)}) custom-call(s32[1,4]{1,0:T(1,128)S(1)} %copy-done.13, f32[32,3072]{1,0:T(8,128)S(1)} %copy-done, bf16[128,3072]{1,0:T(8,128)(2,1)S(1)} %copy-done.2, bf16[1,7,128,128]{3,2,1,0:T(8,128)(2,1)S(1)} %copy-done.5, bf16[1,7,128,128]{3,2,1,0:T(8,128)(2,1)S(1)} %copy-done.7, ...), custom_call_target="tpu_custom_call" | custom-call | tf_op jit(solution)/shard_map/climb/pallas_call | solution.py:121
  9.2 0.5 collective-permute-start
  11.6 0.0 copy-done.12
  11.6 0.0 copy-done.16
  11.7 1.3 %features.1 = (bf16[3072,128]{1,0:T(8,128)(2,1)S(1)}, bf16[128,3072]{1,0:T(8,128)(2,1)S(1)}, bf16[3072,128]{1,0:T(8,128)(2,1)S(1)}) custom-call(s32[1,4]{1,0:T(1,128)S(1)} %copy-done.13, f32[1]{0:T(128)S(6)} %copy.17.length_ref, f32[3,3072]{1,0:T(4,128)S(1)} %copy-done.12, s32[24,128]{1,0:T(8,128)S(1)} %bitcast.11, f32[32,3072]{1,0:T(8,128)S(1)} %copy-done, ...), custom_call_target="tpu_custom_call" | custom-call | tf_op jit(solution)/shard_map/features/pallas_call | solution.py:201
  12.9 7.1 %near_part.3.rest_5_ = f32[32,1024]{1,0:T(8,128)S(1)} custom-call(s32[1,4]{1,0:T(1,128)S(1)} %copy-done.13, bf16[3072,128]{1,0:T(8,128)(2,1)S(1)} %get-tuple-element.12.left_ref, bf16[128,3072]{1,0:T(8,128)(2,1)S(1)} %get-tuple-element.13.right_ref, bf16[3072,128]{1,0:T(8,128)(2,1)S(1)} %get-tuple-element.14.dd_ref, ...), custom_call_target="tpu_custom_call" | custom-call | tf_op jit(solution)/shard_map/near_part/pallas_call | solution.py:264
  20.1 0.0 collective-permute-done
  20.1 4.3 %collective-permute-start.3 = (f32[3,32,128]{2,1,0:T(8,128)S(1)}, f32[3,32,128]{2,1,0:T(8,128)S(1)}, u32[]{:S(2)}, u32[]{:S(2)}) collective-permute-start(f32[3,32,128]{2,1,0:T(8,128)S(1)} %slice.85), channel_id=1, source_target_pairs={{0,6},{1,7},{2,4},{3,5},{4,2},{5,3},{6,0},{7,1},{8,14},{9,15},{10,... | collective-permute-start | bytes 147464 | tf_op jit(solution)/shard_map/ppermute | solution.py:447
  24.4 1.3 %collective-permute-start.2 = (f32[3,32,128]{2,1,0:T(8,128)S(1)}, f32[3,32,128]{2,1,0:T(8,128)S(1)}, u32[]{:S(2)}, u32[]{:S(2)}) collective-permute-start(f32[3,32,128]{2,1,0:T(8,128)S(1)} %slice.85), channel_id=1, source_target_pairs={{0,4},{1,5},{2,6},{3,7},{4,0},{5,1},{6,2},{7,3},{8,12},{9,13},{10,... | collective-permute-start | bytes 147464 | tf_op jit(solution)/shard_map/ppermute | solution.py:447
  25.7 0.0 collective-permute-start.1
  25.7 6.8 %near_part.4.rest_6_ = f32[32,1024]{1,0:T(8,128)S(1)} custom-call(s32[1,4]{1,0:T(1,128)S(1)} %copy-done.13, bf16[3072,128]{1,0:T(8,128)(2,1)S(1)} %get-tuple-element.12.left_ref, bf16[128,3072]{1,0:T(8,128)(2,1)S(1)} %get-tuple-element.13.right_ref, bf16[3072,128]{1,0:T(8,128)(2,1)S(1)} %get-tuple-element.14.dd_ref, f32[4,32,128]{2,1,0:T(8,128)S(1)} %slice_add_fusion.after_ref), custom_call_target="tpu_custom_call" | custom-call | tf_op jit(solution)/shard_map/near_part/pallas_call | solution.py:264
  32.5 0.0 collective-permute-done.3
  32.5 0.0 collective-permute-done.2
  32.5 0.0 collective-permute-done.1
  32.6 0.0 copy-start.14
  32.6 4.7 %collective-permute-start.5 = (f32[1,32,128]{2,1,0:T(8,128)S(1)}, f32[1,32,128]{2,1,0:T(8,128)S(1)}, u32[]{:S(2)}, u32[]{:S(2)}) collective-permute-start(f32[1,32,128]{2,1,0:T(8,128)S(1)} %slice.94), channel_id=1, source_target_pairs={{0,16},{1,17},{2,18},{3,19},{4,20},{5,21},{6,22},{7,23},{8,24},{9,... | collective-permute-start | bytes 49160 | tf_op jit(solution)/shard_map/ppermute | solution.py:447
  37.3 2.5 %collective-permute-start.6 = (f32[1,32,128]{2,1,0:T(8,128)S(1)}, f32[1,32,128]{2,1,0:T(8,128)S(1)}, u32[]{:S(2)}, u32[]{:S(2)}) collective-permute-start(f32[1,32,128]{2,1,0:T(8,128)S(1)} %slice.94), channel_id=1, source_target_pairs={{0,24},{1,25},{2,26},{3,27},{4,28},{5,29},{6,30},{7,31},{8,16},{9,... | collective-permute-start | bytes 49160 | tf_op jit(solution)/shard_map/ppermute | solution.py:447
  39.9 0.2 collective-permute-start.4
  40.1 0.0 copy-done.14
  40.1 0.0 copy-start.1
  40.1 0.0 copy-start.3
  40.1 0.0 copy-start.4
  40.2 0.0 copy-start.6
  40.2 8.3 %near_part.5.rest_7_ = f32[32,1024]{1,0:T(8,128)S(1)} custom-call(s32[1,4]{1,0:T(1,128)S(1)} %copy-done.14, bf16[3072,128]{1,0:T(8,128)(2,1)S(1)} %get-tuple-element.12.left_ref, bf16[128,3072]{1,0:T(8,128)(2,1)S(1)} %get-tuple-element.13.right_ref, bf16[3072,128]{1,0:T(8,128)(2,1)S(1)} %get-tuple-element.14.dd_ref, f32[2,32,128]{2,1,0:T(8,128)S(1)} %slice_add_fusion.1.after_ref), custom_call_target="tpu_custom_call" | custom-call | tf_op jit(solution)/shard_map/near_part/pallas_call | solution.py:264
  48.5 0.0 collective-permute-done.5
  48.5 0.0 collective-permute-done.6
  48.5 0.0 collective-permute-done.4
  48.6 0.0 copy-done.1
  48.6 0.0 copy-done.3
  48.6 0.0 copy-done.4
  48.6 0.0 copy-done.6
  48.6 0.0 copy-start.10
  48.6 2.3 %descend.1 = (f32[32,3072]{1,0:T(8,128)S(1)}, f32[32,128]{1,0:T(8,128)S(1)}) custom-call(s32[1,4]{1,0:T(1,128)S(1)} %copy-done.14, f32[1]{0:T(128)S(6)} %copy.19.noise_ref, f32[1]{0:T(128)S(6)} %copy.18.scale_ref, f32[32,3072]{1,0:T(8,128)S(1)} %copy-done.1, f32[32,3072]{1,0:T(8,128)S(1)} %copy-done.4, bf16[128,3072]{1,0:T(8,128)(2,1)S(1)} %copy-done.3, ...), custom_call_target="tpu_custom_call" | custom-call | tf_op jit(solution)/shard_map/descend/pallas_call | solution.py:376
  50.9 0.1 collective-permute-start.7
  50.9 1.2 %collective-permute-done.7.refs_1_ = f32[32,128]{1,0:T(8,128)S(1)} collective-permute-done((f32[32,128]{1,0:T(8,128)S(1)}, f32[32,128]{1,0:T(8,128)S(1)}, u32[]{:S(2)}, u32[]{:S(2)}) %collective-permute-start.7) | collective-permute-done | bytes 16416 | tf_op jit(solution)/shard_map/ppermute | solution.py:447
  52.1 0.0 copy-done.15
  52.1 0.6 copy-done.20
  52.7 1.4 %merge.2.refs_0_ = f32[32,128]{1,0:T(8,128)} custom-call(f32[32,128]{1,0:T(8,128)} %copy-done.15, f32[32,128]{1,0:T(8,128)} %copy-done.20), custom_call_target="tpu_custom_call" | custom-call | tf_op jit(solution)/shard_map/merge/pallas_call | solution.py:409
  54.2 0.4 collective-permute-start.10
  54.6 1.5 %collective-permute-start.9 = (f32[32,128]{1,0:T(8,128)}, f32[32,128]{1,0:T(8,128)S(1)}, u32[]{:S(2)}, u32[]{:S(2)}) collective-permute-start(f32[32,128]{1,0:T(8,128)} %merge.2.refs_0_), channel_id=1, source_target_pairs={{0,4},{1,5},{2,6},{3,7},{4,0},{5,1},{6,2},{7,3},{8,12},{9,13},{10,... | collective-permute-start | bytes 49160 | tf_op jit(solution)/shard_map/ppermute | solution.py:447
  56.0 1.6 %collective-permute-start.8 = (f32[32,128]{1,0:T(8,128)}, f32[32,128]{1,0:T(8,128)S(1)}, u32[]{:S(2)}, u32[]{:S(2)}) collective-permute-start(f32[32,128]{1,0:T(8,128)} %merge.2.refs_0_), channel_id=1, source_target_pairs={{0,2},{1,3},{2,0},{3,1},{4,6},{5,7},{6,4},{7,5},{8,10},{9,11},{10,... | collective-permute-start | bytes 49160 | tf_op jit(solution)/shard_map/ppermute | solution.py:447
  57.6 1.5 %collective-permute-done.10.refs_3_ = f32[32,128]{1,0:T(8,128)S(1)} collective-permute-done((f32[32,128]{1,0:T(8,128)}, f32[32,128]{1,0:T(8,128)S(1)}, u32[]{:S(2)}, u32[]{:S(2)}) %collective-permute-start.10) | collective-permute-done | bytes 16416 | tf_op jit(solution)/shard_map/ppermute | solution.py:447
  59.1 0.0 collective-permute-done.9.refs_2_
  59.1 0.9 %collective-permute-done.8.refs_1_ = f32[32,128]{1,0:T(8,128)S(1)} collective-permute-done((f32[32,128]{1,0:T(8,128)}, f32[32,128]{1,0:T(8,128)S(1)}, u32[]{:S(2)}, u32[]{:S(2)}) %collective-permute-start.8) | collective-permute-done | bytes 16416 | tf_op jit(solution)/shard_map/ppermute | solution.py:447
  60.0 0.0 copy-done.17
  60.0 0.6 copy-done.19
  60.6 1.5 %merge.3.refs_0_ = f32[32,128]{1,0:T(8,128)} custom-call(f32[32,128]{1,0:T(8,128)} %merge.2.refs_0_, f32[32,128]{1,0:T(8,128)} %copy-done.19, f32[32,128]{1,0:T(8,128)} %copy-done.18, f32[32,128]{1,0:T(8,128)} %copy-done.17), custom_call_target="tpu_custom_call" | custom-call | tf_op jit(solution)/shard_map/merge/pallas_call | solution.py:409
  62.1 2.2 %collective-permute-start.13 = (f32[32,128]{1,0:T(8,128)}, f32[32,128]{1,0:T(8,128)S(1)}, u32[]{:S(2)}, u32[]{:S(2)}) collective-permute-start(f32[32,128]{1,0:T(8,128)} %merge.3.refs_0_), channel_id=1, source_target_pairs={{0,24},{1,25},{2,26},{3,27},{4,28},{5,29},{6,30},{7,31},{8,16},{9,... | collective-permute-start | bytes 49160 | tf_op jit(solution)/shard_map/ppermute | solution.py:447
  64.3 1.3 %collective-permute-start.12 = (f32[32,128]{1,0:T(8,128)}, f32[32,128]{1,0:T(8,128)S(1)}, u32[]{:S(2)}, u32[]{:S(2)}) collective-permute-start(f32[32,128]{1,0:T(8,128)} %merge.3.refs_0_), channel_id=1, source_target_pairs={{0,16},{1,17},{2,18},{3,19},{4,20},{5,21},{6,22},{7,23},{8,24},{9,... | collective-permute-start | bytes 49160 | tf_op jit(solution)/shard_map/ppermute | solution.py:447
  65.6 0.9 %collective-permute-start.11 = (f32[32,128]{1,0:T(8,128)}, f32[32,128]{1,0:T(8,128)S(1)}, u32[]{:S(2)}, u32[]{:S(2)}) collective-permute-start(f32[32,128]{1,0:T(8,128)} %merge.3.refs_0_), channel_id=1, source_target_pairs={{0,8},{1,9},{2,10},{3,11},{4,12},{5,13},{6,14},{7,15},{8,0},{9,1},... | collective-permute-start | bytes 49160 | tf_op jit(solution)/shard_map/ppermute | solution.py:447
  66.5 1.4 %collective-permute-done.13.refs_3_ = f32[32,128]{1,0:T(8,128)S(1)} collective-permute-done((f32[32,128]{1,0:T(8,128)}, f32[32,128]{1,0:T(8,128)S(1)}, u32[]{:S(2)}, u32[]{:S(2)}) %collective-permute-start.13) | collective-permute-done | bytes 16416 | tf_op jit(solution)/shard_map/ppermute | solution.py:447
  67.9 1.2 %collective-permute-done.12.refs_2_ = f32[32,128]{1,0:T(8,128)S(1)} collective-permute-done((f32[32,128]{1,0:T(8,128)}, f32[32,128]{1,0:T(8,128)S(1)}, u32[]{:S(2)}, u32[]{:S(2)}) %collective-permute-start.12) | collective-permute-done | bytes 16416 | tf_op jit(solution)/shard_map/ppermute | solution.py:447
  69.1 0.4 collective-permute-done.11.refs_1_
  69.5 0.0 copy-done.10
  69.5 0.7 %copy-done.11 = f32[32,128]{1,0:T(8,128)S(1)} copy-done((f32[32,128]{1,0:T(8,128)S(1)}, f32[32,128]{1,0:T(8,128)}, u32[]{:S(2)}) %copy-start.11) | copy-done | bytes 16408
  70.3 1.4 %finish.1 = (f32[32,3072]{1,0:T(8,128)}, f32[32,3072]{1,0:T(8,128)}, f32[32,3072]{1,0:T(8,128)}) custom-call(f32[32,128]{1,0:T(8,128)S(1)} %copy-done.11, f32[32,128]{1,0:T(8,128)S(1)} %collective-permute-done.11.refs_1_, f32[32,128]{1,0:T(8,128)S(1)} %collective-permute-done.12.refs_2_, f32[32,128]{1,0:T(8,128)S(1)} %collective-permute-done.13.refs_3_, ...), custom_call_target="tpu_custom_call" | custom-call | tf_op jit(solution)/shard_map/finish/pallas_call | solution.py:435
  (22 shorter events, 0.1 us)
Async XLA Ops:
  0.6 1.0 %copy-start = (f32[32,3072]{1,0:T(8,128)S(1)}, f32[32,3072]{1,0:T(8,128)}, u32[]{:S(2)}) copy-start(f32[32,3072]{1,0:T(8,128)} %refs_6_.1) | copy-start | bytes 1179652
  1.6 1.1 %copy-start.2 = (bf16[128,3072]{1,0:T(8,128)(2,1)S(1)}, bf16[128,3072]{1,0:T(8,128)(2,1)}, u32[]{:S(2)}) copy-start(bf16[128,3072]{1,0:T(8,128)(2,1)} %basis_ref.3) | copy-start | bytes 2359300
  2.8 0.9 %copy-start.5 = (bf16[1,7,128,128]{3,2,1,0:T(8,128)(2,1)S(1)}, bf16[1,7,128,128]{3,2,1,0:T(8,128)(2,1)}, u32[]{:S(2)}) copy-start(bf16[1,7,128,128]{3,2,1,0:T(8,128)(2,1)} %nt_ref.3) | copy-start | bytes 688132
  3.7 0.9 %copy-start.7 = (bf16[1,7,128,128]{3,2,1,0:T(8,128)(2,1)S(1)}, bf16[1,7,128,128]{3,2,1,0:T(8,128)(2,1)}, u32[]{:S(2)}) copy-start(bf16[1,7,128,128]{3,2,1,0:T(8,128)(2,1)} %nc_ref.3) | copy-start | bytes 688132
  4.6 0.9 %copy-start.8 = (bf16[1,4,128,128]{3,2,1,0:T(8,128)(2,1)S(1)}, bf16[1,4,128,128]{3,2,1,0:T(8,128)(2,1)}, u32[]{:S(2)}) copy-start(bf16[1,4,128,128]{3,2,1,0:T(8,128)(2,1)} %uc_ref.3) | copy-start | bytes 393220
  5.5 0.9 %copy-start.9 = (bf16[1,3,128,128]{3,2,1,0:T(8,128)(2,1)S(1)}, bf16[1,3,128,128]{3,2,1,0:T(8,128)(2,1)}, u32[]{:S(2)}) copy-start(bf16[1,3,128,128]{3,2,1,0:T(8,128)(2,1)} %ut_ref.3) | copy-start | bytes 294916
  6.4 0.7 copy-start.13
  7.1 4.5 %copy-start.12 = (f32[3,3072]{1,0:T(4,128)S(1)}, f32[3,3072]{1,0:T(4,128)}, u32[]{:S(2)}) copy-start(f32[3,3072]{1,0:T(4,128)} %coords_ref.1) | copy-start | bytes 110596
  7.1 4.5 %copy-start.16 = (s32[3072]{0:T(1024)S(1)}, s32[3072]{0:T(1024)}, u32[]{:S(2)}) copy-start(s32[3072]{0:T(1024)} %param.18) | copy-start | bytes 36868
  9.2 10.9 %collective-permute-start = (f32[5,32,128]{2,1,0:T(8,128)S(1)}, f32[5,32,128]{2,1,0:T(8,128)S(1)}, u32[]{:S(2)}, u32[]{:S(2)}) collective-permute-start(f32[5,32,128]{2,1,0:T(8,128)S(1)} %get-tuple-element.11.after_ref), channel_id=1, source_target_pairs={{0,1},{1,0},{2,3},{3,2},{4,5},{5,4},{6,7},{7,6},{8,9},{9,8},{10,11... | collective-permute-start | bytes 245768 | tf_op jit(solution)/shard_map/ppermute | solution.py:447
  20.1 12.4 %collective-permute-start.3 = (f32[3,32,128]{2,1,0:T(8,128)S(1)}, f32[3,32,128]{2,1,0:T(8,128)S(1)}, u32[]{:S(2)}, u32[]{:S(2)}) collective-permute-start(f32[3,32,128]{2,1,0:T(8,128)S(1)} %slice.85), channel_id=1, source_target_pairs={{0,6},{1,7},{2,4},{3,5},{4,2},{5,3},{6,0},{7,1},{8,14},{9,15},{10,... | collective-permute-start | bytes 147464 | tf_op jit(solution)/shard_map/ppermute | solution.py:447
  24.4 8.1 %collective-permute-start.2 = (f32[3,32,128]{2,1,0:T(8,128)S(1)}, f32[3,32,128]{2,1,0:T(8,128)S(1)}, u32[]{:S(2)}, u32[]{:S(2)}) collective-permute-start(f32[3,32,128]{2,1,0:T(8,128)S(1)} %slice.85), channel_id=1, source_target_pairs={{0,4},{1,5},{2,6},{3,7},{4,0},{5,1},{6,2},{7,3},{8,12},{9,13},{10,... | collective-permute-start | bytes 147464 | tf_op jit(solution)/shard_map/ppermute | solution.py:447
  25.7 6.8 %collective-permute-start.1 = (f32[4,32,128]{2,1,0:T(8,128)S(1)}, f32[4,32,128]{2,1,0:T(8,128)S(1)}, u32[]{:S(2)}, u32[]{:S(2)}) collective-permute-start(f32[4,32,128]{2,1,0:T(8,128)S(1)} %slice_add_fusion.after_ref), channel_id=1, source_target_pairs={{0,2},{1,3},{2,0},{3,1},{4,6},{5,7},{6,4},{7,5},{8,10},{9,11},{10,... | collective-permute-start | bytes 196616 | tf_op jit(solution)/shard_map/ppermute | solution.py:447
  32.6 7.5 %copy-start.14 = (s32[1,4]{1,0:T(1,128)S(1)}, s32[1,4]{1,0:T(1,128)}, u32[]{:S(2)}) copy-start(s32[1,4]{1,0:T(1,128)} %sizes_ref.11) | copy-start | bytes 52
  32.6 15.9 %collective-permute-start.5 = (f32[1,32,128]{2,1,0:T(8,128)S(1)}, f32[1,32,128]{2,1,0:T(8,128)S(1)}, u32[]{:S(2)}, u32[]{:S(2)}) collective-permute-start(f32[1,32,128]{2,1,0:T(8,128)S(1)} %slice.94), channel_id=1, source_target_pairs={{0,16},{1,17},{2,18},{3,19},{4,20},{5,21},{6,22},{7,23},{8,24},{9,... | collective-permute-start | bytes 49160 | tf_op jit(solution)/shard_map/ppermute | solution.py:447
  37.3 11.2 %collective-permute-start.6 = (f32[1,32,128]{2,1,0:T(8,128)S(1)}, f32[1,32,128]{2,1,0:T(8,128)S(1)}, u32[]{:S(2)}, u32[]{:S(2)}) collective-permute-start(f32[1,32,128]{2,1,0:T(8,128)S(1)} %slice.94), channel_id=1, source_target_pairs={{0,24},{1,25},{2,26},{3,27},{4,28},{5,29},{6,30},{7,31},{8,16},{9,... | collective-permute-start | bytes 49160 | tf_op jit(solution)/shard_map/ppermute | solution.py:447
  39.9 8.7 %collective-permute-start.4 = (f32[2,32,128]{2,1,0:T(8,128)S(1)}, f32[2,32,128]{2,1,0:T(8,128)S(1)}, u32[]{:S(2)}, u32[]{:S(2)}) collective-permute-start(f32[2,32,128]{2,1,0:T(8,128)S(1)} %slice_add_fusion.1.after_ref), channel_id=1, source_target_pairs={{0,8},{1,9},{2,10},{3,11},{4,12},{5,13},{6,14},{7,15},{8,0},{9,1},... | collective-permute-start | bytes 98312 | tf_op jit(solution)/shard_map/ppermute | solution.py:447
  40.1 8.4 %copy-start.1 = (f32[32,3072]{1,0:T(8,128)S(1)}, f32[32,3072]{1,0:T(8,128)}, u32[]{:S(2)}) copy-start(f32[32,3072]{1,0:T(8,128)} %refs_6_.1) | copy-start | bytes 1179652
  40.1 8.4 %copy-start.3 = (bf16[128,3072]{1,0:T(8,128)(2,1)S(1)}, bf16[128,3072]{1,0:T(8,128)(2,1)}, u32[]{:S(2)}) copy-start(bf16[128,3072]{1,0:T(8,128)(2,1)} %basis_ref.3) | copy-start | bytes 2359300
  40.1 8.4 %copy-start.4 = (f32[32,3072]{1,0:T(8,128)S(1)}, f32[32,3072]{1,0:T(8,128)}, u32[]{:S(2)}) copy-start(f32[32,3072]{1,0:T(8,128)} %refs_5_.1) | copy-start | bytes 1179652
  40.2 8.4 %copy-start.6 = (bf16[1,7,128,128]{3,2,1,0:T(8,128)(2,1)S(1)}, bf16[1,7,128,128]{3,2,1,0:T(8,128)(2,1)}, u32[]{:S(2)}) copy-start(bf16[1,7,128,128]{3,2,1,0:T(8,128)(2,1)} %nt_ref.3) | copy-start | bytes 688132
  48.6 20.9 %copy-start.10 = (f32[32,3072]{1,0:T(8,128)S(1)}, f32[32,3072]{1,0:T(8,128)}, u32[]{:S(2)}) copy-start(f32[32,3072]{1,0:T(8,128)} %refs_4_.1) | copy-start | bytes 1179652
  50.9 1.2 %copy-start.15 = (f32[32,128]{1,0:T(8,128)}, f32[32,128]{1,0:T(8,128)S(1)}, u32[]{:S(2)}) copy-start(f32[32,128]{1,0:T(8,128)S(1)} %get-tuple-element.15.refs_0_) | copy-start | bytes 49156
  50.9 1.2 %collective-permute-start.7 = (f32[32,128]{1,0:T(8,128)S(1)}, f32[32,128]{1,0:T(8,128)S(1)}, u32[]{:S(2)}, u32[]{:S(2)}) collective-permute-start(f32[32,128]{1,0:T(8,128)S(1)} %get-tuple-element.15.refs_0_), channel_id=1, source_target_pairs={{0,1},{1,0},{2,3},{3,2},{4,5},{5,4},{6,7},{7,6},{8,9},{9,8},{10,11... | collective-permute-start | bytes 49160 | tf_op jit(solution)/shard_map/ppermute | solution.py:447
  52.1 0.6 copy-start.20
  54.2 4.9 %collective-permute-start.10 = (f32[32,128]{1,0:T(8,128)}, f32[32,128]{1,0:T(8,128)S(1)}, u32[]{:S(2)}, u32[]{:S(2)}) collective-permute-start(f32[32,128]{1,0:T(8,128)} %merge.2.refs_0_), channel_id=1, source_target_pairs={{0,6},{1,7},{2,4},{3,5},{4,2},{5,3},{6,0},{7,1},{8,14},{9,15},{10,... | collective-permute-start | bytes 49160 | tf_op jit(solution)/shard_map/ppermute | solution.py:447
  54.6 4.5 %collective-permute-start.9 = (f32[32,128]{1,0:T(8,128)}, f32[32,128]{1,0:T(8,128)S(1)}, u32[]{:S(2)}, u32[]{:S(2)}) collective-permute-start(f32[32,128]{1,0:T(8,128)} %merge.2.refs_0_), channel_id=1, source_target_pairs={{0,4},{1,5},{2,6},{3,7},{4,0},{5,1},{6,2},{7,3},{8,12},{9,13},{10,... | collective-permute-start | bytes 49160 | tf_op jit(solution)/shard_map/ppermute | solution.py:447
  56.0 3.9 %collective-permute-start.8 = (f32[32,128]{1,0:T(8,128)}, f32[32,128]{1,0:T(8,128)S(1)}, u32[]{:S(2)}, u32[]{:S(2)}) collective-permute-start(f32[32,128]{1,0:T(8,128)} %merge.2.refs_0_), channel_id=1, source_target_pairs={{0,2},{1,3},{2,0},{3,1},{4,6},{5,7},{6,4},{7,5},{8,10},{9,11},{10,... | collective-permute-start | bytes 49160 | tf_op jit(solution)/shard_map/ppermute | solution.py:447
  59.1 0.9 %copy-start.17 = (f32[32,128]{1,0:T(8,128)}, f32[32,128]{1,0:T(8,128)S(1)}, u32[]{:S(2)}) copy-start(f32[32,128]{1,0:T(8,128)S(1)} %collective-permute-done.10.refs_3_) | copy-start | bytes 49156
  59.1 0.9 %copy-start.18 = (f32[32,128]{1,0:T(8,128)}, f32[32,128]{1,0:T(8,128)S(1)}, u32[]{:S(2)}) copy-start(f32[32,128]{1,0:T(8,128)S(1)} %collective-permute-done.9.refs_2_) | copy-start | bytes 49156
  60.0 0.6 copy-start.19
  62.1 5.8 %collective-permute-start.13 = (f32[32,128]{1,0:T(8,128)}, f32[32,128]{1,0:T(8,128)S(1)}, u32[]{:S(2)}, u32[]{:S(2)}) collective-permute-start(f32[32,128]{1,0:T(8,128)} %merge.3.refs_0_), channel_id=1, source_target_pairs={{0,24},{1,25},{2,26},{3,27},{4,28},{5,29},{6,30},{7,31},{8,16},{9,... | collective-permute-start | bytes 49160 | tf_op jit(solution)/shard_map/ppermute | solution.py:447
  64.3 4.8 %collective-permute-start.12 = (f32[32,128]{1,0:T(8,128)}, f32[32,128]{1,0:T(8,128)S(1)}, u32[]{:S(2)}, u32[]{:S(2)}) collective-permute-start(f32[32,128]{1,0:T(8,128)} %merge.3.refs_0_), channel_id=1, source_target_pairs={{0,16},{1,17},{2,18},{3,19},{4,20},{5,21},{6,22},{7,23},{8,24},{9,... | collective-permute-start | bytes 49160 | tf_op jit(solution)/shard_map/ppermute | solution.py:447
  65.6 3.9 %collective-permute-start.11 = (f32[32,128]{1,0:T(8,128)}, f32[32,128]{1,0:T(8,128)S(1)}, u32[]{:S(2)}, u32[]{:S(2)}) collective-permute-start(f32[32,128]{1,0:T(8,128)} %merge.3.refs_0_), channel_id=1, source_target_pairs={{0,8},{1,9},{2,10},{3,11},{4,12},{5,13},{6,14},{7,15},{8,0},{9,1},... | collective-permute-start | bytes 49160 | tf_op jit(solution)/shard_map/ppermute | solution.py:447
  69.5 0.7 %copy-start.11 = (f32[32,128]{1,0:T(8,128)S(1)}, f32[32,128]{1,0:T(8,128)}, u32[]{:S(2)}) copy-start(f32[32,128]{1,0:T(8,128)} %merge.3.refs_0_) | copy-start | bytes 49156

commit v2 on v1

--- a/solution.py
+++ b/solution.py
@@ -20,6 +20,8 @@
 VMEM = pl.BlockSpec(memory_space=pltpu.VMEM)
 SMEM = pl.BlockSpec(memory_space=pltpu.SMEM)
 ANY = pl.BlockSpec(memory_space=pl.ANY)
+HBM = pl.BlockSpec(memory_space=pltpu.HBM)
+GROUP = 4
 PARAMS = pltpu.CompilerParams(vmem_limit_bytes=48 * 1024 * 1024)
 
 
@@ -63,19 +65,18 @@
     return leaf
 
 
-def up_kernel(
-    leaf_count,
-    levels,
-    sizes_ref,
-    d_ref,
-    basis_ref,
-    nt_ref,
-    nc_ref,
-    ut_ref,
-    uc_ref,
-    up_ref,
-    local_ref,
-):
+def up_kernel(leaf_count, levels, *refs):
+    sources, (up_ref, local_ref) = refs[:7], refs[7:9]
+    held, semaphores = refs[9:16], refs[16]
+    copies = [
+        pltpu.make_async_copy(source, target, semaphores.at[index])
+        for index, (source, target) in enumerate(zip(sources, held))
+    ]
+    for copy in copies:
+        copy.start()
+    for copy in copies:
+        copy.wait()
+    sizes_ref, d_ref, basis_ref, nt_ref, nc_ref, ut_ref, uc_ref = held
     probes, points = d_ref.shape
     ends = leaf_ends(sizes_ref, leaf_count)
     split = halves(d_ref[...])
@@ -124,8 +125,16 @@
             jax.ShapeDtypeStruct((levels, probes, rank), F32),
             jax.ShapeDtypeStruct((leaf_count - 1, probes, rank), F32),
         ),
-        in_specs=[SMEM] + [VMEM] * 6,
+        in_specs=[HBM] * 7,
         out_specs=(VMEM, VMEM),
+        scratch_shapes=[pltpu.SMEM(sizes.shape, jnp.int32)]
+        + [
+            pltpu.VMEM(array.shape, array.dtype)
+            for array in (
+                direction, basis, node_transfer, node_coupling, upper_transfer, upper_coupling
+            )
+        ]
+        + [pltpu.SemaphoreType.DMA((7,))],
         compiler_params=PARAMS,
         name="climb",
     )(sizes, direction, basis, node_transfer, node_coupling, upper_transfer, upper_coupling)
@@ -163,7 +172,7 @@
                 place = 128 * (8 * group + row)
                 ordered_ref[axis : axis + 1, place : place + 128] = found[row : row + 1, :]
     row8 = lax.broadcasted_iota(jnp.int32, (8, points), 0)
-    scale = jnp.full((1, 1), math.sqrt(5.0) * LOG2E, F32) / length_ref[0]
+    scale = (math.sqrt(5.0) * LOG2E) / length_ref[...]
     scaled = jnp.where(row8 < 3, (ordered_ref[...] - 0.5) * scale, 0.0)
     z1 = scaled.astype(BF16).astype(F32)
     z2 = (scaled - z1).astype(BF16).astype(F32)
@@ -189,7 +198,8 @@
         [z1, z2, z1, z2, norm_right, leaf_right] + [jnp.zeros((80, points), F32)], axis=0
     )
     right_ref[...] = right.astype(BF16)
-    left_ref[...] = left.T.astype(BF16)
+    left_ref[:points, :] = left.T.astype(BF16)
+    left_ref[points:, :] = jnp.zeros((TILE, 128), BF16)
     split = halves(d_ref[...]).astype(F32)
     split = jnp.concatenate([split, jnp.zeros((128 - split.shape[0], points), F32)], axis=0)
     dd_ref[...] = split.T.astype(BF16)
@@ -201,80 +211,99 @@
     return pl.pallas_call(
         functools.partial(features_kernel, leaf_count),
         out_shape=(
-            jax.ShapeDtypeStruct((points, 128), BF16),
+            jax.ShapeDtypeStruct((points + TILE, 128), BF16),
             jax.ShapeDtypeStruct((128, points), BF16),
             jax.ShapeDtypeStruct((points, 128), BF16),
         ),
-        in_specs=[SMEM, SMEM, VMEM, VMEM, VMEM, ANY],
+        in_specs=[SMEM, VMEM, VMEM, VMEM, VMEM, ANY],
         out_specs=(VMEM, VMEM, VMEM),
         scratch_shapes=[pltpu.VMEM((8, points), F32)],
         compiler_params=PARAMS,
         name="features",
-    )(sizes, lengthscale, coordinates, order.reshape(-1, 128), direction, after)
-
-
-def near_kernel(leaf_count, probes, first, sizes_ref, left_ref, right_ref, dd_ref, after_ref, out_ref):
-    ends = leaf_ends(sizes_ref, leaf_count)
-    count = out_ref.shape[1] // TILE
-
-    def one_tile(step, carry):
-        row = first + step
-        begin = row * TILE
-        last = begin + TILE - 1
+    )(sizes, lengthscale.reshape(1, 1), coordinates, order.reshape(-1, 128), direction, after)
+
+
+def tile_spans(ends, tiles):
+    lows, counts = [], []
+    for tile in range(tiles):
+        begin, last = tile * TILE, tile * TILE + TILE - 1
         low = 0
         high = ends[-1]
         for end in ends:
             low = jnp.where(end <= begin, end, low)
         for end in ends[::-1]:
             high = jnp.where(end > last, end, high)
-        left = left_ref[pl.ds(pl.multiple_of(begin, TILE), TILE), :]
-
-        def one_block(block, total):
-            place = pl.multiple_of(block * TILE, TILE)
-            squared = jnp.dot(left, right_ref[:, pl.ds(place, TILE)], preferred_element_type=F32)
+        low = lax.div(low, TILE)
+        lows.append(low)
+        counts.append(lax.div(high - 1, TILE) + 1 - low)
+    return lows, counts
+
+
+def near_kernel(leaf_count, part, parts, sizes_ref, left_ref, right_ref, dd_ref, before_ref, after_ref, out_ref):
+    ends = leaf_ends(sizes_ref, leaf_count)
+    tiles = right_ref.shape[1] // TILE
+    lows, counts = tile_spans(ends, tiles)
+    firsts = [0]
+    for count in counts:
+        firsts.append(firsts[-1] + count)
+    groups = lax.div(firsts[-1] + (GROUP - 1), GROUP)
+    offsets = [low - first for low, first in zip(lows, firsts)]
+    if part == 0:
+        out_ref[...] = jnp.zeros_like(out_ref)
+
+    def one_group(group, carry):
+        for unit in range(GROUP):
+            item = group * GROUP + unit
+            row = 0
+            offset = offsets[0]
+            for tile in range(1, tiles):
+                inside = item >= firsts[tile]
+                row = jnp.where(inside, tile, row)
+                offset = jnp.where(inside, offsets[tile], offset)
+            spare = item >= firsts[-1]
+            row = jnp.where(spare, tiles, row)
+            column = jnp.where(spare, 0, item + offset)
+            begin = pl.multiple_of(row * TILE, TILE)
+            place = pl.multiple_of(column * TILE, TILE)
+            squared = jnp.dot(
+                left_ref[pl.ds(begin, TILE), :],
+                right_ref[:, pl.ds(place, TILE)],
+                preferred_element_type=F32,
+            )
             squared = jnp.maximum(squared, 1e-12)
             root = squared * lax.rsqrt(squared)
             kernel = (squared + LINEAR * root + CONSTANT) * jnp.exp2(-root)
             high_part = kernel.astype(BF16)
             low_part = (kernel - high_part.astype(F32)).astype(BF16)
             weights = dd_ref[pl.ds(place, TILE), :]
-            return (
-                total
-                + jnp.dot(high_part, weights, preferred_element_type=F32)
-                + jnp.dot(low_part, weights, preferred_element_type=F32)
+            out_ref[pl.ds(begin, TILE), :] += jnp.dot(
+                jnp.concatenate([high_part, low_part], axis=1),
+                jnp.concatenate([weights, weights], axis=0),
+                preferred_element_type=F32,
             )
-
-        total = lax.fori_loop(
-            lax.shift_right_logical(low, 8),
-            lax.shift_right_logical(high - 1, 8) + 1,
-            one_block,
-            jnp.zeros((TILE, 128), F32),
-        )
-        flipped = total.T
-        out_ref[:, pl.ds(pl.multiple_of(step * TILE, TILE), TILE)] = (
-            flipped[:probes] + flipped[probes : 2 * probes]
-        )
         return carry
 
-    lax.fori_loop(0, count, one_tile, 0)
-
-
-def near_part(sizes, left, right, dd, after, probes, first, count):
+    lax.fori_loop(
+        lax.div(groups * part, parts), lax.div(groups * (part + 1), parts), one_group, 0
+    )
+
+
+def near_part(sizes, left, right, dd, before, after, part, parts):
     leaf_count = sizes.shape[1]
     return pl.pallas_call(
-        functools.partial(near_kernel, leaf_count, probes, first),
-        out_shape=jax.ShapeDtypeStruct((probes, count * TILE), F32),
-        in_specs=[SMEM, VMEM, VMEM, VMEM, ANY],
+        functools.partial(near_kernel, leaf_count, part, parts),
+        out_shape=jax.ShapeDtypeStruct(left.shape, F32),
+        in_specs=[SMEM, VMEM, VMEM, VMEM, ANY if part == 0 else VMEM, ANY],
         out_specs=VMEM,
+        input_output_aliases={} if part == 0 else {4: 0},
         compiler_params=PARAMS,
         name="near_part",
-    )(sizes, left, right, dd, after)
+    )(sizes, left, right, dd, before, after)
 
 
 def down_kernel(
     leaf_count,
     levels,
-    parts,
     sizes_ref,
     noise_ref,
     scale_ref,
@@ -289,8 +318,7 @@
     *rest,
 ):
     side_refs = rest[:levels]
-    near_refs = rest[levels : levels + parts]
-    a_ref, sums_ref = rest[levels + parts :]
+    near_ref, a_ref, sums_ref = rest[levels:]
     probes, points = d_ref.shape
     down = None
     for level in range(levels - 1, -1, -1):
@@ -320,13 +348,12 @@
         current = following
     stacked = jnp.concatenate([halves(term) for term in current], axis=0)
     ends = leaf_ends(sizes_ref, leaf_count)
-    noise = noise_ref[0]
-    near_scale = scale_ref[0] * POLY
+    noise = noise_ref[...]
+    near_scale = scale_ref[...] * POLY
     width = 512
     peak = jnp.zeros((probes, 128), F32)
     old = jnp.zeros((probes, 128), F32)
     curve = jnp.zeros((probes, 128), F32)
-    per_part = near_refs[0].shape[1]
 
     def lanes(x):
         return sum(x[:, 128 * i : 128 * i + 128] for i in range(width // 128))
@@ -342,8 +369,8 @@
             far = jnp.where(leaf == index, term, far)
         d = d_ref[:, first : first + width]
         r = r_ref[:, first : first + width]
-        at = first % per_part
-        near = near_refs[first // per_part][:, at : at + width]
+        near = near_ref[first : first + width, :].T
+        near = near[:probes] + near[probes : 2 * probes]
         applied = noise * d + near_scale * near + far
         a_ref[:, first : first + width] = applied
         size = jnp.abs(applied)
@@ -364,65 +391,49 @@
     sums = jnp.where(lane == 1, jnp.sum(curve, axis=1, keepdims=True), sums)
     sums = jnp.where(lane == 2, jnp.sum(cross, axis=1, keepdims=True), sums)
     sums = jnp.where(lane == 3, jnp.sum(square, axis=1, keepdims=True), sums)
-    sums_ref[...] = jnp.where(lane == 4, top, sums)
+    sums_ref[...] = jnp.where(lane == 4, top, sums).T[:8]
 
 
 def descend(
     sizes, noise, scale, direction, residual, basis, node_transfer, node_coupling,
-    upper_transfer, upper_coupling, local, sides, nears,
+    upper_transfer, upper_coupling, local, sides, near,
 ):
     leaf_count = sizes.shape[1]
     probes, points = direction.shape
     return pl.pallas_call(
-        functools.partial(down_kernel, leaf_count, len(sides), len(nears)),
+        functools.partial(down_kernel, leaf_count, len(sides)),
         out_shape=(
             jax.ShapeDtypeStruct((probes, points), F32),
-            jax.ShapeDtypeStruct((probes, 128), F32),
+            jax.ShapeDtypeStruct((8, probes), F32),
         ),
-        in_specs=[SMEM, SMEM, SMEM] + [VMEM] * (8 + len(sides) + len(nears)),
+        in_specs=[SMEM] + [VMEM] * (11 + len(sides)),
         out_specs=(VMEM, VMEM),
         compiler_params=PARAMS,
         name="descend",
     )(
-        sizes, noise, scale, direction, residual, basis, node_transfer, node_coupling,
-        upper_transfer, upper_coupling, local, *sides, *nears,
-    )
-
-
-def merged(pieces):
-    tops = [piece[:, 4:5] for piece in pieces]
-    top = functools.reduce(jnp.maximum, tops)
-    lane = lax.broadcasted_iota(jnp.int32, pieces[0].shape, 1)
-    total = jnp.zeros_like(pieces[0])
-    for piece, own in zip(pieces, tops):
-        ratio = own / top
-        factor = jnp.where(lane < 2, 1.0, jnp.where(lane == 2, ratio, ratio * ratio))
-        total = total + piece * factor
-    return jnp.where(lane == 4, top, total)
-
-
-def merge_kernel(*refs):
-    refs[-1][...] = merged([ref[...] for ref in refs[:-1]])
-
-
-def merge(pieces):
-    return pl.pallas_call(
-        merge_kernel,
-        out_shape=jax.ShapeDtypeStruct(pieces[0].shape, F32),
-        in_specs=[VMEM] * len(pieces),
-        out_specs=VMEM,
-        name="merge",
-    )(*pieces)
-
-
-def step_kernel(pieces, *refs):
-    sums = merged([ref[...] for ref in refs[:pieces]])
-    x_ref, r_ref, d_ref, a_ref, nx_ref, nr_ref, nd_ref = refs[pieces:]
-    old, curve, cross, square, top = (sums[:, i : i + 1] for i in range(5))
+        sizes, noise.reshape(1, 1), scale.reshape(1, 1), direction, residual, basis,
+        node_transfer, node_coupling, upper_transfer, upper_coupling, local, *sides, near,
+    )
+
+
+def step_kernel(sums_ref, x_ref, r_ref, d_ref, a_ref, nx_ref, nr_ref, nd_ref):
+    sums = sums_ref[...]
+    probes = d_ref.shape[0]
+    tops = sums[:, 4:5, :]
+    top = jnp.max(tops, axis=0)
+    ratio = tops / top
+    old, curve = jnp.sum(sums[:, 0:1, :], axis=0), jnp.sum(sums[:, 1:2, :], axis=0)
+    cross = jnp.sum(sums[:, 2:3, :] * ratio, axis=0)
+    square = jnp.sum(sums[:, 3:4, :] * (ratio * ratio), axis=0)
     step = old / curve
     reach = step * top
     fresh = old - 2.0 * (reach * cross) + (reach * reach) * square
     beta = fresh / old
+    own = lax.broadcasted_iota(jnp.int32, (probes, probes), 0) == lax.broadcasted_iota(
+        jnp.int32, (probes, probes), 1
+    )
+    step = jnp.sum(jnp.where(own, step, 0.0), axis=1, keepdims=True)
+    beta = jnp.sum(jnp.where(own, beta, 0.0), axis=1, keepdims=True)
     d = d_ref[...]
     nx_ref[...] = x_ref[...] + step * d
     remaining = r_ref[...] - step * a_ref[...]
@@ -430,16 +441,16 @@
     nd_ref[...] = remaining + beta * d
 
 
-def finish(pieces, solution_block, residual, direction, applied):
+def finish(sums, solution_block, residual, direction, applied):
     shape = jax.ShapeDtypeStruct(direction.shape, F32)
     return pl.pallas_call(
-        functools.partial(step_kernel, len(pieces)),
+        step_kernel,
         out_shape=(shape, shape, shape),
-        in_specs=[VMEM] * (len(pieces) + 4),
+        in_specs=[VMEM] * 5,
         out_specs=(VMEM, VMEM, VMEM),
         compiler_params=PARAMS,
         name="finish",
-    )(*pieces, solution_block, residual, direction, applied)
+    )(sums, solution_block, residual, direction, applied)
 
 
 def from_partner(array, stride):
@@ -479,12 +490,10 @@
         upper_transfer, upper_coupling, levels,
     )
     left, right, dd = features(leaf_sizes, lengthscale, coordinates, cluster_order, direction, up)
-    tiles = points // TILE
     groups = level_groups(levels)
     parts = 3
-    per_part = tiles // parts
     sides = [None] * levels
-    nears = []
+    near = up
     current = up
     for number, group in enumerate(groups):
         base = group[0]
@@ -495,9 +504,7 @@
             top = pick.bit_length() - 1
             incoming[pick] = from_partner(current[top:], stride)
         if number < parts:
-            nears.append(
-                near_part(leaf_sizes, left, right, dd, current, probes, number * per_part, per_part)
-            )
+            near = near_part(leaf_sizes, left, right, dd, near, current, number, parts)
         for position in range(len(group)):
             total = current[position]
             for pick in range(1, 2 ** (position + 1)):
@@ -511,21 +518,13 @@
                 following = following + incoming[pick][len(group) - top :]
         current = following
     for number in range(len(groups), parts):
-        nears.append(
-            near_part(leaf_sizes, left, right, dd, up, probes, number * per_part, per_part)
-        )
+        near = near_part(leaf_sizes, left, right, dd, near, up, number, parts)
     applied, sums = descend(
         leaf_sizes, noise_variance, outputscale, direction, residual, leaf_basis,
-        node_transfer, node_coupling, upper_transfer, upper_coupling, local, sides, nears,
-    )
-    pieces = [sums]
-    for group in groups:
-        own = merge(pieces) if len(pieces) > 1 else pieces[0]
-        pieces = [own]
-        for pick in range(1, 2 ** len(group)):
-            stride = sum(2**level for bit, level in enumerate(group) if pick >> bit & 1)
-            pieces.append(from_partner(own, stride))
-    return finish(pieces, solution, residual, direction, applied)
+        node_transfer, node_coupling, upper_transfer, upper_coupling, local, sides, near,
+    )
+    gathered = lax.all_gather(sums, "leaf")
+    return finish(gathered, solution, residual, direction, applied)
 
 
 def solution(mesh):

time: 73 us -> 86.4 us (1.18)
  blocking collectives: 0 us -> 40.7 us
  starting transfers between devices: 21.5 us -> 9.31 us
  waiting for transfers between devices: 6.67 us -> 0.02 us
  Pallas kernels: 32.1 us -> 26.3 us
  local copies, waits for them, and re-layouts: 8.44 us -> 6.5 us
    all_gather x0 -> x1, blocking collectives: none -> 40.7 us  [shards(): gathered = lax.all_gather(sums, 'leaf')]
    ppermute x14 -> x7, starting transfers between devices: 21.5 us -> 9.31 us  [from_partner(): return lax.ppermute(array, 'leaf', [(i, i ^ stride) for i in range(count)])]
    ppermute x14 -> x7, waiting for transfers between devices: 6.67 us -> 0.02 us  [from_partner(): return lax.ppermute(array, 'leaf', [(i, i ^ stride) for i in range(count)])]
    pallas_call x7 -> x5, Pallas kernels: 28.7 us -> 22.2 us  [the longest x3 18.6 us: near_part(): pl.pallas_call(functools.partial(near_kernel, leaf_count, part, parts), o...]
    unnamed x42 -> x28, local copies, waits for them, and re-layouts: 8.44 us -> 6.49 us
  transfers between devices with their start and end apart: 14 -> 7, of which waited for: 6 -> 0; matrix products, arithmetic and copies ran while one was open for 0% -> 0% of each run, Pallas kernels for 33% -> 23%
where the time goes in v2:
time: 86.4 us; the launch traced here: 85.7 us
  blocking collectives  40.7 us (47%)
  Pallas kernels  26.3 us (30%)
  starting transfers between devices  9.31 us (11%)
  local copies, waits for them, and re-layouts  6.5 us (8%)
  between operations  2.82 us (3%)
    all_gather x1, blocking collectives, shards(): gathered = lax.all_gather(sums, 'leaf')  40.7 us
    pallas_call x3, Pallas kernels, near_part(): pl.pallas_call(functools.partial(near_kernel, leaf_count, part, parts), o...  18.6 us
    ppermute x7, starting transfers between devices, from_partner(): return lax.ppermute(array, 'leaf', [(i, i ^ stride) for i in range(count)])  9.31 us
    unnamed x28, local copies, waits for them, and re-layouts  6.49 us
    pallas_call x1, Pallas kernels, climb(): pl.pallas_call(functools.partial(up_kernel, leaf_count, levels), out_shap...  2.79 us
    pallas_call x1, Pallas kernels, descend(): pl.pallas_call(functools.partial(down_kernel, leaf_count, len(sides)), ou...  2.36 us
  transfers between devices with their start and end apart: 7, of which 0 were waited for; matrix products, arithmetic and copies ran while one was open for 0% of the time, Pallas kernels for 23%

profile of v2, /device:TPU:0, one launch (start us, length us, event | category | flops | bytes accessed | tf_op | source)
XLA Modules:
  0.0 85.7 jit_solution(12136965868831918661)
XLA Ops:
  0.6 0.0 copy-start
  0.6 1.0 %copy-done = f32[32,3072]{1,0:T(8,128)S(1)} copy-done((f32[32,3072]{1,0:T(8,128)S(1)}, f32[32,3072]{1,0:T(8,128)}, u32[]{:S(2)}) %copy-start) | copy-done | bytes 393240
  1.6 0.0 copy-start.2
  1.6 1.1 %copy-done.2 = bf16[128,3072]{1,0:T(8,128)(2,1)S(1)} copy-done((bf16[128,3072]{1,0:T(8,128)(2,1)S(1)}, bf16[128,3072]{1,0:T(8,128)(2,1)}, u32[]{:S(2)}) %copy-start.2) | copy-done | bytes 786456
  2.8 0.0 copy-start.5
  2.8 0.9 %copy-done.5 = bf16[1,7,128,128]{3,2,1,0:T(8,128)(2,1)S(1)} copy-done((bf16[1,7,128,128]{3,2,1,0:T(8,128)(2,1)S(1)}, bf16[1,7,128,128]{3,2,1,0:T(8,128)(2,1)}, u32[]{:S(2)}) %copy-start.5) | copy-done | bytes 229400
  3.7 0.0 copy-start.7
  3.7 0.9 %copy-done.7 = bf16[1,7,128,128]{3,2,1,0:T(8,128)(2,1)S(1)} copy-done((bf16[1,7,128,128]{3,2,1,0:T(8,128)(2,1)S(1)}, bf16[1,7,128,128]{3,2,1,0:T(8,128)(2,1)}, u32[]{:S(2)}) %copy-start.7) | copy-done | bytes 229400
  4.6 0.0 copy-start.8
  4.6 0.9 %copy-done.8 = bf16[1,4,128,128]{3,2,1,0:T(8,128)(2,1)S(1)} copy-done((bf16[1,4,128,128]{3,2,1,0:T(8,128)(2,1)S(1)}, bf16[1,4,128,128]{3,2,1,0:T(8,128)(2,1)}, u32[]{:S(2)}) %copy-start.8) | copy-done | bytes 131096
  5.5 0.0 copy-start.9
  5.5 0.9 %copy-done.9 = bf16[1,3,128,128]{3,2,1,0:T(8,128)(2,1)S(1)} copy-done((bf16[1,3,128,128]{3,2,1,0:T(8,128)(2,1)S(1)}, bf16[1,3,128,128]{3,2,1,0:T(8,128)(2,1)}, u32[]{:S(2)}) %copy-start.9) | copy-done | bytes 98328
  6.4 0.0 copy-start.12
  6.4 0.7 copy-done.12
  7.1 0.0 copy-start.11
  7.1 0.0 copy-start.13
  7.1 2.8 %climb.1 = (f32[5,32,128]{2,1,0:T(8,128)S(1)}, f32[3,32,128]{2,1,0:T(8,128)S(1)}) custom-call(s32[1,4]{1,0:T(1,128)S(1)} %copy-done.12, f32[32,3072]{1,0:T(8,128)S(1)} %copy-done, bf16[128,3072]{1,0:T(8,128)(2,1)S(1)} %copy-done.2, bf16[1,7,128,128]{3,2,1,0:T(8,128)(2,1)S(1)} %copy-done.5, bf16[1,7,128,128]{3,2,1,0:T(8,128)(2,1)S(1)} %copy-done.7, ...), custom_call_target="tpu_custom_call" | custom-call | tf_op jit(solution)/shard_map/climb/pallas_call | solution.py:122
  9.9 0.5 collective-permute-start
  12.4 0.0 copy-done.11
  12.4 0.0 copy-done.13
  12.4 1.3 %features.1 = (bf16[3328,128]{1,0:T(8,128)(2,1)S(1)}, bf16[128,3072]{1,0:T(8,128)(2,1)S(1)}, bf16[3072,128]{1,0:T(8,128)(2,1)S(1)}) custom-call(s32[1,4]{1,0:T(1,128)S(1)} %copy-done.12, f32[1,1]{1,0:T(1,128)} %bitcast.15.length_ref, f32[3,3072]{1,0:T(4,128)S(1)} %copy-done.11, s32[24,128]{1,0:T(8,128)S(1)} %bitcast.19, f32[32,3072]{1,0:T(8,128)S(1)} %copy-done, ...), custom_call_target="tpu_custom_call" | custom-call | tf_op jit(solution)/shard_map/features/pallas_call | solution.py:211
  13.7 6.2 %near_part.3.before_ref = f32[3328,128]{1,0:T(8,128)S(1)} custom-call(s32[1,4]{1,0:T(1,128)S(1)} %copy-done.12, bf16[3328,128]{1,0:T(8,128)(2,1)S(1)} %get-tuple-element.12.left_ref, bf16[128,3072]{1,0:T(8,128)(2,1)S(1)} %get-tuple-element.13.right_ref, bf16[3072,128]{1,0:T(8,128)(2,1)S(1)} %get-tuple-element.14.dd_ref, ...), custom_call_target="tpu_custom_call" | custom-call | tf_op jit(solution)/shard_map/near_part/pallas_call | solution.py:293
  20.0 0.0 collective-permute-done
  20.0 2.4 %collective-permute-start.3 = (f32[3,32,128]{2,1,0:T(8,128)S(1)}, f32[3,32,128]{2,1,0:T(8,128)S(1)}, u32[]{:S(2)}, u32[]{:S(2)}) collective-permute-start(f32[3,32,128]{2,1,0:T(8,128)S(1)} %slice.85), channel_id=1, source_target_pairs={{0,6},{1,7},{2,4},{3,5},{4,2},{5,3},{6,0},{7,1},{8,14},{9,15},{10,... | collective-permute-start | bytes 147464 | tf_op jit(solution)/shard_map/ppermute | solution.py:458
  22.4 0.5 collective-permute-start.2
  22.9 0.6 collective-permute-start.1
  23.6 6.2 %near_part.4.before_ref = f32[3328,128]{1,0:T(8,128)S(1)} custom-call(s32[1,4]{1,0:T(1,128)S(1)} %copy-done.12, bf16[3328,128]{1,0:T(8,128)(2,1)S(1)} %get-tuple-element.12.left_ref, bf16[128,3072]{1,0:T(8,128)(2,1)S(1)} %get-tuple-element.13.right_ref, bf16[3072,128]{1,0:T(8,128)(2,1)S(1)} %get-tuple-element.14.dd_ref, ...), custom_call_target="tpu_custom_call", output_to_operand_aliasing={{}: (4, {})} | custom-call | tf_op jit(solution)/shard_map/near_part/pallas_call | solution.py:293
  29.8 0.0 collective-permute-done.3
  29.8 0.0 collective-permute-done.2
  29.8 0.0 collective-permute-done.1
  29.8 3.7 %collective-permute-start.5 = (f32[1,32,128]{2,1,0:T(8,128)S(1)}, f32[1,32,128]{2,1,0:T(8,128)S(1)}, u32[]{:S(2)}, u32[]{:S(2)}) collective-permute-start(f32[1,32,128]{2,1,0:T(8,128)S(1)} %slice.94), channel_id=1, source_target_pairs={{0,16},{1,17},{2,18},{3,19},{4,20},{5,21},{6,22},{7,23},{8,24},{9,... | collective-permute-start | bytes 49160 | tf_op jit(solution)/shard_map/ppermute | solution.py:458
  33.5 1.1 %collective-permute-start.6 = (f32[1,32,128]{2,1,0:T(8,128)S(1)}, f32[1,32,128]{2,1,0:T(8,128)S(1)}, u32[]{:S(2)}, u32[]{:S(2)}) collective-permute-start(f32[1,32,128]{2,1,0:T(8,128)S(1)} %slice.94), channel_id=1, source_target_pairs={{0,24},{1,25},{2,26},{3,27},{4,28},{5,29},{6,30},{7,31},{8,16},{9,... | collective-permute-start | bytes 49160 | tf_op jit(solution)/shard_map/ppermute | solution.py:458
  34.6 0.5 collective-permute-start.4
  35.1 0.0 copy-start.1
  35.1 0.0 copy-start.3
  35.1 0.0 copy-start.4
  35.1 0.0 copy-start.6
  35.1 6.2 %near_part.5.rest_5_ = f32[3328,128]{1,0:T(8,128)S(1)} custom-call(s32[1,4]{1,0:T(1,128)S(1)} %copy-done.12, bf16[3328,128]{1,0:T(8,128)(2,1)S(1)} %get-tuple-element.12.left_ref, bf16[128,3072]{1,0:T(8,128)(2,1)S(1)} %get-tuple-element.13.right_ref, bf16[3072,128]{1,0:T(8,128)(2,1)S(1)} %get-tuple-element.14.dd_ref, ...), custom_call_target="tpu_custom_call", output_to_operand_aliasing={{}: (4, {})} | custom-call | tf_op jit(solution)/shard_map/near_part/pallas_call | solution.py:293
  41.3 0.0 collective-permute-done.5
  41.3 0.0 collective-permute-done.6
  41.4 0.0 collective-permute-done.4
  41.4 0.0 copy-done.1
  41.4 0.0 copy-done.3
  41.4 0.0 copy-done.4
  41.4 0.0 copy-done.6
  41.4 0.0 copy-start.10
  41.4 2.4 %descend.1 = (f32[32,3072]{1,0:T(8,128)S(1)}, f32[8,32]{1,0:T(8,128)S(1)}) custom-call(s32[1,4]{1,0:T(1,128)S(1)} %copy-done.12, f32[1,1]{1,0:T(1,128)} %bitcast.17.noise_ref, f32[1,1]{1,0:T(1,128)} %bitcast.16.scale_ref, f32[32,3072]{1,0:T(8,128)S(1)} %copy-done.1, f32[32,3072]{1,0:T(8,128)S(1)} %copy-done.4, bf16[128,3072]{1,0:T(8,128)(2,1)S(1)} %copy-done.3, ...), custom_call_target="tpu_custom_call" | custom-call | tf_op jit(solution)/shard_map/descend/pallas_call | solution.py:403
  43.8 40.7 %all-gather = f32[256,32]{1,0:T(8,128)S(1)} all-gather(f32[8,32]{1,0:T(8,128)S(1)} %get-tuple-element.15), channel_id=2, replica_groups=mesh['leaf'=32] {'leaf'}, dimensions={0}, use_global_device_ids=true | all-gather | bytes 33792 | tf_op jit(solution)/shard_map/all_gather | solution.py:526
  84.5 0.0 copy-done.10
  84.5 1.2 %finish.1 = (f32[32,3072]{1,0:T(8,128)}, f32[32,3072]{1,0:T(8,128)}, f32[32,3072]{1,0:T(8,128)}) custom-call(f32[32,8,32]{2,1,0:T(8,128)S(1)} %bitcast.18, f32[32,3072]{1,0:T(8,128)S(1)} %copy-done.10, f32[32,3072]{1,0:T(8,128)S(1)} %copy-done.4, f32[32,3072]{1,0:T(8,128)S(1)} %copy-done.1, f32[32,3072]{1,0:T(8,128)S(1)} %get-tuple-element.16.a_ref), custom_call_target="tpu_custom_call" | custom-call | tf_op jit(solution)/shard_map/finish/pallas_call | solution.py:446
  (7 shorter events, 0.1 us)
Async XLA Ops:
  0.6 1.0 %copy-start = (f32[32,3072]{1,0:T(8,128)S(1)}, f32[32,3072]{1,0:T(8,128)}, u32[]{:S(2)}) copy-start(f32[32,3072]{1,0:T(8,128)} %d_ref.5) | copy-start | bytes 1179652
  1.6 1.1 %copy-start.2 = (bf16[128,3072]{1,0:T(8,128)(2,1)S(1)}, bf16[128,3072]{1,0:T(8,128)(2,1)}, u32[]{:S(2)}) copy-start(bf16[128,3072]{1,0:T(8,128)(2,1)} %basis_ref.1) | copy-start | bytes 2359300
  2.8 0.9 %copy-start.5 = (bf16[1,7,128,128]{3,2,1,0:T(8,128)(2,1)S(1)}, bf16[1,7,128,128]{3,2,1,0:T(8,128)(2,1)}, u32[]{:S(2)}) copy-start(bf16[1,7,128,128]{3,2,1,0:T(8,128)(2,1)} %nt_ref.1) | copy-start | bytes 688132
  3.7 0.9 %copy-start.7 = (bf16[1,7,128,128]{3,2,1,0:T(8,128)(2,1)S(1)}, bf16[1,7,128,128]{3,2,1,0:T(8,128)(2,1)}, u32[]{:S(2)}) copy-start(bf16[1,7,128,128]{3,2,1,0:T(8,128)(2,1)} %nc_ref.1) | copy-start | bytes 688132
  4.6 0.9 %copy-start.8 = (bf16[1,4,128,128]{3,2,1,0:T(8,128)(2,1)S(1)}, bf16[1,4,128,128]{3,2,1,0:T(8,128)(2,1)}, u32[]{:S(2)}) copy-start(bf16[1,4,128,128]{3,2,1,0:T(8,128)(2,1)} %uc_ref.1) | copy-start | bytes 393220
  5.5 0.9 %copy-start.9 = (bf16[1,3,128,128]{3,2,1,0:T(8,128)(2,1)S(1)}, bf16[1,3,128,128]{3,2,1,0:T(8,128)(2,1)}, u32[]{:S(2)}) copy-start(bf16[1,3,128,128]{3,2,1,0:T(8,128)(2,1)} %ut_ref.1) | copy-start | bytes 294916
  6.4 0.7 copy-start.12
  7.1 5.3 %copy-start.11 = (f32[3,3072]{1,0:T(4,128)S(1)}, f32[3,3072]{1,0:T(4,128)}, u32[]{:S(2)}) copy-start(f32[3,3072]{1,0:T(4,128)} %coords_ref.1) | copy-start | bytes 110596
  7.1 5.3 %copy-start.13 = (s32[3072]{0:T(1024)S(1)}, s32[3072]{0:T(1024)}, u32[]{:S(2)}) copy-start(s32[3072]{0:T(1024)} %param.18) | copy-start | bytes 36868
  9.9 10.1 %collective-permute-start = (f32[5,32,128]{2,1,0:T(8,128)S(1)}, f32[5,32,128]{2,1,0:T(8,128)S(1)}, u32[]{:S(2)}, u32[]{:S(2)}) collective-permute-start(f32[5,32,128]{2,1,0:T(8,128)S(1)} %get-tuple-element.11.after_ref.before_ref), channel_id=1, source_target_pairs={{0,1},{1,0},{2,3},{3,2},{4,5},{5,4},{6,7},{7,6},{8,9},{9,8},{10,11... | collective-permute-start | bytes 245768 | tf_op jit(solution)/shard_map/ppermute | solution.py:458
  20.0 9.8 %collective-permute-start.3 = (f32[3,32,128]{2,1,0:T(8,128)S(1)}, f32[3,32,128]{2,1,0:T(8,128)S(1)}, u32[]{:S(2)}, u32[]{:S(2)}) collective-permute-start(f32[3,32,128]{2,1,0:T(8,128)S(1)} %slice.85), channel_id=1, source_target_pairs={{0,6},{1,7},{2,4},{3,5},{4,2},{5,3},{6,0},{7,1},{8,14},{9,15},{10,... | collective-permute-start | bytes 147464 | tf_op jit(solution)/shard_map/ppermute | solution.py:458
  22.4 7.4 %collective-permute-start.2 = (f32[3,32,128]{2,1,0:T(8,128)S(1)}, f32[3,32,128]{2,1,0:T(8,128)S(1)}, u32[]{:S(2)}, u32[]{:S(2)}) collective-permute-start(f32[3,32,128]{2,1,0:T(8,128)S(1)} %slice.85), channel_id=1, source_target_pairs={{0,4},{1,5},{2,6},{3,7},{4,0},{5,1},{6,2},{7,3},{8,12},{9,13},{10,... | collective-permute-start | bytes 147464 | tf_op jit(solution)/shard_map/ppermute | solution.py:458
  22.9 6.9 %collective-permute-start.1 = (f32[4,32,128]{2,1,0:T(8,128)S(1)}, f32[4,32,128]{2,1,0:T(8,128)S(1)}, u32[]{:S(2)}, u32[]{:S(2)}) collective-permute-start(f32[4,32,128]{2,1,0:T(8,128)S(1)} %slice_add_fusion.after_ref), channel_id=1, source_target_pairs={{0,2},{1,3},{2,0},{3,1},{4,6},{5,7},{6,4},{7,5},{8,10},{9,11},{10,... | collective-permute-start | bytes 196616 | tf_op jit(solution)/shard_map/ppermute | solution.py:458
  29.8 11.5 %collective-permute-start.5 = (f32[1,32,128]{2,1,0:T(8,128)S(1)}, f32[1,32,128]{2,1,0:T(8,128)S(1)}, u32[]{:S(2)}, u32[]{:S(2)}) collective-permute-start(f32[1,32,128]{2,1,0:T(8,128)S(1)} %slice.94), channel_id=1, source_target_pairs={{0,16},{1,17},{2,18},{3,19},{4,20},{5,21},{6,22},{7,23},{8,24},{9,... | collective-permute-start | bytes 49160 | tf_op jit(solution)/shard_map/ppermute | solution.py:458
  33.5 7.9 %collective-permute-start.6 = (f32[1,32,128]{2,1,0:T(8,128)S(1)}, f32[1,32,128]{2,1,0:T(8,128)S(1)}, u32[]{:S(2)}, u32[]{:S(2)}) collective-permute-start(f32[1,32,128]{2,1,0:T(8,128)S(1)} %slice.94), channel_id=1, source_target_pairs={{0,24},{1,25},{2,26},{3,27},{4,28},{5,29},{6,30},{7,31},{8,16},{9,... | collective-permute-start | bytes 49160 | tf_op jit(solution)/shard_map/ppermute | solution.py:458
  34.6 6.8 %collective-permute-start.4 = (f32[2,32,128]{2,1,0:T(8,128)S(1)}, f32[2,32,128]{2,1,0:T(8,128)S(1)}, u32[]{:S(2)}, u32[]{:S(2)}) collective-permute-start(f32[2,32,128]{2,1,0:T(8,128)S(1)} %slice_add_fusion.1.after_ref), channel_id=1, source_target_pairs={{0,8},{1,9},{2,10},{3,11},{4,12},{5,13},{6,14},{7,15},{8,0},{9,1},... | collective-permute-start | bytes 98312 | tf_op jit(solution)/shard_map/ppermute | solution.py:458
  35.1 6.3 %copy-start.1 = (f32[32,3072]{1,0:T(8,128)S(1)}, f32[32,3072]{1,0:T(8,128)}, u32[]{:S(2)}) copy-start(f32[32,3072]{1,0:T(8,128)} %d_ref.5) | copy-start | bytes 1179652
  35.1 6.3 %copy-start.3 = (bf16[128,3072]{1,0:T(8,128)(2,1)S(1)}, bf16[128,3072]{1,0:T(8,128)(2,1)}, u32[]{:S(2)}) copy-start(bf16[128,3072]{1,0:T(8,128)(2,1)} %basis_ref.1) | copy-start | bytes 2359300
  35.1 6.3 %copy-start.4 = (f32[32,3072]{1,0:T(8,128)S(1)}, f32[32,3072]{1,0:T(8,128)}, u32[]{:S(2)}) copy-start(f32[32,3072]{1,0:T(8,128)} %r_ref.3) | copy-start | bytes 1179652
  35.1 6.3 %copy-start.6 = (bf16[1,7,128,128]{3,2,1,0:T(8,128)(2,1)S(1)}, bf16[1,7,128,128]{3,2,1,0:T(8,128)(2,1)}, u32[]{:S(2)}) copy-start(bf16[1,7,128,128]{3,2,1,0:T(8,128)(2,1)} %nt_ref.1) | copy-start | bytes 688132
  41.4 43.1 %copy-start.10 = (f32[32,3072]{1,0:T(8,128)S(1)}, f32[32,3072]{1,0:T(8,128)}, u32[]{:S(2)}) copy-start(f32[32,3072]{1,0:T(8,128)} %x_ref.1) | copy-start | bytes 1179652

commit v3 on v2

--- a/solution.py
+++ b/solution.py
@@ -116,28 +116,24 @@
             up_ref[level] = times(coefficient, coupling)
 
 
-def climb(sizes, direction, basis, node_transfer, node_coupling, upper_transfer, upper_coupling, levels):
+def climb(sizes, vectors, levels):
     leaf_count = sizes.shape[1]
-    probes, rank = direction.shape[0], basis.shape[0]
+    probes, rank = vectors[0].shape[0], vectors[1].shape[0]
+    arrays = (sizes, *vectors)
     return pl.pallas_call(
         functools.partial(up_kernel, leaf_count, levels),
         out_shape=(
             jax.ShapeDtypeStruct((levels, probes, rank), F32),
             jax.ShapeDtypeStruct((leaf_count - 1, probes, rank), F32),
         ),
-        in_specs=[HBM] * 7,
+        in_specs=[HBM] * len(arrays),
         out_specs=(VMEM, VMEM),
-        scratch_shapes=[pltpu.SMEM(sizes.shape, jnp.int32)]
-        + [
-            pltpu.VMEM(array.shape, array.dtype)
-            for array in (
-                direction, basis, node_transfer, node_coupling, upper_transfer, upper_coupling
-            )
-        ]
-        + [pltpu.SemaphoreType.DMA((7,))],
+        scratch_shapes=[pltpu.SMEM(sizes.shape, sizes.dtype)]
+        + [pltpu.VMEM(array.shape, array.dtype) for array in vectors]
+        + [pltpu.SemaphoreType.DMA((len(arrays),))],
         compiler_params=PARAMS,
         name="climb",
-    )(sizes, direction, basis, node_transfer, node_coupling, upper_transfer, upper_coupling)
+    )(*(pltpu.with_memory_space_constraint(array, pltpu.HBM) for array in arrays))
 
 
 def features_kernel(
@@ -151,6 +147,7 @@
     left_ref,
     right_ref,
     dd_ref,
+    ds_ref,
     ordered_ref,
 ):
     points = coords_ref.shape[1]
@@ -172,7 +169,7 @@
                 place = 128 * (8 * group + row)
                 ordered_ref[axis : axis + 1, place : place + 128] = found[row : row + 1, :]
     row8 = lax.broadcasted_iota(jnp.int32, (8, points), 0)
-    scale = (math.sqrt(5.0) * LOG2E) / length_ref[...]
+    scale = (math.sqrt(5.0) * LOG2E) / length_ref[...].reshape(1, 1)
     scaled = jnp.where(row8 < 3, (ordered_ref[...] - 0.5) * scale, 0.0)
     z1 = scaled.astype(BF16).astype(F32)
     z2 = (scaled - z1).astype(BF16).astype(F32)
@@ -198,9 +195,10 @@
         [z1, z2, z1, z2, norm_right, leaf_right] + [jnp.zeros((80, points), F32)], axis=0
     )
     right_ref[...] = right.astype(BF16)
-    left_ref[:points, :] = left.T.astype(BF16)
-    left_ref[points:, :] = jnp.zeros((TILE, 128), BF16)
-    split = halves(d_ref[...]).astype(F32)
+    left_ref[...] = left.T.astype(BF16)
+    split = halves(d_ref[...])
+    ds_ref[...] = split
+    split = split.astype(F32)
     split = jnp.concatenate([split, jnp.zeros((128 - split.shape[0], points), F32)], axis=0)
     dd_ref[...] = split.T.astype(BF16)
 
@@ -211,45 +209,44 @@
     return pl.pallas_call(
         functools.partial(features_kernel, leaf_count),
         out_shape=(
-            jax.ShapeDtypeStruct((points + TILE, 128), BF16),
+            jax.ShapeDtypeStruct((points, 128), BF16),
             jax.ShapeDtypeStruct((128, points), BF16),
             jax.ShapeDtypeStruct((points, 128), BF16),
+            jax.ShapeDtypeStruct((2 * direction.shape[0], points), BF16),
         ),
         in_specs=[SMEM, VMEM, VMEM, VMEM, VMEM, ANY],
-        out_specs=(VMEM, VMEM, VMEM),
+        out_specs=(VMEM,) * 4,
         scratch_shapes=[pltpu.VMEM((8, points), F32)],
         compiler_params=PARAMS,
         name="features",
-    )(sizes, lengthscale.reshape(1, 1), coordinates, order.reshape(-1, 128), direction, after)
-
-
-def tile_spans(ends, tiles):
-    lows, counts = [], []
+    )(sizes, lengthscale, coordinates, order.reshape(-1, 128), direction, after)
+
+
+def tile_counts(ends, tiles):
+    counts = []
     for tile in range(tiles):
-        begin, last = tile * TILE, tile * TILE + TILE - 1
-        low = 0
+        last = tile * TILE + TILE - 1
         high = ends[-1]
-        for end in ends:
-            low = jnp.where(end <= begin, end, low)
         for end in ends[::-1]:
             high = jnp.where(end > last, end, high)
-        low = lax.div(low, TILE)
-        lows.append(low)
-        counts.append(lax.div(high - 1, TILE) + 1 - low)
-    return lows, counts
-
-
-def near_kernel(leaf_count, part, parts, sizes_ref, left_ref, right_ref, dd_ref, before_ref, after_ref, out_ref):
+        counts.append(lax.div(high - 1, TILE) + 1 - tile)
+    return counts
+
+
+def near_kernel(
+    leaf_count, part, parts, sizes_ref, left_ref, right_ref, dd_ref, ds_ref, *refs
+):
+    tall_ref, wide_ref = refs[-2:]
     ends = leaf_ends(sizes_ref, leaf_count)
     tiles = right_ref.shape[1] // TILE
-    lows, counts = tile_spans(ends, tiles)
     firsts = [0]
-    for count in counts:
+    for count in tile_counts(ends, tiles):
         firsts.append(firsts[-1] + count)
     groups = lax.div(firsts[-1] + (GROUP - 1), GROUP)
-    offsets = [low - first for low, first in zip(lows, firsts)]
+    offsets = [tile - first for tile, first in zip(range(tiles), firsts)]
     if part == 0:
-        out_ref[...] = jnp.zeros_like(out_ref)
+        tall_ref[...] = jnp.zeros_like(tall_ref)
+        wide_ref[...] = jnp.zeros_like(wide_ref)
 
     def one_group(group, carry):
         for unit in range(GROUP):
@@ -261,26 +258,31 @@
                 row = jnp.where(inside, tile, row)
                 offset = jnp.where(inside, offsets[tile], offset)
             spare = item >= firsts[-1]
-            row = jnp.where(spare, tiles, row)
-            column = jnp.where(spare, 0, item + offset)
-            begin = pl.multiple_of(row * TILE, TILE)
-            place = pl.multiple_of(column * TILE, TILE)
+            column = item + offset
+            tall = pl.multiple_of(jnp.where(spare, tiles, row) * TILE, TILE)
+            wide = pl.multiple_of(jnp.where(spare | (row == column), tiles, column) * TILE, TILE)
+            rows = pl.ds(pl.multiple_of(jnp.where(spare, 0, row) * TILE, TILE), TILE)
+            columns = pl.ds(pl.multiple_of(jnp.where(spare, 0, column) * TILE, TILE), TILE)
             squared = jnp.dot(
-                left_ref[pl.ds(begin, TILE), :],
-                right_ref[:, pl.ds(place, TILE)],
-                preferred_element_type=F32,
+                left_ref[rows, :], right_ref[:, columns], preferred_element_type=F32
             )
             squared = jnp.maximum(squared, 1e-12)
             root = squared * lax.rsqrt(squared)
             kernel = (squared + LINEAR * root + CONSTANT) * jnp.exp2(-root)
             high_part = kernel.astype(BF16)
             low_part = (kernel - high_part.astype(F32)).astype(BF16)
-            weights = dd_ref[pl.ds(place, TILE), :]
-            out_ref[pl.ds(begin, TILE), :] += jnp.dot(
+            weights = dd_ref[columns, :]
+            tall_ref[pl.ds(tall, TILE), :] += jnp.dot(
                 jnp.concatenate([high_part, low_part], axis=1),
                 jnp.concatenate([weights, weights], axis=0),
                 preferred_element_type=F32,
             )
+            vectors = ds_ref[:, rows]
+            wide_ref[:, pl.ds(wide, TILE)] += jnp.dot(
+                jnp.concatenate([vectors, vectors], axis=1),
+                jnp.concatenate([high_part, low_part], axis=0),
+                preferred_element_type=F32,
+            )
         return carry
 
     lax.fori_loop(
@@ -288,17 +290,22 @@
     )
 
 
-def near_part(sizes, left, right, dd, before, after, part, parts):
+def near_part(sizes, prepared, before, after, part, parts):
     leaf_count = sizes.shape[1]
+    left, right, dd, ds = prepared
+    points = right.shape[1]
     return pl.pallas_call(
         functools.partial(near_kernel, leaf_count, part, parts),
-        out_shape=jax.ShapeDtypeStruct(left.shape, F32),
-        in_specs=[SMEM, VMEM, VMEM, VMEM, ANY if part == 0 else VMEM, ANY],
-        out_specs=VMEM,
-        input_output_aliases={} if part == 0 else {4: 0},
+        out_shape=(
+            jax.ShapeDtypeStruct((points + TILE, 128), F32),
+            jax.ShapeDtypeStruct((ds.shape[0], points + TILE), F32),
+        ),
+        in_specs=[SMEM] + [VMEM] * (4 + len(before)) + [ANY],
+        out_specs=(VMEM, VMEM),
+        input_output_aliases={5 + index: index for index in range(len(before))},
         compiler_params=PARAMS,
         name="near_part",
-    )(sizes, left, right, dd, before, after)
+    )(sizes, left, right, dd, ds, *before, after)
 
 
 def down_kernel(
@@ -318,7 +325,7 @@
     *rest,
 ):
     side_refs = rest[:levels]
-    near_ref, a_ref, sums_ref = rest[levels:]
+    tall_ref, wide_ref, a_ref, sums_ref = rest[levels:]
     probes, points = d_ref.shape
     down = None
     for level in range(levels - 1, -1, -1):
@@ -348,8 +355,8 @@
         current = following
     stacked = jnp.concatenate([halves(term) for term in current], axis=0)
     ends = leaf_ends(sizes_ref, leaf_count)
-    noise = noise_ref[...]
-    near_scale = scale_ref[...] * POLY
+    noise = noise_ref[...].reshape(1, 1)
+    near_scale = scale_ref[...].reshape(1, 1) * POLY
     width = 512
     peak = jnp.zeros((probes, 128), F32)
     old = jnp.zeros((probes, 128), F32)
@@ -369,8 +376,8 @@
             far = jnp.where(leaf == index, term, far)
         d = d_ref[:, first : first + width]
         r = r_ref[:, first : first + width]
-        near = near_ref[first : first + width, :].T
-        near = near[:probes] + near[probes : 2 * probes]
+        near = tall_ref[first : first + width, :].T[: 2 * probes]
+        near = folded(near + wide_ref[:, first : first + width])
         applied = noise * d + near_scale * near + far
         a_ref[:, first : first + width] = applied
         size = jnp.abs(applied)
@@ -391,7 +398,8 @@
     sums = jnp.where(lane == 1, jnp.sum(curve, axis=1, keepdims=True), sums)
     sums = jnp.where(lane == 2, jnp.sum(cross, axis=1, keepdims=True), sums)
     sums = jnp.where(lane == 3, jnp.sum(square, axis=1, keepdims=True), sums)
-    sums_ref[...] = jnp.where(lane == 4, top, sums).T[:8]
+    sums = jnp.where(lane == 4, top, sums).T[:8]
+    sums_ref[...] = jnp.broadcast_to(sums[None], sums_ref.shape)
 
 
 def descend(
@@ -404,15 +412,15 @@
         functools.partial(down_kernel, leaf_count, len(sides)),
         out_shape=(
             jax.ShapeDtypeStruct((probes, points), F32),
-            jax.ShapeDtypeStruct((8, probes), F32),
+            jax.ShapeDtypeStruct((2 ** len(sides), 8, probes), F32),
         ),
-        in_specs=[SMEM] + [VMEM] * (11 + len(sides)),
+        in_specs=[SMEM] + [VMEM] * (12 + len(sides)),
         out_specs=(VMEM, VMEM),
         compiler_params=PARAMS,
         name="descend",
     )(
-        sizes, noise.reshape(1, 1), scale.reshape(1, 1), direction, residual, basis,
-        node_transfer, node_coupling, upper_transfer, upper_coupling, local, *sides, near,
+        sizes, noise, scale, direction, residual, basis,
+        node_transfer, node_coupling, upper_transfer, upper_coupling, local, *sides, *near,
     )
 
 
@@ -486,14 +494,15 @@
     levels = lax.axis_size("leaf").bit_length() - 1
     probes, points = direction.shape
     up, local = climb(
-        leaf_sizes, direction, leaf_basis, node_transfer, node_coupling,
-        upper_transfer, upper_coupling, levels,
-    )
-    left, right, dd = features(leaf_sizes, lengthscale, coordinates, cluster_order, direction, up)
+        leaf_sizes,
+        (direction, leaf_basis, node_transfer, node_coupling, upper_transfer, upper_coupling),
+        levels,
+    )
+    prepared = features(leaf_sizes, lengthscale, coordinates, cluster_order, direction, up)
     groups = level_groups(levels)
     parts = 3
     sides = [None] * levels
-    near = up
+    near = ()
     current = up
     for number, group in enumerate(groups):
         base = group[0]
@@ -504,7 +513,7 @@
             top = pick.bit_length() - 1
             incoming[pick] = from_partner(current[top:], stride)
         if number < parts:
-            near = near_part(leaf_sizes, left, right, dd, near, current, number, parts)
+            near = near_part(leaf_sizes, prepared, near, current, number, parts)
         for position in range(len(group)):
             total = current[position]
             for pick in range(1, 2 ** (position + 1)):
@@ -518,12 +527,12 @@
                 following = following + incoming[pick][len(group) - top :]
         current = following
     for number in range(len(groups), parts):
-        near = near_part(leaf_sizes, left, right, dd, near, up, number, parts)
+        near = near_part(leaf_sizes, prepared, near, up, number, parts)
     applied, sums = descend(
         leaf_sizes, noise_variance, outputscale, direction, residual, leaf_basis,
         node_transfer, node_coupling, upper_transfer, upper_coupling, local, sides, near,
     )
-    gathered = lax.all_gather(sums, "leaf")
+    gathered = lax.all_to_all(sums, "leaf", 0, 0)
     return finish(gathered, solution, residual, direction, applied)
 
 

time: 86.4 us -> 48.6 us (0.56); the launches traced: 85.7 us -> 48.9 us
  blocking collectives: 40.7 us -> 13.3 us
  local copies, waits for them, and re-layouts: 6.5 us -> 0.78 us
  Pallas kernels: 26.3 us -> 20.6 us
  starting transfers between devices: 9.31 us -> 10.5 us
    all_gather x1 -> x0, blocking collectives: 40.7 us -> none  [shards(): gathered = lax.all_gather(sums, 'leaf')]
    all_to_all x0 -> x1, blocking collectives: none -> 13.3 us  [shards(): gathered = lax.all_to_all(sums, 'leaf', 0, 0)]
    unnamed x28 -> x24, local copies, waits for them, and re-layouts: 6.49 us -> 0.26 us
    pallas_call x3, Pallas kernels: 18.6 us -> 12.6 us  [near_part(): pl.pallas_call(functools.partial(near_kernel, leaf_count, part, parts), o...]
    ppermute x7, starting transfers between devices: 9.31 us -> 10.5 us  [from_partner(): return lax.ppermute(array, 'leaf', [(i, i ^ stride) for i in range(count)])]
  transfers between devices with their start and end apart: 7 -> 7, of which waited for: 0 -> 0; matrix products, arithmetic and copies ran while one was open for 0% -> 0% of each run, Pallas kernels for 23% -> 29%
where the time goes in v3:
time: 48.6 us; the launch traced here: 48.9 us
  Pallas kernels  20.6 us (42%)
  blocking collectives  13.3 us (27%)
  starting transfers between devices  10.5 us (22%)
  between operations  2.91 us (6%)
  local copies, waits for them, and re-layouts  0.78 us (2%)
  other arithmetic  0.77 us (2%)
    all_to_all x1, blocking collectives, shards(): gathered = lax.all_to_all(sums, 'leaf', 0, 0)  13.3 us
    pallas_call x3, Pallas kernels, near_part(): pl.pallas_call(functools.partial(near_kernel, leaf_count, part, parts), o...  12.6 us
    ppermute x7, starting transfers between devices, from_partner(): return lax.ppermute(array, 'leaf', [(i, i ^ stride) for i in range(count)])  10.5 us
    pallas_call x1, Pallas kernels, climb(): pl.pallas_call(functools.partial(up_kernel, leaf_count, levels), out_shap...  3.13 us
    pallas_call x1, Pallas kernels, descend(): pl.pallas_call(functools.partial(down_kernel, leaf_count, len(sides)), ou...  2.36 us
    pallas_call x1, Pallas kernels, features(): pl.pallas_call(functools.partial(features_kernel, leaf_count), out_shape=...  1.35 us
    pallas_call x1, Pallas kernels, finish(): pl.pallas_call(step_kernel, out_shape=(shape, shape, shape), in_specs=[VM...  1.2 us
  transfers between devices with their start and end apart: 7, of which 0 were waited for; matrix products, arithmetic and copies ran while one was open for 0% of the time, Pallas kernels for 29%

profile of v3, /device:TPU:0, one launch (start us, length us, event | category | flops | bytes accessed | tf_op | source)
XLA Modules:
  0.0 48.9 jit_solution(17640952608721486718)
XLA Ops:
  0.6 0.0 copy-start.9
  0.6 0.0 copy-start
  0.7 0.0 copy-start.8
  0.7 0.0 copy-start.10
  0.7 3.1 %climb.1 = (f32[5,32,128]{2,1,0:T(8,128)S(1)}, f32[3,32,128]{2,1,0:T(8,128)S(1)}) custom-call(s32[1,4]{1,0:T(1,128)} %sizes_ref.9, f32[32,3072]{1,0:T(8,128)} %d_ref.5, bf16[128,3072]{1,0:T(8,128)(2,1)} %basis_ref.1, bf16[1,7,128,128]{3,2,1,0:T(8,128)(2,1)} %nt_ref.1, bf16[1,7,128,128]{3,2,1,0:T(8,128)(2,1)} %nc_ref.1, bf16[1,3,128,128]{3,2,1,0:T(8,128)(2,1)} %ut_ref.1, ...), custom_call_target="tpu_custom_call" | custom-call | tf_op jit(solution)/shard_map/climb/pallas_call | solution.py:123
  3.8 0.5 %collective-permute-start = (f32[5,32,128]{2,1,0:T(8,128)S(1)}, f32[5,32,128]{2,1,0:T(8,128)S(1)}, u32[]{:S(2)}, u32[]{:S(2)}) collective-permute-start(f32[5,32,128]{2,1,0:T(8,128)S(1)} %get-tuple-element.18.after_ref.refs_0_), channel_id=1, source_target_pairs={{0,1},{1,0},{2,3},{3,2},{4,5},{5,4},{6,7},{7,6},{8,9},{9,8},{10,11... | collective-permute-start | bytes 245768 | tf_op jit(solution)/shard_map/ppermute | solution.py:466
  6.3 0.0 copy-done.9
  6.3 0.0 copy-done
  6.3 0.0 copy-done.8
  6.3 0.0 copy-done.10
  6.3 1.4 %features.1 = (bf16[3072,128]{1,0:T(8,128)(2,1)S(1)}, bf16[128,3072]{1,0:T(8,128)(2,1)S(1)}, bf16[3072,128]{1,0:T(8,128)(2,1)S(1)}, bf16[64,3072]{1,0:T(8,128)(2,1)S(1)}) custom-call(s32[1,4]{1,0:T(1,128)S(1)} %copy-done.9, f32[1]{0:T(128)S(6)} %copy.25.length_ref, f32[3,3072]{1,0:T(4,128)S(1)} %copy-done.8, s32[24,128]{1,0:T(8,128)S(1)} %bitcast.11, ...), custom_call_target="tpu_custom_call" | custom-call | tf_op jit(solution)/shard_map/features/pallas_call | solution.py:209
  7.7 3.4 %near_part.3 = (f32[3328,128]{1,0:T(8,128)S(1)}, f32[64,3328]{1,0:T(8,128)S(1)}) custom-call(s32[1,4]{1,0:T(1,128)S(1)} %copy-done.9, bf16[3072,128]{1,0:T(8,128)(2,1)S(1)} %get-tuple-element.19.left_ref, bf16[128,3072]{1,0:T(8,128)(2,1)S(1)} %get-tuple-element.20.right_ref, bf16[3072,128]{1,0:T(8,128)(2,1)S(1)} %get-tuple-element.21.dd_ref, ...), custom_call_target="tpu_custom_call" | custom-call | tf_op jit(solution)/shard_map/near_part/pallas_call | solution.py:297
  11.0 0.0 collective-permute-done
  11.1 4.8 %collective-permute-start.3 = (f32[3,32,128]{2,1,0:T(8,128)S(1)}, f32[3,32,128]{2,1,0:T(8,128)S(1)}, u32[]{:S(2)}, u32[]{:S(2)}) collective-permute-start(f32[3,32,128]{2,1,0:T(8,128)S(1)} %slice.85), channel_id=1, source_target_pairs={{0,6},{1,7},{2,4},{3,5},{4,2},{5,3},{6,0},{7,1},{8,14},{9,15},{10,... | collective-permute-start | bytes 147464 | tf_op jit(solution)/shard_map/ppermute | solution.py:466
  15.9 0.0 collective-permute-start.2
  15.9 0.6 %collective-permute-start.1 = (f32[4,32,128]{2,1,0:T(8,128)S(1)}, f32[4,32,128]{2,1,0:T(8,128)S(1)}, u32[]{:S(2)}, u32[]{:S(2)}) collective-permute-start(f32[4,32,128]{2,1,0:T(8,128)S(1)} %slice_add_fusion.refs_2_), channel_id=1, source_target_pairs={{0,2},{1,3},{2,0},{3,1},{4,6},{5,7},{6,4},{7,5},{8,10},{9,11},{10,... | collective-permute-start | bytes 196616 | tf_op jit(solution)/shard_map/ppermute | solution.py:466
  16.6 4.6 %near_part.4 = (f32[3328,128]{1,0:T(8,128)S(1)}, f32[64,3328]{1,0:T(8,128)S(1)}) custom-call(s32[1,4]{1,0:T(1,128)S(1)} %copy-done.9, bf16[3072,128]{1,0:T(8,128)(2,1)S(1)} %get-tuple-element.19.left_ref, bf16[128,3072]{1,0:T(8,128)(2,1)S(1)} %get-tuple-element.20.right_ref, ...), custom_call_target="tpu_custom_call", output_to_operand_aliasing={{0}: (5, {}), {1}: (6, {})} | custom-call | tf_op jit(solution)/shard_map/near_part/pallas_call | solution.py:297
  21.2 0.0 collective-permute-done.3
  21.2 0.0 collective-permute-done.2
  21.2 0.0 collective-permute-done.1
  21.3 3.7 %collective-permute-start.6 = (f32[1,32,128]{2,1,0:T(8,128)S(1)}, f32[1,32,128]{2,1,0:T(8,128)S(1)}, u32[]{:S(2)}, u32[]{:S(2)}) collective-permute-start(f32[1,32,128]{2,1,0:T(8,128)S(1)} %slice.94), channel_id=1, source_target_pairs={{0,24},{1,25},{2,26},{3,27},{4,28},{5,29},{6,30},{7,31},{8,16},{9,... | collective-permute-start | bytes 49160 | tf_op jit(solution)/shard_map/ppermute | solution.py:466
  24.9 0.0 collective-permute-start.5
  24.9 0.8 %collective-permute-start.4 = (f32[2,32,128]{2,1,0:T(8,128)S(1)}, f32[2,32,128]{2,1,0:T(8,128)S(1)}, u32[]{:S(2)}, u32[]{:S(2)}) collective-permute-start(f32[2,32,128]{2,1,0:T(8,128)S(1)} %slice_add_fusion.1.refs_2_), channel_id=1, source_target_pairs={{0,8},{1,9},{2,10},{3,11},{4,12},{5,13},{6,14},{7,15},{8,0},{9,1},... | collective-permute-start | bytes 98312 | tf_op jit(solution)/shard_map/ppermute | solution.py:466
  25.7 0.0 copy-start.1
  25.7 0.0 copy-start.2
  25.8 0.0 copy-start.3
  25.8 0.0 copy-start.4
  25.8 0.0 copy-start.5
  25.8 0.0 copy-start.6
  25.8 4.6 %near_part.5 = (f32[3328,128]{1,0:T(8,128)S(1)}, f32[64,3328]{1,0:T(8,128)S(1)}) custom-call(s32[1,4]{1,0:T(1,128)S(1)} %copy-done.9, bf16[3072,128]{1,0:T(8,128)(2,1)S(1)} %get-tuple-element.19.left_ref, bf16[128,3072]{1,0:T(8,128)(2,1)S(1)} %get-tuple-element.20.right_ref, ...), custom_call_target="tpu_custom_call", output_to_operand_aliasing={{0}: (5, {}), {1}: (6, {})} | custom-call | tf_op jit(solution)/shard_map/near_part/pallas_call | solution.py:297
  30.4 0.0 collective-permute-done.6
  30.4 0.0 collective-permute-done.5
  30.4 0.0 collective-permute-done.4
  30.5 0.0 copy-done.1
  30.5 0.0 copy-done.2
  30.5 0.0 copy-done.3
  30.5 0.0 copy-done.4
  30.5 0.0 copy-done.5
  30.5 0.0 copy-done.6
  30.5 0.0 copy-start.7
  30.5 2.4 %descend.1 = (f32[32,3072]{1,0:T(8,128)S(1)}, f32[32,8,32]{2,1,0:T(8,128)S(1)}) custom-call(s32[1,4]{1,0:T(1,128)S(1)} %copy-done.9, f32[1]{0:T(128)S(6)} %copy.27.noise_ref, f32[1]{0:T(128)S(6)} %copy.26.scale_ref, f32[32,3072]{1,0:T(8,128)S(1)} %copy-done, f32[32,3072]{1,0:T(8,128)S(1)} %copy-done.2, bf16[128,3072]{1,0:T(8,128)(2,1)S(1)} %copy-done.1, ...), custom_call_target="tpu_custom_call" | custom-call | tf_op jit(solution)/shard_map/descend/pallas_call | solution.py:411
  32.9 0.1 reshape.19
  33.0 13.3 %all_to_all.5 = f32[32,1,256]{2,1,0:T(1,128)S(1)} all-to-all(f32[32,1,256]{2,1,0:T(1,128)S(1)} %reshape.19), channel_id=1, replica_groups=mesh['leaf'=32] {'leaf'}, dimensions={0} | all-to-all | bytes 65536 | tf_op jit(solution)/shard_map/all_to_all | solution.py:535
  46.3 0.5 %broadcast = f32[]{:T(128)} broadcast(f32[]{:T(128)} %constant.16), dimensions={} | broadcast | bytes 8 | tf_op jit(solution)/shard_map/all_to_all | solution.py:535
  46.8 0.7 %reduce = f32[32,256]{1,0:T(8,128)S(1)} reduce(f32[32,1,256]{2,1,0:T(1,128)S(1)} %all_to_all.5, f32[]{:T(128)} %broadcast), dimensions={1}, to_apply=%all_to_all.3.reduce_sub_computation | reduce | bytes 65540 | tf_op jit(solution)/shard_map/all_to_all | solution.py:535
  47.6 0.1 reshape.20.sums_ref
  47.7 0.0 copy-done.7
  47.7 1.2 %finish.1 = (f32[32,3072]{1,0:T(8,128)}, f32[32,3072]{1,0:T(8,128)}, f32[32,3072]{1,0:T(8,128)}) custom-call(f32[32,8,32]{2,1,0:T(8,128)S(1)} %reshape.20.sums_ref, f32[32,3072]{1,0:T(8,128)S(1)} %copy-done.7, f32[32,3072]{1,0:T(8,128)S(1)} %copy-done.2, f32[32,3072]{1,0:T(8,128)S(1)} %copy-done, f32[32,3072]{1,0:T(8,128)S(1)} %get-tuple-element.30.a_ref), custom_call_target="tpu_custom_call" | custom-call | tf_op jit(solution)/shard_map/finish/pallas_call | solution.py:454
  (7 shorter events, 0.1 us)
Async XLA Ops:
  0.6 5.6 %copy-start.9 = (s32[1,4]{1,0:T(1,128)S(1)}, s32[1,4]{1,0:T(1,128)}, u32[]{:S(2)}) copy-start(s32[1,4]{1,0:T(1,128)} %sizes_ref.9) | copy-start | bytes 52
  0.6 5.6 %copy-start = (f32[32,3072]{1,0:T(8,128)S(1)}, f32[32,3072]{1,0:T(8,128)}, u32[]{:S(2)}) copy-start(f32[32,3072]{1,0:T(8,128)} %d_ref.5) | copy-start | bytes 1179652
  0.7 5.6 %copy-start.8 = (f32[3,3072]{1,0:T(4,128)S(1)}, f32[3,3072]{1,0:T(4,128)}, u32[]{:S(2)}) copy-start(f32[3,3072]{1,0:T(4,128)} %coords_ref.1) | copy-start | bytes 110596
  0.7 5.6 %copy-start.10 = (s32[3072]{0:T(1024)S(1)}, s32[3072]{0:T(1024)}, u32[]{:S(2)}) copy-start(s32[3072]{0:T(1024)} %param.18) | copy-start | bytes 36868
  3.8 7.2 %collective-permute-start = (f32[5,32,128]{2,1,0:T(8,128)S(1)}, f32[5,32,128]{2,1,0:T(8,128)S(1)}, u32[]{:S(2)}, u32[]{:S(2)}) collective-permute-start(f32[5,32,128]{2,1,0:T(8,128)S(1)} %get-tuple-element.18.after_ref.refs_0_), channel_id=1, source_target_pairs={{0,1},{1,0},{2,3},{3,2},{4,5},{5,4},{6,7},{7,6},{8,9},{9,8},{10,11... | collective-permute-start | bytes 245768 | tf_op jit(solution)/shard_map/ppermute | solution.py:466
  11.1 10.1 %collective-permute-start.3 = (f32[3,32,128]{2,1,0:T(8,128)S(1)}, f32[3,32,128]{2,1,0:T(8,128)S(1)}, u32[]{:S(2)}, u32[]{:S(2)}) collective-permute-start(f32[3,32,128]{2,1,0:T(8,128)S(1)} %slice.85), channel_id=1, source_target_pairs={{0,6},{1,7},{2,4},{3,5},{4,2},{5,3},{6,0},{7,1},{8,14},{9,15},{10,... | collective-permute-start | bytes 147464 | tf_op jit(solution)/shard_map/ppermute | solution.py:466
  15.9 5.3 %collective-permute-start.2 = (f32[3,32,128]{2,1,0:T(8,128)S(1)}, f32[3,32,128]{2,1,0:T(8,128)S(1)}, u32[]{:S(2)}, u32[]{:S(2)}) collective-permute-start(f32[3,32,128]{2,1,0:T(8,128)S(1)} %slice.85), channel_id=1, source_target_pairs={{0,4},{1,5},{2,6},{3,7},{4,0},{5,1},{6,2},{7,3},{8,12},{9,13},{10,... | collective-permute-start | bytes 147464 | tf_op jit(solution)/shard_map/ppermute | solution.py:466
  15.9 5.3 %collective-permute-start.1 = (f32[4,32,128]{2,1,0:T(8,128)S(1)}, f32[4,32,128]{2,1,0:T(8,128)S(1)}, u32[]{:S(2)}, u32[]{:S(2)}) collective-permute-start(f32[4,32,128]{2,1,0:T(8,128)S(1)} %slice_add_fusion.refs_2_), channel_id=1, source_target_pairs={{0,2},{1,3},{2,0},{3,1},{4,6},{5,7},{6,4},{7,5},{8,10},{9,11},{10,... | collective-permute-start | bytes 196616 | tf_op jit(solution)/shard_map/ppermute | solution.py:466
  21.3 9.2 %collective-permute-start.6 = (f32[1,32,128]{2,1,0:T(8,128)S(1)}, f32[1,32,128]{2,1,0:T(8,128)S(1)}, u32[]{:S(2)}, u32[]{:S(2)}) collective-permute-start(f32[1,32,128]{2,1,0:T(8,128)S(1)} %slice.94), channel_id=1, source_target_pairs={{0,24},{1,25},{2,26},{3,27},{4,28},{5,29},{6,30},{7,31},{8,16},{9,... | collective-permute-start | bytes 49160 | tf_op jit(solution)/shard_map/ppermute | solution.py:466
  24.9 5.5 %collective-permute-start.5 = (f32[1,32,128]{2,1,0:T(8,128)S(1)}, f32[1,32,128]{2,1,0:T(8,128)S(1)}, u32[]{:S(2)}, u32[]{:S(2)}) collective-permute-start(f32[1,32,128]{2,1,0:T(8,128)S(1)} %slice.94), channel_id=1, source_target_pairs={{0,16},{1,17},{2,18},{3,19},{4,20},{5,21},{6,22},{7,23},{8,24},{9,... | collective-permute-start | bytes 49160 | tf_op jit(solution)/shard_map/ppermute | solution.py:466
  24.9 5.5 %collective-permute-start.4 = (f32[2,32,128]{2,1,0:T(8,128)S(1)}, f32[2,32,128]{2,1,0:T(8,128)S(1)}, u32[]{:S(2)}, u32[]{:S(2)}) collective-permute-start(f32[2,32,128]{2,1,0:T(8,128)S(1)} %slice_add_fusion.1.refs_2_), channel_id=1, source_target_pairs={{0,8},{1,9},{2,10},{3,11},{4,12},{5,13},{6,14},{7,15},{8,0},{9,1},... | collective-permute-start | bytes 98312 | tf_op jit(solution)/shard_map/ppermute | solution.py:466
  25.7 4.8 %copy-start.1 = (bf16[128,3072]{1,0:T(8,128)(2,1)S(1)}, bf16[128,3072]{1,0:T(8,128)(2,1)}, u32[]{:S(2)}) copy-start(bf16[128,3072]{1,0:T(8,128)(2,1)} %basis_ref.1) | copy-start | bytes 2359300
  25.7 4.7 %copy-start.2 = (f32[32,3072]{1,0:T(8,128)S(1)}, f32[32,3072]{1,0:T(8,128)}, u32[]{:S(2)}) copy-start(f32[32,3072]{1,0:T(8,128)} %r_ref.3) | copy-start | bytes 1179652
  25.8 4.7 %copy-start.3 = (bf16[1,7,128,128]{3,2,1,0:T(8,128)(2,1)S(1)}, bf16[1,7,128,128]{3,2,1,0:T(8,128)(2,1)}, u32[]{:S(2)}) copy-start(bf16[1,7,128,128]{3,2,1,0:T(8,128)(2,1)} %nt_ref.1) | copy-start | bytes 688132
  25.8 4.7 %copy-start.4 = (bf16[1,7,128,128]{3,2,1,0:T(8,128)(2,1)S(1)}, bf16[1,7,128,128]{3,2,1,0:T(8,128)(2,1)}, u32[]{:S(2)}) copy-start(bf16[1,7,128,128]{3,2,1,0:T(8,128)(2,1)} %nc_ref.1) | copy-start | bytes 688132
  25.8 4.7 %copy-start.5 = (bf16[1,4,128,128]{3,2,1,0:T(8,128)(2,1)S(1)}, bf16[1,4,128,128]{3,2,1,0:T(8,128)(2,1)}, u32[]{:S(2)}) copy-start(bf16[1,4,128,128]{3,2,1,0:T(8,128)(2,1)} %uc_ref.1) | copy-start | bytes 393220
  25.8 4.7 %copy-start.6 = (bf16[1,3,128,128]{3,2,1,0:T(8,128)(2,1)S(1)}, bf16[1,3,128,128]{3,2,1,0:T(8,128)(2,1)}, u32[]{:S(2)}) copy-start(bf16[1,3,128,128]{3,2,1,0:T(8,128)(2,1)} %ut_ref.1) | copy-start | bytes 294916
  30.5 17.1 %copy-start.7 = (f32[32,3072]{1,0:T(8,128)S(1)}, f32[32,3072]{1,0:T(8,128)}, u32[]{:S(2)}) copy-start(f32[32,3072]{1,0:T(8,128)} %x_ref.1) | copy-start | bytes 1179652

commit v4 on v3

--- a/solution.py
+++ b/solution.py
@@ -21,7 +21,9 @@
 SMEM = pl.BlockSpec(memory_space=pltpu.SMEM)
 ANY = pl.BlockSpec(memory_space=pl.ANY)
 HBM = pl.BlockSpec(memory_space=pltpu.HBM)
-GROUP = 4
+STRIP = 512
+GROUP = 2
+PARTS = 5
 PARAMS = pltpu.CompilerParams(vmem_limit_bytes=48 * 1024 * 1024)
 
 
@@ -147,7 +149,6 @@
     left_ref,
     right_ref,
     dd_ref,
-    ds_ref,
     ordered_ref,
 ):
     points = coords_ref.shape[1]
@@ -192,15 +193,15 @@
         axis=0,
     )
     right = jnp.concatenate(
-        [z1, z2, z1, z2, norm_right, leaf_right] + [jnp.zeros((80, points), F32)], axis=0
+        [z1, z2, z1, z2, norm_right, leaf_right], axis=0
     )
     right_ref[...] = right.astype(BF16)
-    left_ref[...] = left.T.astype(BF16)
-    split = halves(d_ref[...])
-    ds_ref[...] = split
-    split = split.astype(F32)
+    left_ref[:points, :] = left.T.astype(BF16)
+    left_ref[points:, :] = jnp.zeros((STRIP, 128), BF16)
+    split = halves(d_ref[...]).astype(F32)
     split = jnp.concatenate([split, jnp.zeros((128 - split.shape[0], points), F32)], axis=0)
-    dd_ref[...] = split.T.astype(BF16)
+    dd_ref[:points, :] = split.T.astype(BF16)
+    dd_ref[points:, :] = jnp.zeros((TILE, 128), BF16)
 
 
 def features(sizes, lengthscale, coordinates, order, direction, after):
@@ -209,103 +210,96 @@
     return pl.pallas_call(
         functools.partial(features_kernel, leaf_count),
         out_shape=(
-            jax.ShapeDtypeStruct((points, 128), BF16),
-            jax.ShapeDtypeStruct((128, points), BF16),
-            jax.ShapeDtypeStruct((points, 128), BF16),
-            jax.ShapeDtypeStruct((2 * direction.shape[0], points), BF16),
+            jax.ShapeDtypeStruct((points + STRIP, 128), BF16),
+            jax.ShapeDtypeStruct((48, points), BF16),
+            jax.ShapeDtypeStruct((points + TILE, 128), BF16),
         ),
         in_specs=[SMEM, VMEM, VMEM, VMEM, VMEM, ANY],
-        out_specs=(VMEM,) * 4,
+        out_specs=(VMEM,) * 3,
         scratch_shapes=[pltpu.VMEM((8, points), F32)],
         compiler_params=PARAMS,
         name="features",
     )(sizes, lengthscale, coordinates, order.reshape(-1, 128), direction, after)
 
 
-def tile_counts(ends, tiles):
-    counts = []
+def strip_spans(ends, tiles):
+    begins, counts = [], []
     for tile in range(tiles):
-        last = tile * TILE + TILE - 1
+        first = tile * TILE
+        last = first + TILE - 1
+        low = 0
         high = ends[-1]
+        for end in ends:
+            low = jnp.where(end <= first, end, low)
         for end in ends[::-1]:
             high = jnp.where(end > last, end, high)
-        counts.append(lax.div(high - 1, TILE) + 1 - tile)
-    return counts
-
-
-def near_kernel(
-    leaf_count, part, parts, sizes_ref, left_ref, right_ref, dd_ref, ds_ref, *refs
-):
-    tall_ref, wide_ref = refs[-2:]
+        low = lax.div(low, 128) * 128
+        begins.append(low)
+        counts.append(lax.div(high - low + (STRIP - 1), STRIP))
+    return begins, counts
+
+
+def near_kernel(leaf_count, part, sizes_ref, left_ref, right_ref, dd_ref, *refs):
+    out_ref = refs[-1]
     ends = leaf_ends(sizes_ref, leaf_count)
     tiles = right_ref.shape[1] // TILE
+    depth = right_ref.shape[0]
+    begins, counts = strip_spans(ends, tiles)
     firsts = [0]
-    for count in tile_counts(ends, tiles):
+    for count in counts:
         firsts.append(firsts[-1] + count)
     groups = lax.div(firsts[-1] + (GROUP - 1), GROUP)
-    offsets = [tile - first for tile, first in zip(range(tiles), firsts)]
+    offsets = [begin - first * STRIP for begin, first in zip(begins, firsts)]
     if part == 0:
-        tall_ref[...] = jnp.zeros_like(tall_ref)
-        wide_ref[...] = jnp.zeros_like(wide_ref)
+        out_ref[...] = jnp.zeros_like(out_ref)
 
     def one_group(group, carry):
         for unit in range(GROUP):
             item = group * GROUP + unit
-            row = 0
+            tile_at = 0
             offset = offsets[0]
             for tile in range(1, tiles):
                 inside = item >= firsts[tile]
-                row = jnp.where(inside, tile, row)
+                tile_at = jnp.where(inside, tile, tile_at)
                 offset = jnp.where(inside, offsets[tile], offset)
             spare = item >= firsts[-1]
-            column = item + offset
-            tall = pl.multiple_of(jnp.where(spare, tiles, row) * TILE, TILE)
-            wide = pl.multiple_of(jnp.where(spare | (row == column), tiles, column) * TILE, TILE)
-            rows = pl.ds(pl.multiple_of(jnp.where(spare, 0, row) * TILE, TILE), TILE)
-            columns = pl.ds(pl.multiple_of(jnp.where(spare, 0, column) * TILE, TILE), TILE)
+            begin = jnp.where(spare, 0, item * STRIP + offset)
+            rows = pl.ds(pl.multiple_of(begin, 128), STRIP)
+            columns = pl.ds(pl.multiple_of(tile_at * TILE, TILE), TILE)
+            source = pl.ds(pl.multiple_of(jnp.where(spare, tiles, tile_at) * TILE, TILE), TILE)
             squared = jnp.dot(
-                left_ref[rows, :], right_ref[:, columns], preferred_element_type=F32
+                left_ref[rows, :depth], right_ref[:, columns], preferred_element_type=F32
             )
             squared = jnp.maximum(squared, 1e-12)
             root = squared * lax.rsqrt(squared)
             kernel = (squared + LINEAR * root + CONSTANT) * jnp.exp2(-root)
             high_part = kernel.astype(BF16)
             low_part = (kernel - high_part.astype(F32)).astype(BF16)
-            weights = dd_ref[columns, :]
-            tall_ref[pl.ds(tall, TILE), :] += jnp.dot(
-                jnp.concatenate([high_part, low_part], axis=1),
-                jnp.concatenate([weights, weights], axis=0),
+            both = jnp.dot(
+                jnp.concatenate([high_part, low_part], axis=0),
+                dd_ref[source, :],
                 preferred_element_type=F32,
             )
-            vectors = ds_ref[:, rows]
-            wide_ref[:, pl.ds(wide, TILE)] += jnp.dot(
-                jnp.concatenate([vectors, vectors], axis=1),
-                jnp.concatenate([high_part, low_part], axis=0),
-                preferred_element_type=F32,
-            )
+            out_ref[rows, :] += folded(both)
         return carry
 
     lax.fori_loop(
-        lax.div(groups * part, parts), lax.div(groups * (part + 1), parts), one_group, 0
-    )
-
-
-def near_part(sizes, prepared, before, after, part, parts):
+        lax.div(groups * part, PARTS), lax.div(groups * (part + 1), PARTS), one_group, 0
+    )
+
+
+def near_part(sizes, prepared, before, after, part):
     leaf_count = sizes.shape[1]
-    left, right, dd, ds = prepared
-    points = right.shape[1]
+    left, right, dd = prepared
     return pl.pallas_call(
-        functools.partial(near_kernel, leaf_count, part, parts),
-        out_shape=(
-            jax.ShapeDtypeStruct((points + TILE, 128), F32),
-            jax.ShapeDtypeStruct((ds.shape[0], points + TILE), F32),
-        ),
-        in_specs=[SMEM] + [VMEM] * (4 + len(before)) + [ANY],
-        out_specs=(VMEM, VMEM),
-        input_output_aliases={5 + index: index for index in range(len(before))},
+        functools.partial(near_kernel, leaf_count, part),
+        out_shape=jax.ShapeDtypeStruct(left.shape, F32),
+        in_specs=[SMEM] + [VMEM] * (3 + len(before)) + [ANY],
+        out_specs=VMEM,
+        input_output_aliases={4: 0} if before else {},
         compiler_params=PARAMS,
         name="near_part",
-    )(sizes, left, right, dd, ds, *before, after)
+    )(sizes, left, right, dd, *before, after)
 
 
 def down_kernel(
@@ -325,7 +319,7 @@
     *rest,
 ):
     side_refs = rest[:levels]
-    tall_ref, wide_ref, a_ref, sums_ref = rest[levels:]
+    near_ref, a_ref, sums_ref = rest[levels:]
     probes, points = d_ref.shape
     down = None
     for level in range(levels - 1, -1, -1):
@@ -376,8 +370,7 @@
             far = jnp.where(leaf == index, term, far)
         d = d_ref[:, first : first + width]
         r = r_ref[:, first : first + width]
-        near = tall_ref[first : first + width, :].T[: 2 * probes]
-        near = folded(near + wide_ref[:, first : first + width])
+        near = folded(near_ref[first : first + width, :].T[: 2 * probes])
         applied = noise * d + near_scale * near + far
         a_ref[:, first : first + width] = applied
         size = jnp.abs(applied)
@@ -393,13 +386,21 @@
         unit = a_ref[:, first : first + width] * inverse
         cross = cross + lanes(r_ref[:, first : first + width] * unit)
         square = square + lanes(unit * unit)
+    columns = [jnp.sum(x, axis=1, keepdims=True) for x in (old, curve, cross, square)]
     lane = lax.broadcasted_iota(jnp.int32, (probes, 128), 1)
-    sums = jnp.where(lane == 0, jnp.sum(old, axis=1, keepdims=True), 0.0)
-    sums = jnp.where(lane == 1, jnp.sum(curve, axis=1, keepdims=True), sums)
-    sums = jnp.where(lane == 2, jnp.sum(cross, axis=1, keepdims=True), sums)
-    sums = jnp.where(lane == 3, jnp.sum(square, axis=1, keepdims=True), sums)
-    sums = jnp.where(lane == 4, top, sums).T[:8]
-    sums_ref[...] = jnp.broadcast_to(sums[None], sums_ref.shape)
+    quantity = lax.div(lane, probes)
+    own = lax.rem(lane, probes) == lax.broadcasted_iota(jnp.int32, (probes, 128), 0)
+    picked = columns[0]
+    for index in range(1, 4):
+        picked = jnp.where(quantity == index, columns[index], picked)
+    row = jnp.concatenate(
+        [
+            jnp.sum(jnp.where(own, picked, 0.0), axis=0, keepdims=True),
+            jnp.sum(jnp.where(own, top, 0.0), axis=0, keepdims=True),
+        ],
+        axis=1,
+    )
+    sums_ref[...] = jnp.broadcast_to(row[None], sums_ref.shape)
 
 
 def descend(
@@ -412,36 +413,39 @@
         functools.partial(down_kernel, leaf_count, len(sides)),
         out_shape=(
             jax.ShapeDtypeStruct((probes, points), F32),
-            jax.ShapeDtypeStruct((2 ** len(sides), 8, probes), F32),
+            jax.ShapeDtypeStruct((2 ** len(sides), 1, 256), F32),
         ),
-        in_specs=[SMEM] + [VMEM] * (12 + len(sides)),
+        in_specs=[SMEM] + [VMEM] * (11 + len(sides)),
         out_specs=(VMEM, VMEM),
         compiler_params=PARAMS,
         name="descend",
     )(
         sizes, noise, scale, direction, residual, basis,
-        node_transfer, node_coupling, upper_transfer, upper_coupling, local, *sides, *near,
+        node_transfer, node_coupling, upper_transfer, upper_coupling, local, *sides, near,
     )
 
 
 def step_kernel(sums_ref, x_ref, r_ref, d_ref, a_ref, nx_ref, nr_ref, nd_ref):
-    sums = sums_ref[...]
     probes = d_ref.shape[0]
-    tops = sums[:, 4:5, :]
+    sums, tops = sums_ref[:, :, :128], sums_ref[:, :, 128:]
     top = jnp.max(tops, axis=0)
     ratio = tops / top
-    old, curve = jnp.sum(sums[:, 0:1, :], axis=0), jnp.sum(sums[:, 1:2, :], axis=0)
-    cross = jnp.sum(sums[:, 2:3, :] * ratio, axis=0)
-    square = jnp.sum(sums[:, 3:4, :] * (ratio * ratio), axis=0)
+    quantity = lax.div(lax.broadcasted_iota(jnp.int32, (1, 1, 128), 2), probes)
+    factor = jnp.where(quantity < 2, 1.0, jnp.where(quantity == 2, ratio, ratio * ratio))
+    total = jnp.sum(sums * factor, axis=0)
+    lane = lax.broadcasted_iota(jnp.int32, (probes, 128), 1)
+    probe = lax.broadcasted_iota(jnp.int32, (probes, 128), 0)
+
+    def column(row, index):
+        return jnp.sum(
+            jnp.where(lane == index * probes + probe, row, 0.0), axis=1, keepdims=True
+        )
+
+    old, curve, cross, square = (column(total, index) for index in range(4))
     step = old / curve
-    reach = step * top
+    reach = step * column(top, 0)
     fresh = old - 2.0 * (reach * cross) + (reach * reach) * square
     beta = fresh / old
-    own = lax.broadcasted_iota(jnp.int32, (probes, probes), 0) == lax.broadcasted_iota(
-        jnp.int32, (probes, probes), 1
-    )
-    step = jnp.sum(jnp.where(own, step, 0.0), axis=1, keepdims=True)
-    beta = jnp.sum(jnp.where(own, beta, 0.0), axis=1, keepdims=True)
     d = d_ref[...]
     nx_ref[...] = x_ref[...] + step * d
     remaining = r_ref[...] - step * a_ref[...]
@@ -464,15 +468,6 @@
 def from_partner(array, stride):
     count = lax.axis_size("leaf")
     return lax.ppermute(array, "leaf", [(i, i ^ stride) for i in range(count)])
-
-
-def level_groups(levels):
-    groups = [[0]]
-    level = 1
-    while level < levels:
-        groups.append(list(range(level, min(level + 2, levels))))
-        level += 2
-    return groups
 
 
 def shards(
@@ -499,40 +494,24 @@
         levels,
     )
     prepared = features(leaf_sizes, lengthscale, coordinates, cluster_order, direction, up)
-    groups = level_groups(levels)
-    parts = 3
-    sides = [None] * levels
+    sides = []
     near = ()
     current = up
-    for number, group in enumerate(groups):
-        base = group[0]
-        strides = [2**level for level in group]
-        incoming = {}
-        for pick in range(1, 2 ** len(group)):
-            stride = sum(s for bit, s in enumerate(strides) if pick >> bit & 1)
-            top = pick.bit_length() - 1
-            incoming[pick] = from_partner(current[top:], stride)
-        if number < parts:
-            near = near_part(leaf_sizes, prepared, near, current, number, parts)
-        for position in range(len(group)):
-            total = current[position]
-            for pick in range(1, 2 ** (position + 1)):
-                top = pick.bit_length() - 1
-                total = total + incoming[pick][position - top]
-            sides[base + position] = total
-        following = current[len(group) :]
-        if following.shape[0]:
-            for pick in range(1, 2 ** len(group)):
-                top = pick.bit_length() - 1
-                following = following + incoming[pick][len(group) - top :]
-        current = following
-    for number in range(len(groups), parts):
-        near = near_part(leaf_sizes, prepared, near, up, number, parts)
+    for level in range(max(levels, PARTS)):
+        if level < levels:
+            incoming = from_partner(current, 2**level)
+        if level < PARTS:
+            near = (near_part(leaf_sizes, prepared, near, current, level),)
+        if level < levels:
+            current = current + incoming
+            sides.append(current[0])
+            current = current[1:] if level + 1 < levels else current
+    near = near[0]
     applied, sums = descend(
         leaf_sizes, noise_variance, outputscale, direction, residual, leaf_basis,
         node_transfer, node_coupling, upper_transfer, upper_coupling, local, sides, near,
     )
-    gathered = lax.all_to_all(sums, "leaf", 0, 0)
+    gathered = lax.all_to_all(sums, "leaf", 0, 0, tiled=True)
     return finish(gathered, solution, residual, direction, applied)
 
 

time: 48.6 us -> 46.7 us (0.961); the launches traced: 48.9 us -> 46.4 us
  Pallas kernels: 20.6 us -> 25.1 us
  blocking collectives: 13.3 us -> 8.95 us
  starting transfers between devices: 10.5 us -> 8.3 us
  waiting for transfers between devices: 0.02 us -> 1.11 us
  other arithmetic: 0.77 us -> 0.05 us
  local copies, waits for them, and re-layouts: 0.78 us -> 0.09 us
    pallas_call x3 -> x5, Pallas kernels: 12.6 us -> 17 us  [near_part(): pl.pallas_call(functools.partial(near_kernel, leaf_count, part), out_shap...]
    all_to_all x1, blocking collectives: 13.3 us -> 8.95 us  [shards(): gathered = lax.all_to_all(sums, 'leaf', 0, 0, tiled=True)]
    ppermute x7 -> x5, starting transfers between devices: 10.5 us -> 8.3 us  [from_partner(): return lax.ppermute(array, 'leaf', [(i, i ^ stride) for i in range(count)])]
    ppermute x7 -> x5, waiting for transfers between devices: 0.02 us -> 1.11 us  [from_partner(): return lax.ppermute(array, 'leaf', [(i, i ^ stride) for i in range(count)])]
    all_to_all x1 -> x0, other arithmetic: 0.72 us -> none  [shards(): gathered = lax.all_to_all(sums, 'leaf', 0, 0)]
    all_to_all x1 -> x0, local copies, waits for them, and re-layouts: 0.51 us -> none  [shards(): gathered = lax.all_to_all(sums, 'leaf', 0, 0)]
  transfers between devices with their start and end apart: 7 -> 5, of which waited for: 0 -> 2; matrix products, arithmetic and copies ran while one was open for 0% -> 0% of each run, Pallas kernels for 29% -> 40%
where the time goes in v4:
time: 46.7 us; the launch traced here: 46.4 us
  Pallas kernels  25.1 us (54%)
  blocking collectives  8.95 us (19%)
  starting transfers between devices  8.3 us (18%)
  between operations  2.89 us (6%)
  waiting for transfers between devices  1.11 us (2%)
    pallas_call x5, Pallas kernels, near_part(): pl.pallas_call(functools.partial(near_kernel, leaf_count, part), out_shap...  17 us
    all_to_all x1, blocking collectives, shards(): gathered = lax.all_to_all(sums, 'leaf', 0, 0, tiled=True)  8.95 us
    ppermute x5, starting transfers between devices, from_partner(): return lax.ppermute(array, 'leaf', [(i, i ^ stride) for i in range(count)])  8.3 us
    pallas_call x1, Pallas kernels, climb(): pl.pallas_call(functools.partial(up_kernel, leaf_count, levels), out_shap...  3.12 us
    pallas_call x1, Pallas kernels, descend(): pl.pallas_call(functools.partial(down_kernel, leaf_count, len(sides)), ou...  2.32 us
    pallas_call x1, Pallas kernels, features(): pl.pallas_call(functools.partial(features_kernel, leaf_count), out_shape=...  1.34 us
    pallas_call x1, Pallas kernels, finish(): pl.pallas_call(step_kernel, out_shape=(shape, shape, shape), in_specs=[VM...  1.26 us
    ppermute x5, waiting for transfers between devices, from_partner(): return lax.ppermute(array, 'leaf', [(i, i ^ stride) for i in range(count)])  1.11 us
  transfers between devices with their start and end apart: 5, of which 2 were waited for; matrix products, arithmetic and copies ran while one was open for 0% of the time, Pallas kernels for 40%

profile of v4, /device:TPU:0, one launch (start us, length us, event | category | flops | bytes accessed | tf_op | source)
XLA Modules:
  0.0 46.4 jit_solution(13305817206048421444)
XLA Ops:
  0.6 0.0 copy-start
  0.6 0.0 copy-start.9
  0.7 0.0 copy-start.10
  0.7 0.0 copy-start.8
  0.7 3.1 %climb.1 = (f32[5,32,128]{2,1,0:T(8,128)S(1)}, f32[3,32,128]{2,1,0:T(8,128)S(1)}) custom-call(s32[1,4]{1,0:T(1,128)} %sizes_ref.13, f32[32,3072]{1,0:T(8,128)} %d_ref.5, bf16[128,3072]{1,0:T(8,128)(2,1)} %basis_ref.1, bf16[1,7,128,128]{3,2,1,0:T(8,128)(2,1)} %nt_ref.1, bf16[1,7,128,128]{3,2,1,0:T(8,128)(2,1)} %nc_ref.1, bf16[1,3,128,128]{3,2,1,0:T(8,128)(2,1)} %ut_ref.1, ...), custom_call_target="tpu_custom_call" | custom-call | tf_op jit(solution)/shard_map/climb/pallas_call | solution.py:125
  3.8 0.5 %collective-permute-start = (f32[5,32,128]{2,1,0:T(8,128)S(1)}, f32[5,32,128]{2,1,0:T(8,128)S(1)}, u32[]{:S(2)}, u32[]{:S(2)}) collective-permute-start(f32[5,32,128]{2,1,0:T(8,128)S(1)} %get-tuple-element.11.after_ref.refs_0_), channel_id=1, source_target_pairs={{0,1},{1,0},{2,3},{3,2},{4,5},{5,4},{6,7},{7,6},{8,9},{9,8},{10,11... | collective-permute-start | bytes 245768 | tf_op jit(solution)/shard_map/ppermute | solution.py:470
  4.3 0.9 %collective-permute-done = f32[5,32,128]{2,1,0:T(8,128)S(1)} collective-permute-done((f32[5,32,128]{2,1,0:T(8,128)S(1)}, f32[5,32,128]{2,1,0:T(8,128)S(1)}, u32[]{:S(2)}, u32[]{:S(2)}) %collective-permute-start) | collective-permute-done | bytes 81952 | tf_op jit(solution)/shard_map/ppermute | solution.py:470
  5.3 2.9 %collective-permute-start.1 = (f32[4,32,128]{2,1,0:T(8,128)S(1)}, f32[4,32,128]{2,1,0:T(8,128)S(1)}, u32[]{:S(2)}, u32[]{:S(2)}) collective-permute-start(f32[4,32,128]{2,1,0:T(8,128)S(1)} %slice.33.refs_1_), channel_id=1, source_target_pairs={{0,2},{1,3},{2,0},{3,1},{4,6},{5,7},{6,4},{7,5},{8,10},{9,11},{10,... | collective-permute-start | bytes 196616 | tf_op jit(solution)/shard_map/ppermute | solution.py:470
  10.1 0.0 copy-done
  10.1 0.0 copy-done.9
  10.1 0.0 copy-done.10
  10.2 0.0 copy-done.8
  10.2 1.3 %features.1 = (bf16[3584,128]{1,0:T(8,128)(2,1)S(1)}, bf16[48,3072]{1,0:T(8,128)(2,1)S(1)}, bf16[3328,128]{1,0:T(8,128)(2,1)S(1)}) custom-call(s32[1,4]{1,0:T(1,128)S(1)} %copy-done.9, f32[1]{0:T(128)S(6)} %copy.25.length_ref, f32[3,3072]{1,0:T(4,128)S(1)} %copy-done.8, s32[24,128]{1,0:T(8,128)S(1)} %bitcast.11, f32[32,3072]{1,0:T(8,128)S(1)} %copy-done, ...), custom_call_target="tpu_custom_call" | custom-call | tf_op jit(solution)/shard_map/features/pallas_call | solution.py:210
  11.5 3.3 %near_part.5.refs_0_ = f32[3584,128]{1,0:T(8,128)S(1)} custom-call(s32[1,4]{1,0:T(1,128)S(1)} %copy-done.9, bf16[3584,128]{1,0:T(8,128)(2,1)S(1)} %get-tuple-element.12.left_ref, bf16[48,3072]{1,0:T(8,128)(2,1)S(1)} %get-tuple-element.13.right_ref, bf16[3328,128]{1,0:T(8,128)(2,1)S(1)} %get-tuple-element.14.dd_ref, ...), custom_call_target="tpu_custom_call" | custom-call | tf_op jit(solution)/shard_map/near_part/pallas_call | solution.py:294
  14.8 0.0 collective-permute-done.1
  14.8 0.7 %collective-permute-start.2 = (f32[3,32,128]{2,1,0:T(8,128)S(1)}, f32[3,32,128]{2,1,0:T(8,128)S(1)}, u32[]{:S(2)}, u32[]{:S(2)}) collective-permute-start(f32[3,32,128]{2,1,0:T(8,128)S(1)} %slice.35.refs_1_), channel_id=1, source_target_pairs={{0,4},{1,5},{2,6},{3,7},{4,0},{5,1},{6,2},{7,3},{8,12},{9,13},{10,... | collective-permute-start | bytes 147464 | tf_op jit(solution)/shard_map/ppermute | solution.py:470
  15.6 3.2 %near_part.6.refs_0_ = f32[3584,128]{1,0:T(8,128)S(1)} custom-call(s32[1,4]{1,0:T(1,128)S(1)} %copy-done.9, bf16[3584,128]{1,0:T(8,128)(2,1)S(1)} %get-tuple-element.12.left_ref, bf16[48,3072]{1,0:T(8,128)(2,1)S(1)} %get-tuple-element.13.right_ref, bf16[3328,128]{1,0:T(8,128)(2,1)S(1)} %get-tuple-element.14.dd_ref, ...), custom_call_target="tpu_custom_call", output_to_operand_aliasing={{}: (4, {})} | custom-call | tf_op jit(solution)/shard_map/near_part/pallas_call | solution.py:294
  18.8 0.2 collective-permute-done.2
  19.0 1.5 %collective-permute-start.3 = (f32[2,32,128]{2,1,0:T(8,128)S(1)}, f32[2,32,128]{2,1,0:T(8,128)S(1)}, u32[]{:S(2)}, u32[]{:S(2)}) collective-permute-start(f32[2,32,128]{2,1,0:T(8,128)S(1)} %slice.37.refs_1_), channel_id=1, source_target_pairs={{0,8},{1,9},{2,10},{3,11},{4,12},{5,13},{6,14},{7,15},{8,0},{9,1},... | collective-permute-start | bytes 98312 | tf_op jit(solution)/shard_map/ppermute | solution.py:470
  20.5 3.2 %near_part.7.refs_0_ = f32[3584,128]{1,0:T(8,128)S(1)} custom-call(s32[1,4]{1,0:T(1,128)S(1)} %copy-done.9, bf16[3584,128]{1,0:T(8,128)(2,1)S(1)} %get-tuple-element.12.left_ref, bf16[48,3072]{1,0:T(8,128)(2,1)S(1)} %get-tuple-element.13.right_ref, bf16[3328,128]{1,0:T(8,128)(2,1)S(1)} %get-tuple-element.14.dd_ref, ...), custom_call_target="tpu_custom_call", output_to_operand_aliasing={{}: (4, {})} | custom-call | tf_op jit(solution)/shard_map/near_part/pallas_call | solution.py:294
  23.7 0.0 collective-permute-done.3
  23.8 2.7 %collective-permute-start.4 = (f32[1,32,128]{2,1,0:T(8,128)S(1)}, f32[1,32,128]{2,1,0:T(8,128)S(1)}, u32[]{:S(2)}, u32[]{:S(2)}) collective-permute-start(f32[1,32,128]{2,1,0:T(8,128)S(1)} %slice.39.refs_1_), channel_id=1, source_target_pairs={{0,16},{1,17},{2,18},{3,19},{4,20},{5,21},{6,22},{7,23},{8,24},{9,... | collective-permute-start | bytes 49160 | tf_op jit(solution)/shard_map/ppermute | solution.py:470
  26.4 3.2 %near_part.8.refs_0_ = f32[3584,128]{1,0:T(8,128)S(1)} custom-call(s32[1,4]{1,0:T(1,128)S(1)} %copy-done.9, bf16[3584,128]{1,0:T(8,128)(2,1)S(1)} %get-tuple-element.12.left_ref, bf16[48,3072]{1,0:T(8,128)(2,1)S(1)} %get-tuple-element.13.right_ref, bf16[3328,128]{1,0:T(8,128)(2,1)S(1)} %get-tuple-element.14.dd_ref, ...), custom_call_target="tpu_custom_call", output_to_operand_aliasing={{}: (4, {})} | custom-call | tf_op jit(solution)/shard_map/near_part/pallas_call | solution.py:294
  29.7 0.0 copy-start.1
  29.7 0.0 copy-start.2
  29.7 0.0 copy-start.3
  29.7 0.0 copy-start.4
  29.7 0.0 copy-start.5
  29.7 0.0 copy-start.6
  29.7 4.1 %near_part.9.rest_5_ = f32[3584,128]{1,0:T(8,128)S(1)} custom-call(s32[1,4]{1,0:T(1,128)S(1)} %copy-done.9, bf16[3584,128]{1,0:T(8,128)(2,1)S(1)} %get-tuple-element.12.left_ref, bf16[48,3072]{1,0:T(8,128)(2,1)S(1)} %get-tuple-element.13.right_ref, bf16[3328,128]{1,0:T(8,128)(2,1)S(1)} %get-tuple-element.14.dd_ref, ...), custom_call_target="tpu_custom_call", output_to_operand_aliasing={{}: (4, {})} | custom-call | tf_op jit(solution)/shard_map/near_part/pallas_call | solution.py:294
  33.8 0.0 collective-permute-done.4
  33.8 0.0 copy-done.1
  33.8 0.0 copy-done.2
  33.9 0.0 copy-done.3
  33.9 0.0 copy-done.4
  33.9 0.0 copy-done.5
  33.9 0.0 copy-done.6
  33.9 0.0 copy-start.7
  33.9 2.3 %descend.1 = (f32[32,3072]{1,0:T(8,128)S(1)}, f32[32,1,256]{2,1,0:T(1,128)S(1)}) custom-call(s32[1,4]{1,0:T(1,128)S(1)} %copy-done.9, f32[1]{0:T(128)S(6)} %copy.27.noise_ref, f32[1]{0:T(128)S(6)} %copy.26.scale_ref, f32[32,3072]{1,0:T(8,128)S(1)} %copy-done, f32[32,3072]{1,0:T(8,128)S(1)} %copy-done.2, bf16[128,3072]{1,0:T(8,128)(2,1)S(1)} %copy-done.1, ...), custom_call_target="tpu_custom_call" | custom-call | tf_op jit(solution)/shard_map/descend/pallas_call | solution.py:412
  36.2 8.9 %all_to_all.5.sums_ref = f32[32,1,256]{2,1,0:T(1,128)S(1)} all-to-all(f32[32,1,256]{2,1,0:T(1,128)S(1)} %get-tuple-element.15), channel_id=1, replica_groups=mesh['leaf'=32] {'leaf'}, dimensions={0} | all-to-all | bytes 65536 | tf_op jit(solution)/shard_map/all_to_all | solution.py:514
  45.2 0.0 copy-done.7
  45.2 1.3 %finish.1 = (f32[32,3072]{1,0:T(8,128)}, f32[32,3072]{1,0:T(8,128)}, f32[32,3072]{1,0:T(8,128)}) custom-call(f32[32,1,256]{2,1,0:T(1,128)S(1)} %all_to_all.5.sums_ref, f32[32,3072]{1,0:T(8,128)S(1)} %copy-done.7, f32[32,3072]{1,0:T(8,128)S(1)} %copy-done.2, f32[32,3072]{1,0:T(8,128)S(1)} %copy-done, f32[32,3072]{1,0:T(8,128)S(1)} %get-tuple-element.16.a_ref), custom_call_target="tpu_custom_call" | custom-call | tf_op jit(solution)/shard_map/finish/pallas_call | solution.py:458
  (12 shorter events, 0.1 us)
Async XLA Ops:
  0.6 9.5 %copy-start = (f32[32,3072]{1,0:T(8,128)S(1)}, f32[32,3072]{1,0:T(8,128)}, u32[]{:S(2)}) copy-start(f32[32,3072]{1,0:T(8,128)} %d_ref.5) | copy-start | bytes 1179652
  0.6 9.5 %copy-start.9 = (s32[1,4]{1,0:T(1,128)S(1)}, s32[1,4]{1,0:T(1,128)}, u32[]{:S(2)}) copy-start(s32[1,4]{1,0:T(1,128)} %sizes_ref.13) | copy-start | bytes 52
  0.7 9.5 %copy-start.10 = (s32[3072]{0:T(1024)S(1)}, s32[3072]{0:T(1024)}, u32[]{:S(2)}) copy-start(s32[3072]{0:T(1024)} %param.18) | copy-start | bytes 36868
  0.7 9.5 %copy-start.8 = (f32[3,3072]{1,0:T(4,128)S(1)}, f32[3,3072]{1,0:T(4,128)}, u32[]{:S(2)}) copy-start(f32[3,3072]{1,0:T(4,128)} %coords_ref.1) | copy-start | bytes 110596
  3.8 1.4 %collective-permute-start = (f32[5,32,128]{2,1,0:T(8,128)S(1)}, f32[5,32,128]{2,1,0:T(8,128)S(1)}, u32[]{:S(2)}, u32[]{:S(2)}) collective-permute-start(f32[5,32,128]{2,1,0:T(8,128)S(1)} %get-tuple-element.11.after_ref.refs_0_), channel_id=1, source_target_pairs={{0,1},{1,0},{2,3},{3,2},{4,5},{5,4},{6,7},{7,6},{8,9},{9,8},{10,11... | collective-permute-start | bytes 245768 | tf_op jit(solution)/shard_map/ppermute | solution.py:470
  5.3 9.5 %collective-permute-start.1 = (f32[4,32,128]{2,1,0:T(8,128)S(1)}, f32[4,32,128]{2,1,0:T(8,128)S(1)}, u32[]{:S(2)}, u32[]{:S(2)}) collective-permute-start(f32[4,32,128]{2,1,0:T(8,128)S(1)} %slice.33.refs_1_), channel_id=1, source_target_pairs={{0,2},{1,3},{2,0},{3,1},{4,6},{5,7},{6,4},{7,5},{8,10},{9,11},{10,... | collective-permute-start | bytes 196616 | tf_op jit(solution)/shard_map/ppermute | solution.py:470
  14.8 4.2 %collective-permute-start.2 = (f32[3,32,128]{2,1,0:T(8,128)S(1)}, f32[3,32,128]{2,1,0:T(8,128)S(1)}, u32[]{:S(2)}, u32[]{:S(2)}) collective-permute-start(f32[3,32,128]{2,1,0:T(8,128)S(1)} %slice.35.refs_1_), channel_id=1, source_target_pairs={{0,4},{1,5},{2,6},{3,7},{4,0},{5,1},{6,2},{7,3},{8,12},{9,13},{10,... | collective-permute-start | bytes 147464 | tf_op jit(solution)/shard_map/ppermute | solution.py:470
  19.0 4.7 %collective-permute-start.3 = (f32[2,32,128]{2,1,0:T(8,128)S(1)}, f32[2,32,128]{2,1,0:T(8,128)S(1)}, u32[]{:S(2)}, u32[]{:S(2)}) collective-permute-start(f32[2,32,128]{2,1,0:T(8,128)S(1)} %slice.37.refs_1_), channel_id=1, source_target_pairs={{0,8},{1,9},{2,10},{3,11},{4,12},{5,13},{6,14},{7,15},{8,0},{9,1},... | collective-permute-start | bytes 98312 | tf_op jit(solution)/shard_map/ppermute | solution.py:470
  23.8 10.1 %collective-permute-start.4 = (f32[1,32,128]{2,1,0:T(8,128)S(1)}, f32[1,32,128]{2,1,0:T(8,128)S(1)}, u32[]{:S(2)}, u32[]{:S(2)}) collective-permute-start(f32[1,32,128]{2,1,0:T(8,128)S(1)} %slice.39.refs_1_), channel_id=1, source_target_pairs={{0,16},{1,17},{2,18},{3,19},{4,20},{5,21},{6,22},{7,23},{8,24},{9,... | collective-permute-start | bytes 49160 | tf_op jit(solution)/shard_map/ppermute | solution.py:470
  29.7 4.2 %copy-start.1 = (bf16[128,3072]{1,0:T(8,128)(2,1)S(1)}, bf16[128,3072]{1,0:T(8,128)(2,1)}, u32[]{:S(2)}) copy-start(bf16[128,3072]{1,0:T(8,128)(2,1)} %basis_ref.1) | copy-start | bytes 2359300
  29.7 4.2 %copy-start.2 = (f32[32,3072]{1,0:T(8,128)S(1)}, f32[32,3072]{1,0:T(8,128)}, u32[]{:S(2)}) copy-start(f32[32,3072]{1,0:T(8,128)} %r_ref.3) | copy-start | bytes 1179652
  29.7 4.2 %copy-start.3 = (bf16[1,7,128,128]{3,2,1,0:T(8,128)(2,1)S(1)}, bf16[1,7,128,128]{3,2,1,0:T(8,128)(2,1)}, u32[]{:S(2)}) copy-start(bf16[1,7,128,128]{3,2,1,0:T(8,128)(2,1)} %nt_ref.1) | copy-start | bytes 688132
  29.7 4.2 %copy-start.4 = (bf16[1,7,128,128]{3,2,1,0:T(8,128)(2,1)S(1)}, bf16[1,7,128,128]{3,2,1,0:T(8,128)(2,1)}, u32[]{:S(2)}) copy-start(bf16[1,7,128,128]{3,2,1,0:T(8,128)(2,1)} %nc_ref.1) | copy-start | bytes 688132
  29.7 4.2 %copy-start.5 = (bf16[1,4,128,128]{3,2,1,0:T(8,128)(2,1)S(1)}, bf16[1,4,128,128]{3,2,1,0:T(8,128)(2,1)}, u32[]{:S(2)}) copy-start(bf16[1,4,128,128]{3,2,1,0:T(8,128)(2,1)} %uc_ref.1) | copy-start | bytes 393220
  29.7 4.2 %copy-start.6 = (bf16[1,3,128,128]{3,2,1,0:T(8,128)(2,1)S(1)}, bf16[1,3,128,128]{3,2,1,0:T(8,128)(2,1)}, u32[]{:S(2)}) copy-start(bf16[1,3,128,128]{3,2,1,0:T(8,128)(2,1)} %ut_ref.1) | copy-start | bytes 294916
  33.9 11.3 %copy-start.7 = (f32[32,3072]{1,0:T(8,128)S(1)}, f32[32,3072]{1,0:T(8,128)}, u32[]{:S(2)}) copy-start(f32[32,3072]{1,0:T(8,128)} %x_ref.1) | copy-start | bytes 1179652

commit v5 on v4

--- a/solution.py
+++ b/solution.py
@@ -10,7 +10,7 @@
 
 F32 = jnp.float32
 BF16 = jnp.bfloat16
-TILE = 256
+TILE = 128
 FAR_AWAY = 32768.0
 LOG2E = 1.0 / math.log(2.0)
 POLY = math.log(2.0) ** 2 / 3.0
@@ -21,8 +21,8 @@
 SMEM = pl.BlockSpec(memory_space=pltpu.SMEM)
 ANY = pl.BlockSpec(memory_space=pl.ANY)
 HBM = pl.BlockSpec(memory_space=pltpu.HBM)
-STRIP = 512
-GROUP = 2
+STRIP = 384
+GROUP = 4
 PARTS = 5
 PARAMS = pltpu.CompilerParams(vmem_limit_bytes=48 * 1024 * 1024)
 
@@ -275,12 +275,12 @@
             kernel = (squared + LINEAR * root + CONSTANT) * jnp.exp2(-root)
             high_part = kernel.astype(BF16)
             low_part = (kernel - high_part.astype(F32)).astype(BF16)
-            both = jnp.dot(
-                jnp.concatenate([high_part, low_part], axis=0),
-                dd_ref[source, :],
+            weights = dd_ref[source, :]
+            out_ref[rows, :] += jnp.dot(
+                jnp.concatenate([high_part, low_part], axis=1),
+                jnp.concatenate([weights, weights], axis=0),
                 preferred_element_type=F32,
             )
-            out_ref[rows, :] += folded(both)
         return carry
 
     lax.fori_loop(
@@ -400,7 +400,7 @@
         ],
         axis=1,
     )
-    sums_ref[...] = jnp.broadcast_to(row[None], sums_ref.shape)
+    sums_ref[...] = row[None]
 
 
 def descend(
@@ -413,7 +413,7 @@
         functools.partial(down_kernel, leaf_count, len(sides)),
         out_shape=(
             jax.ShapeDtypeStruct((probes, points), F32),
-            jax.ShapeDtypeStruct((2 ** len(sides), 1, 256), F32),
+            jax.ShapeDtypeStruct((1, 1, 256), F32),
         ),
         in_specs=[SMEM] + [VMEM] * (11 + len(sides)),
         out_specs=(VMEM, VMEM),
@@ -425,14 +425,34 @@
     )
 
 
-def step_kernel(sums_ref, x_ref, r_ref, d_ref, a_ref, nx_ref, nr_ref, nd_ref):
-    probes = d_ref.shape[0]
-    sums, tops = sums_ref[:, :, :128], sums_ref[:, :, 128:]
+def merged(sums, probes):
+    values, tops = sums[:, :, :128], sums[:, :, 128:]
     top = jnp.max(tops, axis=0)
     ratio = tops / top
     quantity = lax.div(lax.broadcasted_iota(jnp.int32, (1, 1, 128), 2), probes)
     factor = jnp.where(quantity < 2, 1.0, jnp.where(quantity == 2, ratio, ratio * ratio))
-    total = jnp.sum(sums * factor, axis=0)
+    return jnp.sum(values * factor, axis=0), top
+
+
+def pair_kernel(probes, own_ref, other_ref, out_ref):
+    total, top = merged(jnp.concatenate([own_ref[...], other_ref[...]], axis=0), probes)
+    out_ref[...] = jnp.broadcast_to(jnp.concatenate([total, top], axis=1)[None], out_ref.shape)
+
+
+def merge_pair(own, other, probes, copies):
+    return pl.pallas_call(
+        functools.partial(pair_kernel, probes),
+        out_shape=jax.ShapeDtypeStruct((copies, 1, 256), F32),
+        in_specs=[VMEM, VMEM],
+        out_specs=VMEM,
+        compiler_params=PARAMS,
+        name="merge_pair",
+    )(own, other)
+
+
+def step_kernel(sums_ref, x_ref, r_ref, d_ref, a_ref, nx_ref, nr_ref, nd_ref):
+    probes = d_ref.shape[0]
+    total, top = merged(sums_ref[...], probes)
     lane = lax.broadcasted_iota(jnp.int32, (probes, 128), 1)
     probe = lax.broadcasted_iota(jnp.int32, (probes, 128), 0)
 
@@ -511,7 +531,16 @@
         leaf_sizes, noise_variance, outputscale, direction, residual, leaf_basis,
         node_transfer, node_coupling, upper_transfer, upper_coupling, local, sides, near,
     )
-    gathered = lax.all_to_all(sums, "leaf", 0, 0, tiled=True)
+    chips = lax.axis_size("leaf") // 2
+    copies = merge_pair(sums, from_partner(sums, 1), probes, chips)
+    gathered = lax.all_to_all(
+        copies,
+        "leaf",
+        0,
+        0,
+        axis_index_groups=[[2 * chip + core for chip in range(chips)] for core in range(2)],
+        tiled=True,
+    )
     return finish(gathered, solution, residual, direction, applied)
 
 

time: 46.7 us -> 52.5 us (1.12)
  Pallas kernels: 25.1 us -> 27.9 us
  starting transfers between devices: 8.3 us -> 9.37 us
  blocking collectives: 8.95 us -> 9.91 us
  waiting for transfers between devices: 1.11 us -> 2.06 us
    pallas_call x5, Pallas kernels: 17 us -> 19.9 us  [near_part(): pl.pallas_call(functools.partial(near_kernel, leaf_count, part), out_shap...]
    ppermute x5 -> x6, starting transfers between devices: 8.3 us -> 9.37 us  [from_partner(): return lax.ppermute(array, 'leaf', [(i, i ^ stride) for i in range(count)])]
    all_to_all x1, blocking collectives: 8.95 us -> 9.91 us  [shards(): lax.all_to_all(copies, 'leaf', 0, 0, axis_index_groups=[[2 * chip + core...]
    ppermute x5 -> x6, waiting for transfers between devices: 1.11 us -> 2.06 us  [from_partner(): return lax.ppermute(array, 'leaf', [(i, i ^ stride) for i in range(count)])]
  transfers between devices with their start and end apart: 5 -> 6, of which waited for: 2 -> 2; matrix products, arithmetic and copies ran while one was open for 0% -> 0% of each run, Pallas kernels for 40% -> 41%
where the time goes in v5:
time: 52.5 us; the launch traced here: 52.3 us
  Pallas kernels  27.9 us (53%)
  blocking collectives  9.91 us (19%)
  starting transfers between devices  9.37 us (18%)
  between operations  2.91 us (6%)
  waiting for transfers between devices  2.06 us (4%)
    pallas_call x5, Pallas kernels, near_part(): pl.pallas_call(functools.partial(near_kernel, leaf_count, part), out_shap...  19.9 us
    all_to_all x1, blocking collectives, shards(): lax.all_to_all(copies, 'leaf', 0, 0, axis_index_groups=[[2 * chip + core...  9.91 us
    ppermute x6, starting transfers between devices, from_partner(): return lax.ppermute(array, 'leaf', [(i, i ^ stride) for i in range(count)])  9.37 us
    pallas_call x1, Pallas kernels, climb(): pl.pallas_call(functools.partial(up_kernel, leaf_count, levels), out_shap...  3.12 us
    pallas_call x1, Pallas kernels, descend(): pl.pallas_call(functools.partial(down_kernel, leaf_count, len(sides)), ou...  2.33 us
    ppermute x6, waiting for transfers between devices, from_partner(): return lax.ppermute(array, 'leaf', [(i, i ^ stride) for i in range(count)])  2.06 us
    pallas_call x1, Pallas kernels, features(): pl.pallas_call(functools.partial(features_kernel, leaf_count), out_shape=...  1.34 us
    pallas_call x1, Pallas kernels, finish(): pl.pallas_call(step_kernel, out_shape=(shape, shape, shape), in_specs=[VM...  1.25 us
  transfers between devices with their start and end apart: 6, of which 2 were waited for; matrix products, arithmetic and copies ran while one was open for 0% of the time, Pallas kernels for 41%

profile of v5, /device:TPU:0, one launch (start us, length us, event | category | flops | bytes accessed | tf_op | source)
XLA Modules:
  0.0 52.3 jit_solution(11731803310731280979)
XLA Ops:
  0.6 0.0 copy-start
  0.6 0.0 copy-start.9
  0.7 0.0 copy-start.10
  0.7 0.0 copy-start.8
  0.7 3.1 %climb.1 = (f32[5,32,128]{2,1,0:T(8,128)S(1)}, f32[3,32,128]{2,1,0:T(8,128)S(1)}) custom-call(s32[1,4]{1,0:T(1,128)} %sizes_ref.13, f32[32,3072]{1,0:T(8,128)} %d_ref.5, bf16[128,3072]{1,0:T(8,128)(2,1)} %basis_ref.1, bf16[1,7,128,128]{3,2,1,0:T(8,128)(2,1)} %nt_ref.1, bf16[1,7,128,128]{3,2,1,0:T(8,128)(2,1)} %nc_ref.1, bf16[1,3,128,128]{3,2,1,0:T(8,128)(2,1)} %ut_ref.1, ...), custom_call_target="tpu_custom_call" | custom-call | tf_op jit(solution)/shard_map/climb/pallas_call | solution.py:125
  3.8 0.5 collective-permute-start
  4.3 0.9 %collective-permute-done = f32[5,32,128]{2,1,0:T(8,128)S(1)} collective-permute-done((f32[5,32,128]{2,1,0:T(8,128)S(1)}, f32[5,32,128]{2,1,0:T(8,128)S(1)}, u32[]{:S(2)}, u32[]{:S(2)}) %collective-permute-start) | collective-permute-done | bytes 81952 | tf_op jit(solution)/shard_map/ppermute | solution.py:490
  5.3 2.9 %collective-permute-start.1 = (f32[4,32,128]{2,1,0:T(8,128)S(1)}, f32[4,32,128]{2,1,0:T(8,128)S(1)}, u32[]{:S(2)}, u32[]{:S(2)}) collective-permute-start(f32[4,32,128]{2,1,0:T(8,128)S(1)} %slice.33.refs_1_), channel_id=1, source_target_pairs={{0,2},{1,3},{2,0},{3,1},{4,6},{5,7},{6,4},{7,5},{8,10},{9,11},{10,... | collective-permute-start | bytes 196616 | tf_op jit(solution)/shard_map/ppermute | solution.py:490
  10.1 0.0 copy-done
  10.1 0.0 copy-done.9
  10.1 0.0 copy-done.10
  10.2 0.0 copy-done.8
  10.2 1.3 %features.1 = (bf16[3456,128]{1,0:T(8,128)(2,1)S(1)}, bf16[48,3072]{1,0:T(8,128)(2,1)S(1)}, bf16[3200,128]{1,0:T(8,128)(2,1)S(1)}) custom-call(s32[1,4]{1,0:T(1,128)S(1)} %copy-done.9, f32[1]{0:T(128)S(6)} %copy.25.length_ref, f32[3,3072]{1,0:T(4,128)S(1)} %copy-done.8, s32[24,128]{1,0:T(8,128)S(1)} %bitcast.11, f32[32,3072]{1,0:T(8,128)S(1)} %copy-done, ...), custom_call_target="tpu_custom_call" | custom-call | tf_op jit(solution)/shard_map/features/pallas_call | solution.py:210
  11.5 3.5 %near_part.5.refs_0_ = f32[3456,128]{1,0:T(8,128)S(1)} custom-call(s32[1,4]{1,0:T(1,128)S(1)} %copy-done.9, bf16[3456,128]{1,0:T(8,128)(2,1)S(1)} %get-tuple-element.12.left_ref, bf16[48,3072]{1,0:T(8,128)(2,1)S(1)} %get-tuple-element.13.right_ref, bf16[3200,128]{1,0:T(8,128)(2,1)S(1)} %get-tuple-element.14.dd_ref, ...), custom_call_target="tpu_custom_call" | custom-call | tf_op jit(solution)/shard_map/near_part/pallas_call | solution.py:294
  15.0 0.0 collective-permute-done.1
  15.0 1.6 %collective-permute-start.2 = (f32[3,32,128]{2,1,0:T(8,128)S(1)}, f32[3,32,128]{2,1,0:T(8,128)S(1)}, u32[]{:S(2)}, u32[]{:S(2)}) collective-permute-start(f32[3,32,128]{2,1,0:T(8,128)S(1)} %slice.35.refs_1_), channel_id=1, source_target_pairs={{0,4},{1,5},{2,6},{3,7},{4,0},{5,1},{6,2},{7,3},{8,12},{9,13},{10,... | collective-permute-start | bytes 147464 | tf_op jit(solution)/shard_map/ppermute | solution.py:490
  16.6 4.3 %near_part.6.refs_0_ = f32[3456,128]{1,0:T(8,128)S(1)} custom-call(s32[1,4]{1,0:T(1,128)S(1)} %copy-done.9, bf16[3456,128]{1,0:T(8,128)(2,1)S(1)} %get-tuple-element.12.left_ref, bf16[48,3072]{1,0:T(8,128)(2,1)S(1)} %get-tuple-element.13.right_ref, bf16[3200,128]{1,0:T(8,128)(2,1)S(1)} %get-tuple-element.14.dd_ref, ...), custom_call_target="tpu_custom_call", output_to_operand_aliasing={{}: (4, {})} | custom-call | tf_op jit(solution)/shard_map/near_part/pallas_call | solution.py:294
  20.9 0.0 collective-permute-done.2
  21.0 1.6 %collective-permute-start.3 = (f32[2,32,128]{2,1,0:T(8,128)S(1)}, f32[2,32,128]{2,1,0:T(8,128)S(1)}, u32[]{:S(2)}, u32[]{:S(2)}) collective-permute-start(f32[2,32,128]{2,1,0:T(8,128)S(1)} %slice.37.refs_1_), channel_id=1, source_target_pairs={{0,8},{1,9},{2,10},{3,11},{4,12},{5,13},{6,14},{7,15},{8,0},{9,1},... | collective-permute-start | bytes 98312 | tf_op jit(solution)/shard_map/ppermute | solution.py:490
  22.6 3.5 %near_part.7.refs_0_ = f32[3456,128]{1,0:T(8,128)S(1)} custom-call(s32[1,4]{1,0:T(1,128)S(1)} %copy-done.9, bf16[3456,128]{1,0:T(8,128)(2,1)S(1)} %get-tuple-element.12.left_ref, bf16[48,3072]{1,0:T(8,128)(2,1)S(1)} %get-tuple-element.13.right_ref, bf16[3200,128]{1,0:T(8,128)(2,1)S(1)} %get-tuple-element.14.dd_ref, ...), custom_call_target="tpu_custom_call", output_to_operand_aliasing={{}: (4, {})} | custom-call | tf_op jit(solution)/shard_map/near_part/pallas_call | solution.py:294
  26.1 0.0 collective-permute-done.3
  26.1 2.7 %collective-permute-start.4 = (f32[1,32,128]{2,1,0:T(8,128)S(1)}, f32[1,32,128]{2,1,0:T(8,128)S(1)}, u32[]{:S(2)}, u32[]{:S(2)}) collective-permute-start(f32[1,32,128]{2,1,0:T(8,128)S(1)} %slice.39.refs_1_), channel_id=1, source_target_pairs={{0,16},{1,17},{2,18},{3,19},{4,20},{5,21},{6,22},{7,23},{8,24},{9,... | collective-permute-start | bytes 49160 | tf_op jit(solution)/shard_map/ppermute | solution.py:490
  28.8 4.3 %near_part.8.refs_0_ = f32[3456,128]{1,0:T(8,128)S(1)} custom-call(s32[1,4]{1,0:T(1,128)S(1)} %copy-done.9, bf16[3456,128]{1,0:T(8,128)(2,1)S(1)} %get-tuple-element.12.left_ref, bf16[48,3072]{1,0:T(8,128)(2,1)S(1)} %get-tuple-element.13.right_ref, bf16[3200,128]{1,0:T(8,128)(2,1)S(1)} %get-tuple-element.14.dd_ref, ...), custom_call_target="tpu_custom_call", output_to_operand_aliasing={{}: (4, {})} | custom-call | tf_op jit(solution)/shard_map/near_part/pallas_call | solution.py:294
  33.1 0.0 copy-start.1
  33.1 0.0 copy-start.2
  33.1 0.0 copy-start.3
  33.1 0.0 copy-start.4
  33.1 0.0 copy-start.5
  33.2 0.0 copy-start.6
  33.2 4.3 %near_part.9.rest_5_ = f32[3456,128]{1,0:T(8,128)S(1)} custom-call(s32[1,4]{1,0:T(1,128)S(1)} %copy-done.9, bf16[3456,128]{1,0:T(8,128)(2,1)S(1)} %get-tuple-element.12.left_ref, bf16[48,3072]{1,0:T(8,128)(2,1)S(1)} %get-tuple-element.13.right_ref, bf16[3200,128]{1,0:T(8,128)(2,1)S(1)} %get-tuple-element.14.dd_ref, ...), custom_call_target="tpu_custom_call", output_to_operand_aliasing={{}: (4, {})} | custom-call | tf_op jit(solution)/shard_map/near_part/pallas_call | solution.py:294
  37.5 0.0 collective-permute-done.4
  37.5 0.0 copy-done.1
  37.5 0.0 copy-done.2
  37.5 0.0 copy-done.3
  37.6 0.0 copy-done.4
  37.6 0.0 copy-done.5
  37.6 0.0 copy-done.6
  37.6 0.0 copy-start.7
  37.6 2.3 %descend.1 = (f32[32,3072]{1,0:T(8,128)S(1)}, f32[1,1,256]{2,1,0:T(1,128)S(1)}) custom-call(s32[1,4]{1,0:T(1,128)S(1)} %copy-done.9, f32[1]{0:T(128)S(6)} %copy.27.noise_ref, f32[1]{0:T(128)S(6)} %copy.26.scale_ref, f32[32,3072]{1,0:T(8,128)S(1)} %copy-done, f32[32,3072]{1,0:T(8,128)S(1)} %copy-done.2, bf16[128,3072]{1,0:T(8,128)(2,1)S(1)} %copy-done.1, ...), custom_call_target="tpu_custom_call" | custom-call | tf_op jit(solution)/shard_map/descend/pallas_call | solution.py:412
  39.9 0.1 collective-permute-start.5
  40.0 1.1 %collective-permute-done.5.other_ref = f32[1,1,256]{2,1,0:T(1,128)S(1)} collective-permute-done((f32[1,1,256]{2,1,0:T(1,128)S(1)}, f32[1,1,256]{2,1,0:T(1,128)S(1)}, u32[]{:S(2)}, u32[]{:S(2)}) %collective-permute-start.5) | collective-permute-done | bytes 1056 | tf_op jit(solution)/shard_map/ppermute | solution.py:490
  41.1 9.9 %all_to_all.5.sums_ref = f32[16,1,256]{2,1,0:T(1,128)S(1)} all-to-all(f32[16,1,256]{2,1,0:T(1,128)S(1)} %merge_pair.1), channel_id=1, replica_groups={{0,2,4,6,8,10,12,14,16,18,20,22,24,26,28,30},{1,3,5,7,9,11,13,15,17,19,..., dimensions={0} | all-to-all | bytes 32768 | tf_op jit(solution)/shard_map/all_to_all | solution.py:536
  51.1 0.0 copy-done.7
  51.1 1.2 %finish.1 = (f32[32,3072]{1,0:T(8,128)}, f32[32,3072]{1,0:T(8,128)}, f32[32,3072]{1,0:T(8,128)}) custom-call(f32[16,1,256]{2,1,0:T(1,128)S(1)} %all_to_all.5.sums_ref, f32[32,3072]{1,0:T(8,128)S(1)} %copy-done.7, f32[32,3072]{1,0:T(8,128)S(1)} %copy-done.2, f32[32,3072]{1,0:T(8,128)S(1)} %copy-done, f32[32,3072]{1,0:T(8,128)S(1)} %get-tuple-element.16.a_ref), custom_call_target="tpu_custom_call" | custom-call | tf_op jit(solution)/shard_map/finish/pallas_call | solution.py:478
  (13 shorter events, 0.1 us)
Async XLA Ops:
  0.6 9.5 %copy-start = (f32[32,3072]{1,0:T(8,128)S(1)}, f32[32,3072]{1,0:T(8,128)}, u32[]{:S(2)}) copy-start(f32[32,3072]{1,0:T(8,128)} %d_ref.5) | copy-start | bytes 1179652
  0.6 9.5 %copy-start.9 = (s32[1,4]{1,0:T(1,128)S(1)}, s32[1,4]{1,0:T(1,128)}, u32[]{:S(2)}) copy-start(s32[1,4]{1,0:T(1,128)} %sizes_ref.13) | copy-start | bytes 52
  0.7 9.5 %copy-start.10 = (s32[3072]{0:T(1024)S(1)}, s32[3072]{0:T(1024)}, u32[]{:S(2)}) copy-start(s32[3072]{0:T(1024)} %param.18) | copy-start | bytes 36868
  0.7 9.5 %copy-start.8 = (f32[3,3072]{1,0:T(4,128)S(1)}, f32[3,3072]{1,0:T(4,128)}, u32[]{:S(2)}) copy-start(f32[3,3072]{1,0:T(4,128)} %coords_ref.1) | copy-start | bytes 110596
  3.8 1.4 %collective-permute-start = (f32[5,32,128]{2,1,0:T(8,128)S(1)}, f32[5,32,128]{2,1,0:T(8,128)S(1)}, u32[]{:S(2)}, u32[]{:S(2)}) collective-permute-start(f32[5,32,128]{2,1,0:T(8,128)S(1)} %get-tuple-element.11.after_ref.refs_0_), channel_id=1, source_target_pairs={{0,1},{1,0},{2,3},{3,2},{4,5},{5,4},{6,7},{7,6},{8,9},{9,8},{10,11... | collective-permute-start | bytes 245768 | tf_op jit(solution)/shard_map/ppermute | solution.py:490
  5.3 9.7 %collective-permute-start.1 = (f32[4,32,128]{2,1,0:T(8,128)S(1)}, f32[4,32,128]{2,1,0:T(8,128)S(1)}, u32[]{:S(2)}, u32[]{:S(2)}) collective-permute-start(f32[4,32,128]{2,1,0:T(8,128)S(1)} %slice.33.refs_1_), channel_id=1, source_target_pairs={{0,2},{1,3},{2,0},{3,1},{4,6},{5,7},{6,4},{7,5},{8,10},{9,11},{10,... | collective-permute-start | bytes 196616 | tf_op jit(solution)/shard_map/ppermute | solution.py:490
  15.0 5.9 %collective-permute-start.2 = (f32[3,32,128]{2,1,0:T(8,128)S(1)}, f32[3,32,128]{2,1,0:T(8,128)S(1)}, u32[]{:S(2)}, u32[]{:S(2)}) collective-permute-start(f32[3,32,128]{2,1,0:T(8,128)S(1)} %slice.35.refs_1_), channel_id=1, source_target_pairs={{0,4},{1,5},{2,6},{3,7},{4,0},{5,1},{6,2},{7,3},{8,12},{9,13},{10,... | collective-permute-start | bytes 147464 | tf_op jit(solution)/shard_map/ppermute | solution.py:490
  21.0 5.1 %collective-permute-start.3 = (f32[2,32,128]{2,1,0:T(8,128)S(1)}, f32[2,32,128]{2,1,0:T(8,128)S(1)}, u32[]{:S(2)}, u32[]{:S(2)}) collective-permute-start(f32[2,32,128]{2,1,0:T(8,128)S(1)} %slice.37.refs_1_), channel_id=1, source_target_pairs={{0,8},{1,9},{2,10},{3,11},{4,12},{5,13},{6,14},{7,15},{8,0},{9,1},... | collective-permute-start | bytes 98312 | tf_op jit(solution)/shard_map/ppermute | solution.py:490
  26.1 11.4 %collective-permute-start.4 = (f32[1,32,128]{2,1,0:T(8,128)S(1)}, f32[1,32,128]{2,1,0:T(8,128)S(1)}, u32[]{:S(2)}, u32[]{:S(2)}) collective-permute-start(f32[1,32,128]{2,1,0:T(8,128)S(1)} %slice.39.refs_1_), channel_id=1, source_target_pairs={{0,16},{1,17},{2,18},{3,19},{4,20},{5,21},{6,22},{7,23},{8,24},{9,... | collective-permute-start | bytes 49160 | tf_op jit(solution)/shard_map/ppermute | solution.py:490
  33.1 4.4 %copy-start.1 = (bf16[128,3072]{1,0:T(8,128)(2,1)S(1)}, bf16[128,3072]{1,0:T(8,128)(2,1)}, u32[]{:S(2)}) copy-start(bf16[128,3072]{1,0:T(8,128)(2,1)} %basis_ref.1) | copy-start | bytes 2359300
  33.1 4.4 %copy-start.2 = (f32[32,3072]{1,0:T(8,128)S(1)}, f32[32,3072]{1,0:T(8,128)}, u32[]{:S(2)}) copy-start(f32[32,3072]{1,0:T(8,128)} %r_ref.3) | copy-start | bytes 1179652
  33.1 4.4 %copy-start.3 = (bf16[1,7,128,128]{3,2,1,0:T(8,128)(2,1)S(1)}, bf16[1,7,128,128]{3,2,1,0:T(8,128)(2,1)}, u32[]{:S(2)}) copy-start(bf16[1,7,128,128]{3,2,1,0:T(8,128)(2,1)} %nt_ref.1) | copy-start | bytes 688132
  33.1 4.4 %copy-start.4 = (bf16[1,7,128,128]{3,2,1,0:T(8,128)(2,1)S(1)}, bf16[1,7,128,128]{3,2,1,0:T(8,128)(2,1)}, u32[]{:S(2)}) copy-start(bf16[1,7,128,128]{3,2,1,0:T(8,128)(2,1)} %nc_ref.1) | copy-start | bytes 688132
  33.1 4.4 %copy-start.5 = (bf16[1,4,128,128]{3,2,1,0:T(8,128)(2,1)S(1)}, bf16[1,4,128,128]{3,2,1,0:T(8,128)(2,1)}, u32[]{:S(2)}) copy-start(bf16[1,4,128,128]{3,2,1,0:T(8,128)(2,1)} %uc_ref.1) | copy-start | bytes 393220
  33.2 4.4 %copy-start.6 = (bf16[1,3,128,128]{3,2,1,0:T(8,128)(2,1)S(1)}, bf16[1,3,128,128]{3,2,1,0:T(8,128)(2,1)}, u32[]{:S(2)}) copy-start(bf16[1,3,128,128]{3,2,1,0:T(8,128)(2,1)} %ut_ref.1) | copy-start | bytes 294916
  37.6 13.5 %copy-start.7 = (f32[32,3072]{1,0:T(8,128)S(1)}, f32[32,3072]{1,0:T(8,128)}, u32[]{:S(2)}) copy-start(f32[32,3072]{1,0:T(8,128)} %x_ref.1) | copy-start | bytes 1179652
  39.9 1.2 %collective-permute-start.5 = (f32[1,1,256]{2,1,0:T(1,128)S(1)}, f32[1,1,256]{2,1,0:T(1,128)S(1)}, u32[]{:S(2)}, u32[]{:S(2)}) collective-permute-start(f32[1,1,256]{2,1,0:T(1,128)S(1)} %get-tuple-element.15.own_ref), channel_id=1, source_target_pairs={{0,1},{1,0},{2,3},{3,2},{4,5},{5,4},{6,7},{7,6},{8,9},{9,8},{10,11... | collective-permute-start | bytes 3080 | tf_op jit(solution)/shard_map/ppermute | solution.py:490

commit v6 on v4

--- a/solution.py
+++ b/solution.py
@@ -10,7 +10,7 @@
 
 F32 = jnp.float32
 BF16 = jnp.bfloat16
-TILE = 256
+TILE = 128
 FAR_AWAY = 32768.0
 LOG2E = 1.0 / math.log(2.0)
 POLY = math.log(2.0) ** 2 / 3.0
@@ -21,9 +21,9 @@
 SMEM = pl.BlockSpec(memory_space=pltpu.SMEM)
 ANY = pl.BlockSpec(memory_space=pl.ANY)
 HBM = pl.BlockSpec(memory_space=pltpu.HBM)
-STRIP = 512
-GROUP = 2
-PARTS = 5
+STRIP = 384
+GROUP = 8
+PARTS = 3
 PARAMS = pltpu.CompilerParams(vmem_limit_bytes=48 * 1024 * 1024)
 
 
@@ -149,6 +149,7 @@
     left_ref,
     right_ref,
     dd_ref,
+    plan_ref,
     ordered_ref,
 ):
     points = coords_ref.shape[1]
@@ -180,6 +181,7 @@
     n2 = (norm - n1).astype(BF16).astype(F32)
     n3 = norm - n1 - n2
     ends = leaf_ends(sizes_ref, leaf_count)
+    plan_ref[...] = near_plan(ends, points // TILE)
     leaf = leaf_row(ends, 0, (8, points))
     parts = jnp.where(row8 % 3 == 0, n1, jnp.where(row8 % 3 == 1, n2, n3))
     norm_left = jnp.where(row8 < 3, parts, jnp.where(row8 < 6, 1.0, 0.0))
@@ -213,9 +215,10 @@
             jax.ShapeDtypeStruct((points + STRIP, 128), BF16),
             jax.ShapeDtypeStruct((48, points), BF16),
             jax.ShapeDtypeStruct((points + TILE, 128), BF16),
+            jax.ShapeDtypeStruct((8, 128), jnp.int32),
         ),
         in_specs=[SMEM, VMEM, VMEM, VMEM, VMEM, ANY],
-        out_specs=(VMEM,) * 3,
+        out_specs=(VMEM,) * 4,
         scratch_shapes=[pltpu.VMEM((8, points), F32)],
         compiler_params=PARAMS,
         name="features",
@@ -239,34 +242,37 @@
     return begins, counts
 
 
-def near_kernel(leaf_count, part, sizes_ref, left_ref, right_ref, dd_ref, *refs):
+def near_plan(ends, tiles):
+    begins, counts = strip_spans(ends, tiles)
+    item = lax.broadcasted_iota(jnp.int32, (8, 128), 1)
+    first = 0
+    begin = jnp.zeros((8, 128), jnp.int32)
+    column = jnp.full((8, 128), tiles * TILE, jnp.int32)
+    for tile, (low, count) in enumerate(zip(begins, counts)):
+        inside = (item >= first) & (item < first + count)
+        begin = jnp.where(inside, low + (item - first) * STRIP, begin)
+        column = jnp.where(inside, tile * TILE, column)
+        first = first + count
+    groups = jnp.full((8, 128), lax.div(first + (GROUP - 1), GROUP), jnp.int32)
+    row = lax.broadcasted_iota(jnp.int32, (8, 128), 0)
+    return jnp.where(row == 0, begin, jnp.where(row == 1, column, groups))
+
+
+def near_kernel(part, plan_ref, left_ref, right_ref, dd_ref, *refs):
     out_ref = refs[-1]
-    ends = leaf_ends(sizes_ref, leaf_count)
-    tiles = right_ref.shape[1] // TILE
-    depth = right_ref.shape[0]
-    begins, counts = strip_spans(ends, tiles)
-    firsts = [0]
-    for count in counts:
-        firsts.append(firsts[-1] + count)
-    groups = lax.div(firsts[-1] + (GROUP - 1), GROUP)
-    offsets = [begin - first * STRIP for begin, first in zip(begins, firsts)]
+    depth, points = right_ref.shape
+    groups = plan_ref[2, 0]
     if part == 0:
         out_ref[...] = jnp.zeros_like(out_ref)
 
     def one_group(group, carry):
         for unit in range(GROUP):
             item = group * GROUP + unit
-            tile_at = 0
-            offset = offsets[0]
-            for tile in range(1, tiles):
-                inside = item >= firsts[tile]
-                tile_at = jnp.where(inside, tile, tile_at)
-                offset = jnp.where(inside, offsets[tile], offset)
-            spare = item >= firsts[-1]
-            begin = jnp.where(spare, 0, item * STRIP + offset)
+            begin = plan_ref[0, item]
+            column = plan_ref[1, item]
             rows = pl.ds(pl.multiple_of(begin, 128), STRIP)
-            columns = pl.ds(pl.multiple_of(tile_at * TILE, TILE), TILE)
-            source = pl.ds(pl.multiple_of(jnp.where(spare, tiles, tile_at) * TILE, TILE), TILE)
+            source = pl.ds(pl.multiple_of(column, TILE), TILE)
+            columns = pl.ds(pl.multiple_of(jnp.minimum(column, points - TILE), TILE), TILE)
             squared = jnp.dot(
                 left_ref[rows, :depth], right_ref[:, columns], preferred_element_type=F32
             )
@@ -275,12 +281,12 @@
             kernel = (squared + LINEAR * root + CONSTANT) * jnp.exp2(-root)
             high_part = kernel.astype(BF16)
             low_part = (kernel - high_part.astype(F32)).astype(BF16)
-            both = jnp.dot(
-                jnp.concatenate([high_part, low_part], axis=0),
-                dd_ref[source, :],
+            weights = dd_ref[source, :]
+            out_ref[rows, :] += jnp.dot(
+                jnp.concatenate([high_part, low_part], axis=1),
+                jnp.concatenate([weights, weights], axis=0),
                 preferred_element_type=F32,
             )
-            out_ref[rows, :] += folded(both)
         return carry
 
     lax.fori_loop(
@@ -288,18 +294,17 @@
     )
 
 
-def near_part(sizes, prepared, before, after, part):
-    leaf_count = sizes.shape[1]
-    left, right, dd = prepared
+def near_part(prepared, before, after, part):
+    left, right, dd, plan = prepared
     return pl.pallas_call(
-        functools.partial(near_kernel, leaf_count, part),
+        functools.partial(near_kernel, part),
         out_shape=jax.ShapeDtypeStruct(left.shape, F32),
         in_specs=[SMEM] + [VMEM] * (3 + len(before)) + [ANY],
         out_specs=VMEM,
         input_output_aliases={4: 0} if before else {},
         compiler_params=PARAMS,
         name="near_part",
-    )(sizes, left, right, dd, *before, after)
+    )(plan, left, right, dd, *before, after)
 
 
 def down_kernel(
@@ -425,14 +430,18 @@
     )
 
 
-def step_kernel(sums_ref, x_ref, r_ref, d_ref, a_ref, nx_ref, nr_ref, nd_ref):
-    probes = d_ref.shape[0]
-    sums, tops = sums_ref[:, :, :128], sums_ref[:, :, 128:]
+def merged(sums, probes):
+    values, tops = sums[:, :, :128], sums[:, :, 128:]
     top = jnp.max(tops, axis=0)
     ratio = tops / top
     quantity = lax.div(lax.broadcasted_iota(jnp.int32, (1, 1, 128), 2), probes)
     factor = jnp.where(quantity < 2, 1.0, jnp.where(quantity == 2, ratio, ratio * ratio))
-    total = jnp.sum(sums * factor, axis=0)
+    return jnp.sum(values * factor, axis=0), top
+
+
+def step_kernel(sums_ref, x_ref, r_ref, d_ref, a_ref, nx_ref, nr_ref, nd_ref):
+    probes = d_ref.shape[0]
+    total, top = merged(sums_ref[...], probes)
     lane = lax.broadcasted_iota(jnp.int32, (probes, 128), 1)
     probe = lax.broadcasted_iota(jnp.int32, (probes, 128), 0)
 
@@ -493,19 +502,26 @@
         (direction, leaf_basis, node_transfer, node_coupling, upper_transfer, upper_coupling),
         levels,
     )
-    prepared = features(leaf_sizes, lengthscale, coordinates, cluster_order, direction, up)
     sides = []
     near = ()
     current = up
-    for level in range(max(levels, PARTS)):
+    for level in range(max(levels, PARTS + 2)):
         if level < levels:
             incoming = from_partner(current, 2**level)
-        if level < PARTS:
-            near = (near_part(leaf_sizes, prepared, near, current, level),)
+        if level == 1:
+            prepared = features(
+                leaf_sizes, lengthscale, coordinates, cluster_order, direction, current
+            )
+        if 2 <= level < PARTS + 2:
+            near = (near_part(prepared, near, current, level - 2),)
         if level < levels:
             current = current + incoming
             sides.append(current[0])
             current = current[1:] if level + 1 < levels else current
+            if level == 1:
+                current, *prepared = lax.optimization_barrier((current, *prepared))
+            elif near and level < PARTS + 2:
+                current, *near = lax.optimization_barrier((current, *near))
     near = near[0]
     applied, sums = descend(
         leaf_sizes, noise_variance, outputscale, direction, residual, leaf_basis,

time: 46.7 us -> 46.2 us (0.989)
  Pallas kernels: 25.1 us -> 22.8 us
  starting transfers between devices: 8.3 us -> 9.29 us
  blocking collectives: 8.95 us -> 9.66 us
    pallas_call x5 -> x3, Pallas kernels: 17 us -> 14.7 us  [near_part(): pl.pallas_call(functools.partial(near_kernel, part), out_shape=jax.ShapeD...]
    ppermute x5, starting transfers between devices: 8.3 us -> 9.29 us  [from_partner(): return lax.ppermute(array, 'leaf', [(i, i ^ stride) for i in range(count)])]
    all_to_all x1, blocking collectives: 8.95 us -> 9.66 us  [shards(): gathered = lax.all_to_all(sums, 'leaf', 0, 0, tiled=True)]
  transfers between devices with their start and end apart: 5 -> 5, of which waited for: 2 -> 1; matrix products, arithmetic and copies ran while one was open for 0% -> 0% of each run, Pallas kernels for 40% -> 35%
where the time goes in v6:
time: 46.2 us; the launch traced here: 45.7 us
  Pallas kernels  22.8 us (49%)
  blocking collectives  9.66 us (21%)
  starting transfers between devices  9.29 us (20%)
  between operations  2.87 us (6%)
  waiting for transfers between devices  0.93 us (2%)
    pallas_call x3, Pallas kernels, near_part(): pl.pallas_call(functools.partial(near_kernel, part), out_shape=jax.ShapeD...  14.7 us
    all_to_all x1, blocking collectives, shards(): gathered = lax.all_to_all(sums, 'leaf', 0, 0, tiled=True)  9.66 us
    ppermute x5, starting transfers between devices, from_partner(): return lax.ppermute(array, 'leaf', [(i, i ^ stride) for i in range(count)])  9.29 us
    pallas_call x1, Pallas kernels, climb(): pl.pallas_call(functools.partial(up_kernel, leaf_count, levels), out_shap...  3.12 us
    pallas_call x1, Pallas kernels, descend(): pl.pallas_call(functools.partial(down_kernel, leaf_count, len(sides)), ou...  2.31 us
    pallas_call x1, Pallas kernels, features(): pl.pallas_call(functools.partial(features_kernel, leaf_count), out_shape=...  1.39 us
    pallas_call x1, Pallas kernels, finish(): pl.pallas_call(step_kernel, out_shape=(shape, shape, shape), in_specs=[VM...  1.27 us
    ppermute x5, waiting for transfers between devices, from_partner(): return lax.ppermute(array, 'leaf', [(i, i ^ stride) for i in range(count)])  0.93 us
  transfers between devices with their start and end apart: 5, of which 1 were waited for; matrix products, arithmetic and copies ran while one was open for 0% of the time, Pallas kernels for 35%

profile of v6, /device:TPU:0, one launch (start us, length us, event | category | flops | bytes accessed | tf_op | source)
XLA Modules:
  0.0 45.7 jit_solution(2175213604391188576)
XLA Ops:
  0.6 0.0 copy-start
  0.6 0.0 copy-start.10
  0.7 0.0 copy-start.9
  0.7 0.0 copy-start.8
  0.7 3.1 %climb.1 = (f32[5,32,128]{2,1,0:T(8,128)S(1)}, f32[3,32,128]{2,1,0:T(8,128)S(1)}) custom-call(s32[1,4]{1,0:T(1,128)} %sizes_ref.3, f32[32,3072]{1,0:T(8,128)} %d_ref.5, bf16[128,3072]{1,0:T(8,128)(2,1)} %basis_ref.1, bf16[1,7,128,128]{3,2,1,0:T(8,128)(2,1)} %nt_ref.1, bf16[1,7,128,128]{3,2,1,0:T(8,128)(2,1)} %nc_ref.1, bf16[1,3,128,128]{3,2,1,0:T(8,128)(2,1)} %ut_ref.1, ...), custom_call_target="tpu_custom_call" | custom-call | tf_op jit(solution)/shard_map/climb/pallas_call | solution.py:125
  3.8 0.5 %collective-permute-start = (f32[5,32,128]{2,1,0:T(8,128)S(1)}, f32[5,32,128]{2,1,0:T(8,128)S(1)}, u32[]{:S(2)}, u32[]{:S(2)}) collective-permute-start(f32[5,32,128]{2,1,0:T(8,128)S(1)} %get-tuple-element.22), channel_id=1, source_target_pairs={{0,1},{1,0},{2,3},{3,2},{4,5},{5,4},{6,7},{7,6},{8,9},{9,8},{10,11... | collective-permute-start | bytes 245768 | tf_op jit(solution)/shard_map/ppermute | solution.py:479
  4.3 0.9 %collective-permute-done = f32[5,32,128]{2,1,0:T(8,128)S(1)} collective-permute-done((f32[5,32,128]{2,1,0:T(8,128)S(1)}, f32[5,32,128]{2,1,0:T(8,128)S(1)}, u32[]{:S(2)}, u32[]{:S(2)}) %collective-permute-start) | collective-permute-done | bytes 81952 | tf_op jit(solution)/shard_map/ppermute | solution.py:479
  5.3 2.9 %collective-permute-start.1 = (f32[4,32,128]{2,1,0:T(8,128)S(1)}, f32[4,32,128]{2,1,0:T(8,128)S(1)}, u32[]{:S(2)}, u32[]{:S(2)}) collective-permute-start(f32[4,32,128]{2,1,0:T(8,128)S(1)} %slice.33.after_ref), channel_id=1, source_target_pairs={{0,2},{1,3},{2,0},{3,1},{4,6},{5,7},{6,4},{7,5},{8,10},{9,11},{10,... | collective-permute-start | bytes 196616 | tf_op jit(solution)/shard_map/ppermute | solution.py:479
  10.1 0.0 copy-done
  10.1 0.0 copy-done.10
  10.1 0.0 copy-done.9
  10.2 0.0 copy-done.8
  10.2 1.4 %features.1 = (bf16[3456,128]{1,0:T(8,128)(2,1)S(1)}, bf16[48,3072]{1,0:T(8,128)(2,1)S(1)}, bf16[3200,128]{1,0:T(8,128)(2,1)S(1)}, s32[8,128]{1,0:T(8,128)S(1)}) custom-call(s32[1,4]{1,0:T(1,128)S(1)} %copy-done.10, f32[1]{0:T(128)S(6)} %copy.21.length_ref, f32[3,3072]{1,0:T(4,128)S(1)} %copy-done.8, s32[24,128]{1,0:T(8,128)S(1)} %bitcast.11, ...), custom_call_target="tpu_custom_call" | custom-call | tf_op jit(solution)/shard_map/features/pallas_call | solution.py:212
  11.6 0.0 collective-permute-done.1
  11.6 1.6 %collective-permute-start.2 = (f32[3,32,128]{2,1,0:T(8,128)S(1)}, f32[3,32,128]{2,1,0:T(8,128)S(1)}, u32[]{:S(2)}, u32[]{:S(2)}) collective-permute-start(f32[3,32,128]{2,1,0:T(8,128)S(1)} %slice.35.refs_0_), channel_id=1, source_target_pairs={{0,4},{1,5},{2,6},{3,7},{4,0},{5,1},{6,2},{7,3},{8,12},{9,13},{10,... | collective-permute-start | bytes 147464 | tf_op jit(solution)/shard_map/ppermute | solution.py:479
  13.2 5.0 %near_part.3.refs_0_ = f32[3456,128]{1,0:T(8,128)S(1)} custom-call(s32[8,128]{1,0:T(8,128)S(1)} %get-tuple-element.28.plan_ref, bf16[3456,128]{1,0:T(8,128)(2,1)S(1)} %get-tuple-element.29.left_ref, bf16[48,3072]{1,0:T(8,128)(2,1)S(1)} %get-tuple-element.30.right_ref, bf16[3200,128]{1,0:T(8,128)(2,1)S(1)} %get-tuple-element.31.dd_ref, ...), custom_call_target="tpu_custom_call" | custom-call | tf_op jit(solution)/shard_map/near_part/pallas_call | solution.py:299
  18.2 0.0 collective-permute-done.2
  18.2 1.6 %collective-permute-start.3 = (f32[2,32,128]{2,1,0:T(8,128)S(1)}, f32[2,32,128]{2,1,0:T(8,128)S(1)}, u32[]{:S(2)}, u32[]{:S(2)}) collective-permute-start(f32[2,32,128]{2,1,0:T(8,128)S(1)} %slice.37.refs_1_), channel_id=1, source_target_pairs={{0,8},{1,9},{2,10},{3,11},{4,12},{5,13},{6,14},{7,15},{8,0},{9,1},... | collective-permute-start | bytes 98312 | tf_op jit(solution)/shard_map/ppermute | solution.py:479
  19.8 4.9 %near_part.4.refs_0_ = f32[3456,128]{1,0:T(8,128)S(1)} custom-call(s32[8,128]{1,0:T(8,128)S(1)} %get-tuple-element.28.plan_ref, bf16[3456,128]{1,0:T(8,128)(2,1)S(1)} %get-tuple-element.29.left_ref, bf16[48,3072]{1,0:T(8,128)(2,1)S(1)} %get-tuple-element.30.right_ref, ...), custom_call_target="tpu_custom_call", output_to_operand_aliasing={{}: (4, {})} | custom-call | tf_op jit(solution)/shard_map/near_part/pallas_call | solution.py:299
  24.7 0.0 collective-permute-done.3
  24.8 2.6 %collective-permute-start.4 = (f32[1,32,128]{2,1,0:T(8,128)S(1)}, f32[1,32,128]{2,1,0:T(8,128)S(1)}, u32[]{:S(2)}, u32[]{:S(2)}) collective-permute-start(f32[1,32,128]{2,1,0:T(8,128)S(1)} %get-tuple-element.34.refs_1_), channel_id=1, source_target_pairs={{0,16},{1,17},{2,18},{3,19},{4,20},{5,21},{6,22},{7,23},{8,24},{9,... | collective-permute-start | bytes 49160 | tf_op jit(solution)/shard_map/ppermute | solution.py:479
  27.4 0.0 copy-start.1
  27.4 0.0 copy-start.2
  27.4 0.0 copy-start.3
  27.4 0.0 copy-start.4
  27.4 0.0 copy-start.5
  27.5 0.0 copy-start.6
  27.5 4.9 %near_part.5.rest_5_ = f32[3456,128]{1,0:T(8,128)S(1)} custom-call(s32[8,128]{1,0:T(8,128)S(1)} %get-tuple-element.28.plan_ref, bf16[3456,128]{1,0:T(8,128)(2,1)S(1)} %get-tuple-element.29.left_ref, bf16[48,3072]{1,0:T(8,128)(2,1)S(1)} %get-tuple-element.30.right_ref, ...), custom_call_target="tpu_custom_call", output_to_operand_aliasing={{}: (4, {})} | custom-call | tf_op jit(solution)/shard_map/near_part/pallas_call | solution.py:299
  32.3 0.0 collective-permute-done.4
  32.4 0.0 copy-done.1
  32.4 0.0 copy-done.2
  32.4 0.0 copy-done.3
  32.4 0.0 copy-done.4
  32.4 0.0 copy-done.5
  32.4 0.0 copy-done.6
  32.4 0.0 copy-start.7
  32.4 2.3 %descend.1 = (f32[32,3072]{1,0:T(8,128)S(1)}, f32[32,1,256]{2,1,0:T(1,128)S(1)}) custom-call(s32[1,4]{1,0:T(1,128)S(1)} %copy-done.10, f32[1]{0:T(128)S(6)} %copy.23.noise_ref, f32[1]{0:T(128)S(6)} %copy.22.scale_ref, f32[32,3072]{1,0:T(8,128)S(1)} %copy-done, f32[32,3072]{1,0:T(8,128)S(1)} %copy-done.2, bf16[128,3072]{1,0:T(8,128)(2,1)S(1)} %copy-done.1, ...), custom_call_target="tpu_custom_call" | custom-call | tf_op jit(solution)/shard_map/descend/pallas_call | solution.py:417
  34.7 9.7 %all_to_all.5.sums_ref = f32[32,1,256]{2,1,0:T(1,128)S(1)} all-to-all(f32[32,1,256]{2,1,0:T(1,128)S(1)} %get-tuple-element.37), channel_id=1, replica_groups=mesh['leaf'=32] {'leaf'}, dimensions={0} | all-to-all | bytes 65536 | tf_op jit(solution)/shard_map/all_to_all | solution.py:530
  44.4 0.0 copy-done.7
  44.4 1.3 %finish.1 = (f32[32,3072]{1,0:T(8,128)}, f32[32,3072]{1,0:T(8,128)}, f32[32,3072]{1,0:T(8,128)}) custom-call(f32[32,1,256]{2,1,0:T(1,128)S(1)} %all_to_all.5.sums_ref, f32[32,3072]{1,0:T(8,128)S(1)} %copy-done.7, f32[32,3072]{1,0:T(8,128)S(1)} %copy-done.2, f32[32,3072]{1,0:T(8,128)S(1)} %copy-done, f32[32,3072]{1,0:T(8,128)S(1)} %get-tuple-element.38.a_ref), custom_call_target="tpu_custom_call" | custom-call | tf_op jit(solution)/shard_map/finish/pallas_call | solution.py:467
  (12 shorter events, 0.1 us)
Async XLA Ops:
  0.6 9.5 %copy-start = (f32[32,3072]{1,0:T(8,128)S(1)}, f32[32,3072]{1,0:T(8,128)}, u32[]{:S(2)}) copy-start(f32[32,3072]{1,0:T(8,128)} %d_ref.5) | copy-start | bytes 1179652
  0.6 9.5 %copy-start.10 = (s32[1,4]{1,0:T(1,128)S(1)}, s32[1,4]{1,0:T(1,128)}, u32[]{:S(2)}) copy-start(s32[1,4]{1,0:T(1,128)} %sizes_ref.3) | copy-start | bytes 52
  0.7 9.5 %copy-start.9 = (s32[3072]{0:T(1024)S(1)}, s32[3072]{0:T(1024)}, u32[]{:S(2)}) copy-start(s32[3072]{0:T(1024)} %param.18) | copy-start | bytes 36868
  0.7 9.5 %copy-start.8 = (f32[3,3072]{1,0:T(4,128)S(1)}, f32[3,3072]{1,0:T(4,128)}, u32[]{:S(2)}) copy-start(f32[3,3072]{1,0:T(4,128)} %coords_ref.1) | copy-start | bytes 110596
  3.8 1.4 %collective-permute-start = (f32[5,32,128]{2,1,0:T(8,128)S(1)}, f32[5,32,128]{2,1,0:T(8,128)S(1)}, u32[]{:S(2)}, u32[]{:S(2)}) collective-permute-start(f32[5,32,128]{2,1,0:T(8,128)S(1)} %get-tuple-element.22), channel_id=1, source_target_pairs={{0,1},{1,0},{2,3},{3,2},{4,5},{5,4},{6,7},{7,6},{8,9},{9,8},{10,11... | collective-permute-start | bytes 245768 | tf_op jit(solution)/shard_map/ppermute | solution.py:479
  5.3 6.3 %collective-permute-start.1 = (f32[4,32,128]{2,1,0:T(8,128)S(1)}, f32[4,32,128]{2,1,0:T(8,128)S(1)}, u32[]{:S(2)}, u32[]{:S(2)}) collective-permute-start(f32[4,32,128]{2,1,0:T(8,128)S(1)} %slice.33.after_ref), channel_id=1, source_target_pairs={{0,2},{1,3},{2,0},{3,1},{4,6},{5,7},{6,4},{7,5},{8,10},{9,11},{10,... | collective-permute-start | bytes 196616 | tf_op jit(solution)/shard_map/ppermute | solution.py:479
  11.6 6.6 %collective-permute-start.2 = (f32[3,32,128]{2,1,0:T(8,128)S(1)}, f32[3,32,128]{2,1,0:T(8,128)S(1)}, u32[]{:S(2)}, u32[]{:S(2)}) collective-permute-start(f32[3,32,128]{2,1,0:T(8,128)S(1)} %slice.35.refs_0_), channel_id=1, source_target_pairs={{0,4},{1,5},{2,6},{3,7},{4,0},{5,1},{6,2},{7,3},{8,12},{9,13},{10,... | collective-permute-start | bytes 147464 | tf_op jit(solution)/shard_map/ppermute | solution.py:479
  18.2 6.5 %collective-permute-start.3 = (f32[2,32,128]{2,1,0:T(8,128)S(1)}, f32[2,32,128]{2,1,0:T(8,128)S(1)}, u32[]{:S(2)}, u32[]{:S(2)}) collective-permute-start(f32[2,32,128]{2,1,0:T(8,128)S(1)} %slice.37.refs_1_), channel_id=1, source_target_pairs={{0,8},{1,9},{2,10},{3,11},{4,12},{5,13},{6,14},{7,15},{8,0},{9,1},... | collective-permute-start | bytes 98312 | tf_op jit(solution)/shard_map/ppermute | solution.py:479
  24.8 7.6 %collective-permute-start.4 = (f32[1,32,128]{2,1,0:T(8,128)S(1)}, f32[1,32,128]{2,1,0:T(8,128)S(1)}, u32[]{:S(2)}, u32[]{:S(2)}) collective-permute-start(f32[1,32,128]{2,1,0:T(8,128)S(1)} %get-tuple-element.34.refs_1_), channel_id=1, source_target_pairs={{0,16},{1,17},{2,18},{3,19},{4,20},{5,21},{6,22},{7,23},{8,24},{9,... | collective-permute-start | bytes 49160 | tf_op jit(solution)/shard_map/ppermute | solution.py:479
  27.4 4.9 %copy-start.1 = (bf16[128,3072]{1,0:T(8,128)(2,1)S(1)}, bf16[128,3072]{1,0:T(8,128)(2,1)}, u32[]{:S(2)}) copy-start(bf16[128,3072]{1,0:T(8,128)(2,1)} %basis_ref.1) | copy-start | bytes 2359300
  27.4 4.9 %copy-start.2 = (f32[32,3072]{1,0:T(8,128)S(1)}, f32[32,3072]{1,0:T(8,128)}, u32[]{:S(2)}) copy-start(f32[32,3072]{1,0:T(8,128)} %r_ref.3) | copy-start | bytes 1179652
  27.4 4.9 %copy-start.3 = (bf16[1,7,128,128]{3,2,1,0:T(8,128)(2,1)S(1)}, bf16[1,7,128,128]{3,2,1,0:T(8,128)(2,1)}, u32[]{:S(2)}) copy-start(bf16[1,7,128,128]{3,2,1,0:T(8,128)(2,1)} %nt_ref.1) | copy-start | bytes 688132
  27.4 5.0 %copy-start.4 = (bf16[1,7,128,128]{3,2,1,0:T(8,128)(2,1)S(1)}, bf16[1,7,128,128]{3,2,1,0:T(8,128)(2,1)}, u32[]{:S(2)}) copy-start(bf16[1,7,128,128]{3,2,1,0:T(8,128)(2,1)} %nc_ref.1) | copy-start | bytes 688132
  27.4 5.0 %copy-start.5 = (bf16[1,4,128,128]{3,2,1,0:T(8,128)(2,1)S(1)}, bf16[1,4,128,128]{3,2,1,0:T(8,128)(2,1)}, u32[]{:S(2)}) copy-start(bf16[1,4,128,128]{3,2,1,0:T(8,128)(2,1)} %uc_ref.1) | copy-start | bytes 393220
  27.5 4.9 %copy-start.6 = (bf16[1,3,128,128]{3,2,1,0:T(8,128)(2,1)S(1)}, bf16[1,3,128,128]{3,2,1,0:T(8,128)(2,1)}, u32[]{:S(2)}) copy-start(bf16[1,3,128,128]{3,2,1,0:T(8,128)(2,1)} %ut_ref.1) | copy-start | bytes 294916
  32.4 12.0 %copy-start.7 = (f32[32,3072]{1,0:T(8,128)S(1)}, f32[32,3072]{1,0:T(8,128)}, u32[]{:S(2)}) copy-start(f32[32,3072]{1,0:T(8,128)} %x_ref.1) | copy-start | bytes 1179652

commit v7 on v6

--- a/solution.py
+++ b/solution.py
@@ -10,7 +10,7 @@
 
 F32 = jnp.float32
 BF16 = jnp.bfloat16
-TILE = 128
+TILE = 256
 FAR_AWAY = 32768.0
 LOG2E = 1.0 / math.log(2.0)
 POLY = math.log(2.0) ** 2 / 3.0
@@ -22,8 +22,9 @@
 ANY = pl.BlockSpec(memory_space=pl.ANY)
 HBM = pl.BlockSpec(memory_space=pltpu.HBM)
 STRIP = 384
-GROUP = 8
+GROUP = 4
 PARTS = 3
+BLOCKS = 3
 PARAMS = pltpu.CompilerParams(vmem_limit_bytes=48 * 1024 * 1024)
 
 
@@ -70,26 +71,42 @@
 def up_kernel(leaf_count, levels, *refs):
     sources, (up_ref, local_ref) = refs[:7], refs[7:9]
     held, semaphores = refs[9:16], refs[16]
-    copies = [
-        pltpu.make_async_copy(source, target, semaphores.at[index])
-        for index, (source, target) in enumerate(zip(sources, held))
-    ]
-    for copy in copies:
-        copy.start()
-    for copy in copies:
-        copy.wait()
     sizes_ref, d_ref, basis_ref, nt_ref, nc_ref, ut_ref, uc_ref = held
     probes, points = d_ref.shape
+    block = points // BLOCKS
+
+    def copy(index, place, window=None):
+        source, target = sources[index], held[index]
+        if window is not None:
+            source, target = source.at[:, window], target.at[:, window]
+        return pltpu.make_async_copy(source, target, semaphores.at[place])
+
+    windows = [pl.ds(block * number, block) for number in range(BLOCKS)]
+    first = [copy(0, 0)]
+    blocks = [
+        [copy(1, 1 + 2 * number, window), copy(2, 2 + 2 * number, window)]
+        for number, window in enumerate(windows)
+    ]
+    others = [copy(index, 2 * BLOCKS + index - 2) for index in range(3, 7)]
+    for pending in first + sum(blocks, []) + others:
+        pending.start()
+    first[0].wait()
     ends = leaf_ends(sizes_ref, leaf_count)
-    split = halves(d_ref[...])
-    leaf = leaf_row(ends, 0, (2 * probes, points))
-    zero = jnp.zeros_like(split)
-    masked = jnp.concatenate(
-        [jnp.where(leaf == index, split, zero) for index in range(leaf_count)], axis=0
-    )
-    raw = lax.dot_general(
-        masked, basis_ref[...], (((1,), (1,)), ((), ())), preferred_element_type=F32
-    )
+    raw = jnp.zeros((2 * probes * leaf_count, basis_ref.shape[0]), F32)
+    for number, window in enumerate(windows):
+        for pending in blocks[number]:
+            pending.wait()
+        split = halves(d_ref[:, window])
+        leaf = leaf_row(ends, block * number, split.shape)
+        zero = jnp.zeros_like(split)
+        masked = jnp.concatenate(
+            [jnp.where(leaf == index, split, zero) for index in range(leaf_count)], axis=0
+        )
+        raw = raw + lax.dot_general(
+            masked, basis_ref[:, window], (((1,), (1,)), ((), ())), preferred_element_type=F32
+        )
+    for pending in others:
+        pending.wait()
     current = [
         folded(raw[2 * probes * index : 2 * probes * (index + 1)]) for index in range(leaf_count)
     ]
@@ -132,7 +149,7 @@
         out_specs=(VMEM, VMEM),
         scratch_shapes=[pltpu.SMEM(sizes.shape, sizes.dtype)]
         + [pltpu.VMEM(array.shape, array.dtype) for array in vectors]
-        + [pltpu.SemaphoreType.DMA((len(arrays),))],
+        + [pltpu.SemaphoreType.DMA((2 * BLOCKS + 5,))],
         compiler_params=PARAMS,
         name="climb",
     )(*(pltpu.with_memory_space_constraint(array, pltpu.HBM) for array in arrays))
@@ -141,7 +158,7 @@
 def features_kernel(
     leaf_count,
     sizes_ref,
-    length_ref,
+    scalars_ref,
     coords_ref,
     order_ref,
     d_ref,
@@ -171,7 +188,7 @@
                 place = 128 * (8 * group + row)
                 ordered_ref[axis : axis + 1, place : place + 128] = found[row : row + 1, :]
     row8 = lax.broadcasted_iota(jnp.int32, (8, points), 0)
-    scale = (math.sqrt(5.0) * LOG2E) / length_ref[...].reshape(1, 1)
+    scale = (math.sqrt(5.0) * LOG2E) / scalars_ref[0:1, 0:1]
     scaled = jnp.where(row8 < 3, (ordered_ref[...] - 0.5) * scale, 0.0)
     z1 = scaled.astype(BF16).astype(F32)
     z2 = (scaled - z1).astype(BF16).astype(F32)
@@ -206,7 +223,25 @@
     dd_ref[points:, :] = jnp.zeros((TILE, 128), BF16)
 
 
-def features(sizes, lengthscale, coordinates, order, direction, after):
+def scalars_kernel(length_ref, scale_ref, noise_ref, after_ref, out_ref):
+    row = lax.broadcasted_iota(jnp.int32, out_ref.shape, 0)
+    out_ref[...] = jnp.where(
+        row == 0, length_ref[0], jnp.where(row == 1, scale_ref[0], noise_ref[0])
+    )
+
+
+def spread_scalars(lengthscale, outputscale, noise_variance, after):
+    return pl.pallas_call(
+        scalars_kernel,
+        out_shape=jax.ShapeDtypeStruct((8, 128), F32),
+        in_specs=[SMEM, SMEM, SMEM, ANY],
+        out_specs=VMEM,
+        compiler_params=PARAMS,
+        name="spread_scalars",
+    )(lengthscale, outputscale, noise_variance, after)
+
+
+def features(sizes, scalars, coordinates, order, direction, after):
     leaf_count = sizes.shape[1]
     points = direction.shape[1]
     return pl.pallas_call(
@@ -222,7 +257,7 @@
         scratch_shapes=[pltpu.VMEM((8, points), F32)],
         compiler_params=PARAMS,
         name="features",
-    )(sizes, lengthscale, coordinates, order.reshape(-1, 128), direction, after)
+    )(sizes, scalars, coordinates, order.reshape(-1, 128), direction, after)
 
 
 def strip_spans(ends, tiles):
@@ -281,12 +316,12 @@
             kernel = (squared + LINEAR * root + CONSTANT) * jnp.exp2(-root)
             high_part = kernel.astype(BF16)
             low_part = (kernel - high_part.astype(F32)).astype(BF16)
-            weights = dd_ref[source, :]
-            out_ref[rows, :] += jnp.dot(
-                jnp.concatenate([high_part, low_part], axis=1),
-                jnp.concatenate([weights, weights], axis=0),
+            both = jnp.dot(
+                jnp.concatenate([high_part, low_part], axis=0),
+                dd_ref[source, :],
                 preferred_element_type=F32,
             )
+            out_ref[rows, :] += folded(both)
         return carry
 
     lax.fori_loop(
@@ -311,8 +346,7 @@
     leaf_count,
     levels,
     sizes_ref,
-    noise_ref,
-    scale_ref,
+    scalars_ref,
     d_ref,
     r_ref,
     basis_ref,
@@ -354,8 +388,8 @@
         current = following
     stacked = jnp.concatenate([halves(term) for term in current], axis=0)
     ends = leaf_ends(sizes_ref, leaf_count)
-    noise = noise_ref[...].reshape(1, 1)
-    near_scale = scale_ref[...].reshape(1, 1) * POLY
+    noise = scalars_ref[2:3, 0:1]
+    near_scale = scalars_ref[1:2, 0:1] * POLY
     width = 512
     peak = jnp.zeros((probes, 128), F32)
     old = jnp.zeros((probes, 128), F32)
@@ -409,7 +443,7 @@
 
 
 def descend(
-    sizes, noise, scale, direction, residual, basis, node_transfer, node_coupling,
+    sizes, scalars, direction, residual, basis, node_transfer, node_coupling,
     upper_transfer, upper_coupling, local, sides, near,
 ):
     leaf_count = sizes.shape[1]
@@ -420,12 +454,12 @@
             jax.ShapeDtypeStruct((probes, points), F32),
             jax.ShapeDtypeStruct((2 ** len(sides), 1, 256), F32),
         ),
-        in_specs=[SMEM] + [VMEM] * (11 + len(sides)),
+        in_specs=[SMEM] + [VMEM] * (10 + len(sides)),
         out_specs=(VMEM, VMEM),
         compiler_params=PARAMS,
         name="descend",
     )(
-        sizes, noise, scale, direction, residual, basis,
+        sizes, scalars, direction, residual, basis,
         node_transfer, node_coupling, upper_transfer, upper_coupling, local, *sides, near,
     )
 
@@ -508,9 +542,11 @@
     for level in range(max(levels, PARTS + 2)):
         if level < levels:
             incoming = from_partner(current, 2**level)
+        if level == 0:
+            scalars = spread_scalars(lengthscale, outputscale, noise_variance, current)
         if level == 1:
             prepared = features(
-                leaf_sizes, lengthscale, coordinates, cluster_order, direction, current
+                leaf_sizes, scalars, coordinates, cluster_order, direction, current
             )
         if 2 <= level < PARTS + 2:
             near = (near_part(prepared, near, current, level - 2),)
@@ -518,13 +554,15 @@
             current = current + incoming
             sides.append(current[0])
             current = current[1:] if level + 1 < levels else current
-            if level == 1:
+            if level == 0:
+                current, scalars = lax.optimization_barrier((current, scalars))
+            elif level == 1:
                 current, *prepared = lax.optimization_barrier((current, *prepared))
             elif near and level < PARTS + 2:
                 current, *near = lax.optimization_barrier((current, *near))
     near = near[0]
     applied, sums = descend(
-        leaf_sizes, noise_variance, outputscale, direction, residual, leaf_basis,
+        leaf_sizes, scalars, direction, residual, leaf_basis,
         node_transfer, node_coupling, upper_transfer, upper_coupling, local, sides, near,
     )
     gathered = lax.all_to_all(sums, "leaf", 0, 0, tiled=True)

time: 46.2 us -> 44.8 us (0.970)
  Pallas kernels: 22.8 us -> 22 us
  blocking collectives: 9.66 us -> 8.95 us
  waiting for transfers between devices: 0.93 us -> 1.46 us
    all_to_all x1, blocking collectives: 9.66 us -> 8.95 us  [shards(): gathered = lax.all_to_all(sums, 'leaf', 0, 0, tiled=True)]
    pallas_call x3, Pallas kernels: 14.7 us -> 14 us  [near_part(): pl.pallas_call(functools.partial(near_kernel, part), out_shape=jax.ShapeD...]
    ppermute x5, waiting for transfers between devices: 0.93 us -> 1.46 us  [from_partner(): return lax.ppermute(array, 'leaf', [(i, i ^ stride) for i in range(count)])]
  transfers between devices with their start and end apart: 5 -> 5, of which waited for: 1 -> 1; matrix products, arithmetic and copies ran while one was open for 0% -> 0% of each run, Pallas kernels for 35% -> 34%
where the time goes in v7:
time: 44.8 us; the launch traced here: 44.6 us
  Pallas kernels  22 us (49%)
  starting transfers between devices  9.23 us (21%)
  blocking collectives  8.95 us (20%)
  between operations  2.84 us (6%)
  waiting for transfers between devices  1.46 us (3%)
    pallas_call x3, Pallas kernels, near_part(): pl.pallas_call(functools.partial(near_kernel, part), out_shape=jax.ShapeD...  14 us
    ppermute x5, starting transfers between devices, from_partner(): return lax.ppermute(array, 'leaf', [(i, i ^ stride) for i in range(count)])  9.23 us
    all_to_all x1, blocking collectives, shards(): gathered = lax.all_to_all(sums, 'leaf', 0, 0, tiled=True)  8.95 us
    pallas_call x1, Pallas kernels, climb(): pl.pallas_call(functools.partial(up_kernel, leaf_count, levels), out_shap...  3.08 us
    pallas_call x1, Pallas kernels, descend(): pl.pallas_call(functools.partial(down_kernel, leaf_count, len(sides)), ou...  2.33 us
    ppermute x5, waiting for transfers between devices, from_partner(): return lax.ppermute(array, 'leaf', [(i, i ^ stride) for i in range(count)])  1.46 us
    pallas_call x1, Pallas kernels, features(): pl.pallas_call(functools.partial(features_kernel, leaf_count), out_shape=...  1.29 us
    pallas_call x1, Pallas kernels, finish(): pl.pallas_call(step_kernel, out_shape=(shape, shape, shape), in_specs=[VM...  1.27 us
  transfers between devices with their start and end apart: 5, of which 1 were waited for; matrix products, arithmetic and copies ran while one was open for 0% of the time, Pallas kernels for 34%

profile of v7, /device:TPU:0, one launch (start us, length us, event | category | flops | bytes accessed | tf_op | source)
XLA Modules:
  0.0 44.6 jit_solution(8429729978385394804)
XLA Ops:
  0.6 0.0 copy-start
  0.6 0.0 copy-start.10
  0.7 0.0 copy-start.9
  0.7 0.0 copy-start.8
  0.7 3.1 %climb.1 = (f32[5,32,128]{2,1,0:T(8,128)S(1)}, f32[3,32,128]{2,1,0:T(8,128)S(1)}) custom-call(s32[1,4]{1,0:T(1,128)} %sizes_ref.3, f32[32,3072]{1,0:T(8,128)} %d_ref.5, bf16[128,3072]{1,0:T(8,128)(2,1)} %basis_ref.1, bf16[1,7,128,128]{3,2,1,0:T(8,128)(2,1)} %nt_ref.1, bf16[1,7,128,128]{3,2,1,0:T(8,128)(2,1)} %nc_ref.1, bf16[1,3,128,128]{3,2,1,0:T(8,128)(2,1)} %ut_ref.1, ...), custom_call_target="tpu_custom_call" | custom-call | tf_op jit(solution)/shard_map/climb/pallas_call | solution.py:142
  3.8 0.5 %collective-permute-start = (f32[5,32,128]{2,1,0:T(8,128)S(1)}, f32[5,32,128]{2,1,0:T(8,128)S(1)}, u32[]{:S(2)}, u32[]{:S(2)}) collective-permute-start(f32[5,32,128]{2,1,0:T(8,128)S(1)} %get-tuple-element.23.after_ref), channel_id=1, source_target_pairs={{0,1},{1,0},{2,3},{3,2},{4,5},{5,4},{6,7},{7,6},{8,9},{9,8},{10,11... | collective-permute-start | bytes 245768 | tf_op jit(solution)/shard_map/ppermute | solution.py:513
  6.2 0.0 collective-permute-done
  6.3 2.6 %collective-permute-start.1 = (f32[4,32,128]{2,1,0:T(8,128)S(1)}, f32[4,32,128]{2,1,0:T(8,128)S(1)}, u32[]{:S(2)}, u32[]{:S(2)}) collective-permute-start(f32[4,32,128]{2,1,0:T(8,128)S(1)} %slice.32.after_ref), channel_id=1, source_target_pairs={{0,2},{1,3},{2,0},{3,1},{4,6},{5,7},{6,4},{7,5},{8,10},{9,11},{10,... | collective-permute-start | bytes 196616 | tf_op jit(solution)/shard_map/ppermute | solution.py:513
  8.8 0.0 copy-done
  8.8 0.0 copy-done.10
  8.8 0.0 copy-done.9
  8.8 0.0 copy-done.8
  8.9 1.3 %features.1 = (bf16[3456,128]{1,0:T(8,128)(2,1)S(1)}, bf16[48,3072]{1,0:T(8,128)(2,1)S(1)}, bf16[3328,128]{1,0:T(8,128)(2,1)S(1)}, s32[8,128]{1,0:T(8,128)S(1)}) custom-call(s32[1,4]{1,0:T(1,128)S(1)} %copy-done.10, f32[8,128]{1,0:T(8,128)S(1)} %spread_scalars.1.scalars_ref, f32[3,3072]{1,0:T(4,128)S(1)} %copy-done.8, s32[24,128]{1,0:T(8,128)S(1)} %bitcast.11, ...), custom_call_target="tpu_custom_call" | custom-call | tf_op jit(solution)/shard_map/features/pallas_call | solution.py:247
  10.2 1.4 %collective-permute-done.1 = f32[4,32,128]{2,1,0:T(8,128)S(1)} collective-permute-done((f32[4,32,128]{2,1,0:T(8,128)S(1)}, f32[4,32,128]{2,1,0:T(8,128)S(1)}, u32[]{:S(2)}, u32[]{:S(2)}) %collective-permute-start.1) | collective-permute-done | bytes 65568 | tf_op jit(solution)/shard_map/ppermute | solution.py:513
  11.6 1.8 %collective-permute-start.2 = (f32[3,32,128]{2,1,0:T(8,128)S(1)}, f32[3,32,128]{2,1,0:T(8,128)S(1)}, u32[]{:S(2)}, u32[]{:S(2)}) collective-permute-start(f32[3,32,128]{2,1,0:T(8,128)S(1)} %slice.35.refs_0_), channel_id=1, source_target_pairs={{0,4},{1,5},{2,6},{3,7},{4,0},{5,1},{6,2},{7,3},{8,12},{9,13},{10,... | collective-permute-start | bytes 147464 | tf_op jit(solution)/shard_map/ppermute | solution.py:513
  13.5 4.3 %near_part.3.refs_0_ = f32[3456,128]{1,0:T(8,128)S(1)} custom-call(s32[8,128]{1,0:T(8,128)S(1)} %get-tuple-element.32.plan_ref, bf16[3456,128]{1,0:T(8,128)(2,1)S(1)} %get-tuple-element.33.left_ref, bf16[48,3072]{1,0:T(8,128)(2,1)S(1)} %get-tuple-element.34.right_ref, bf16[3328,128]{1,0:T(8,128)(2,1)S(1)} %get-tuple-element.35.dd_ref, ...), custom_call_target="tpu_custom_call" | custom-call | tf_op jit(solution)/shard_map/near_part/pallas_call | solution.py:334
  17.8 0.0 collective-permute-done.2
  17.9 1.6 %collective-permute-start.3 = (f32[2,32,128]{2,1,0:T(8,128)S(1)}, f32[2,32,128]{2,1,0:T(8,128)S(1)}, u32[]{:S(2)}, u32[]{:S(2)}) collective-permute-start(f32[2,32,128]{2,1,0:T(8,128)S(1)} %slice.37.refs_1_), channel_id=1, source_target_pairs={{0,8},{1,9},{2,10},{3,11},{4,12},{5,13},{6,14},{7,15},{8,0},{9,1},... | collective-permute-start | bytes 98312 | tf_op jit(solution)/shard_map/ppermute | solution.py:513
  19.5 4.2 %near_part.4.refs_0_ = f32[3456,128]{1,0:T(8,128)S(1)} custom-call(s32[8,128]{1,0:T(8,128)S(1)} %get-tuple-element.32.plan_ref, bf16[3456,128]{1,0:T(8,128)(2,1)S(1)} %get-tuple-element.33.left_ref, bf16[48,3072]{1,0:T(8,128)(2,1)S(1)} %get-tuple-element.34.right_ref, ...), custom_call_target="tpu_custom_call", output_to_operand_aliasing={{}: (4, {})} | custom-call | tf_op jit(solution)/shard_map/near_part/pallas_call | solution.py:334
  23.7 0.0 collective-permute-done.3
  23.8 2.7 %collective-permute-start.4 = (f32[1,32,128]{2,1,0:T(8,128)S(1)}, f32[1,32,128]{2,1,0:T(8,128)S(1)}, u32[]{:S(2)}, u32[]{:S(2)}) collective-permute-start(f32[1,32,128]{2,1,0:T(8,128)S(1)} %get-tuple-element.38.refs_1_), channel_id=1, source_target_pairs={{0,16},{1,17},{2,18},{3,19},{4,20},{5,21},{6,22},{7,23},{8,24},{9,... | collective-permute-start | bytes 49160 | tf_op jit(solution)/shard_map/ppermute | solution.py:513
  26.4 0.0 copy-start.1
  26.4 0.0 copy-start.2
  26.5 0.0 copy-start.3
  26.5 0.0 copy-start.4
  26.5 0.0 copy-start.5
  26.5 0.0 copy-start.6
  26.5 5.5 %near_part.5.rest_5_ = f32[3456,128]{1,0:T(8,128)S(1)} custom-call(s32[8,128]{1,0:T(8,128)S(1)} %get-tuple-element.32.plan_ref, bf16[3456,128]{1,0:T(8,128)(2,1)S(1)} %get-tuple-element.33.left_ref, bf16[48,3072]{1,0:T(8,128)(2,1)S(1)} %get-tuple-element.34.right_ref, ...), custom_call_target="tpu_custom_call", output_to_operand_aliasing={{}: (4, {})} | custom-call | tf_op jit(solution)/shard_map/near_part/pallas_call | solution.py:334
  32.0 0.0 collective-permute-done.4
  32.0 0.0 copy-done.1
  32.0 0.0 copy-done.2
  32.0 0.0 copy-done.3
  32.0 0.0 copy-done.4
  32.0 0.0 copy-done.5
  32.0 0.0 copy-done.6
  32.0 0.0 copy-start.7
  32.1 2.3 %descend.1 = (f32[32,3072]{1,0:T(8,128)S(1)}, f32[32,1,256]{2,1,0:T(1,128)S(1)}) custom-call(s32[1,4]{1,0:T(1,128)S(1)} %copy-done.10, f32[8,128]{1,0:T(8,128)S(1)} %spread_scalars.1.scalars_ref, f32[32,3072]{1,0:T(8,128)S(1)} %copy-done, f32[32,3072]{1,0:T(8,128)S(1)} %copy-done.2, bf16[128,3072]{1,0:T(8,128)(2,1)S(1)} %copy-done.1, ...), custom_call_target="tpu_custom_call" | custom-call | tf_op jit(solution)/shard_map/descend/pallas_call | solution.py:451
  34.4 8.9 %all_to_all.5.sums_ref = f32[32,1,256]{2,1,0:T(1,128)S(1)} all-to-all(f32[32,1,256]{2,1,0:T(1,128)S(1)} %get-tuple-element.41), channel_id=1, replica_groups=mesh['leaf'=32] {'leaf'}, dimensions={0} | all-to-all | bytes 65536 | tf_op jit(solution)/shard_map/all_to_all | solution.py:568
  43.3 0.0 copy-done.7
  43.3 1.3 %finish.1 = (f32[32,3072]{1,0:T(8,128)}, f32[32,3072]{1,0:T(8,128)}, f32[32,3072]{1,0:T(8,128)}) custom-call(f32[32,1,256]{2,1,0:T(1,128)S(1)} %all_to_all.5.sums_ref, f32[32,3072]{1,0:T(8,128)S(1)} %copy-done.7, f32[32,3072]{1,0:T(8,128)S(1)} %copy-done.2, f32[32,3072]{1,0:T(8,128)S(1)} %copy-done, f32[32,3072]{1,0:T(8,128)S(1)} %get-tuple-element.42.a_ref), custom_call_target="tpu_custom_call" | custom-call | tf_op jit(solution)/shard_map/finish/pallas_call | solution.py:501
  (13 shorter events, 0.1 us)
Async XLA Ops:
  0.6 8.2 %copy-start = (f32[32,3072]{1,0:T(8,128)S(1)}, f32[32,3072]{1,0:T(8,128)}, u32[]{:S(2)}) copy-start(f32[32,3072]{1,0:T(8,128)} %d_ref.5) | copy-start | bytes 1179652
  0.6 8.2 %copy-start.10 = (s32[1,4]{1,0:T(1,128)S(1)}, s32[1,4]{1,0:T(1,128)}, u32[]{:S(2)}) copy-start(s32[1,4]{1,0:T(1,128)} %sizes_ref.3) | copy-start | bytes 52
  0.7 8.2 %copy-start.9 = (s32[3072]{0:T(1024)S(1)}, s32[3072]{0:T(1024)}, u32[]{:S(2)}) copy-start(s32[3072]{0:T(1024)} %param.18) | copy-start | bytes 36868
  0.7 8.2 %copy-start.8 = (f32[3,3072]{1,0:T(4,128)S(1)}, f32[3,3072]{1,0:T(4,128)}, u32[]{:S(2)}) copy-start(f32[3,3072]{1,0:T(4,128)} %coords_ref.1) | copy-start | bytes 110596
  3.8 2.5 %collective-permute-start = (f32[5,32,128]{2,1,0:T(8,128)S(1)}, f32[5,32,128]{2,1,0:T(8,128)S(1)}, u32[]{:S(2)}, u32[]{:S(2)}) collective-permute-start(f32[5,32,128]{2,1,0:T(8,128)S(1)} %get-tuple-element.23.after_ref), channel_id=1, source_target_pairs={{0,1},{1,0},{2,3},{3,2},{4,5},{5,4},{6,7},{7,6},{8,9},{9,8},{10,11... | collective-permute-start | bytes 245768 | tf_op jit(solution)/shard_map/ppermute | solution.py:513
  6.3 5.3 %collective-permute-start.1 = (f32[4,32,128]{2,1,0:T(8,128)S(1)}, f32[4,32,128]{2,1,0:T(8,128)S(1)}, u32[]{:S(2)}, u32[]{:S(2)}) collective-permute-start(f32[4,32,128]{2,1,0:T(8,128)S(1)} %slice.32.after_ref), channel_id=1, source_target_pairs={{0,2},{1,3},{2,0},{3,1},{4,6},{5,7},{6,4},{7,5},{8,10},{9,11},{10,... | collective-permute-start | bytes 196616 | tf_op jit(solution)/shard_map/ppermute | solution.py:513
  11.6 6.2 %collective-permute-start.2 = (f32[3,32,128]{2,1,0:T(8,128)S(1)}, f32[3,32,128]{2,1,0:T(8,128)S(1)}, u32[]{:S(2)}, u32[]{:S(2)}) collective-permute-start(f32[3,32,128]{2,1,0:T(8,128)S(1)} %slice.35.refs_0_), channel_id=1, source_target_pairs={{0,4},{1,5},{2,6},{3,7},{4,0},{5,1},{6,2},{7,3},{8,12},{9,13},{10,... | collective-permute-start | bytes 147464 | tf_op jit(solution)/shard_map/ppermute | solution.py:513
  17.9 5.9 %collective-permute-start.3 = (f32[2,32,128]{2,1,0:T(8,128)S(1)}, f32[2,32,128]{2,1,0:T(8,128)S(1)}, u32[]{:S(2)}, u32[]{:S(2)}) collective-permute-start(f32[2,32,128]{2,1,0:T(8,128)S(1)} %slice.37.refs_1_), channel_id=1, source_target_pairs={{0,8},{1,9},{2,10},{3,11},{4,12},{5,13},{6,14},{7,15},{8,0},{9,1},... | collective-permute-start | bytes 98312 | tf_op jit(solution)/shard_map/ppermute | solution.py:513
  23.8 8.2 %collective-permute-start.4 = (f32[1,32,128]{2,1,0:T(8,128)S(1)}, f32[1,32,128]{2,1,0:T(8,128)S(1)}, u32[]{:S(2)}, u32[]{:S(2)}) collective-permute-start(f32[1,32,128]{2,1,0:T(8,128)S(1)} %get-tuple-element.38.refs_1_), channel_id=1, source_target_pairs={{0,16},{1,17},{2,18},{3,19},{4,20},{5,21},{6,22},{7,23},{8,24},{9,... | collective-permute-start | bytes 49160 | tf_op jit(solution)/shard_map/ppermute | solution.py:513
  26.4 5.5 %copy-start.1 = (bf16[128,3072]{1,0:T(8,128)(2,1)S(1)}, bf16[128,3072]{1,0:T(8,128)(2,1)}, u32[]{:S(2)}) copy-start(bf16[128,3072]{1,0:T(8,128)(2,1)} %basis_ref.1) | copy-start | bytes 2359300
  26.4 5.5 %copy-start.2 = (f32[32,3072]{1,0:T(8,128)S(1)}, f32[32,3072]{1,0:T(8,128)}, u32[]{:S(2)}) copy-start(f32[32,3072]{1,0:T(8,128)} %r_ref.3) | copy-start | bytes 1179652
  26.5 5.6 %copy-start.3 = (bf16[1,7,128,128]{3,2,1,0:T(8,128)(2,1)S(1)}, bf16[1,7,128,128]{3,2,1,0:T(8,128)(2,1)}, u32[]{:S(2)}) copy-start(bf16[1,7,128,128]{3,2,1,0:T(8,128)(2,1)} %nt_ref.1) | copy-start | bytes 688132
  26.5 5.6 %copy-start.4 = (bf16[1,7,128,128]{3,2,1,0:T(8,128)(2,1)S(1)}, bf16[1,7,128,128]{3,2,1,0:T(8,128)(2,1)}, u32[]{:S(2)}) copy-start(bf16[1,7,128,128]{3,2,1,0:T(8,128)(2,1)} %nc_ref.1) | copy-start | bytes 688132
  26.5 5.6 %copy-start.5 = (bf16[1,4,128,128]{3,2,1,0:T(8,128)(2,1)S(1)}, bf16[1,4,128,128]{3,2,1,0:T(8,128)(2,1)}, u32[]{:S(2)}) copy-start(bf16[1,4,128,128]{3,2,1,0:T(8,128)(2,1)} %uc_ref.1) | copy-start | bytes 393220
  26.5 5.6 %copy-start.6 = (bf16[1,3,128,128]{3,2,1,0:T(8,128)(2,1)S(1)}, bf16[1,3,128,128]{3,2,1,0:T(8,128)(2,1)}, u32[]{:S(2)}) copy-start(bf16[1,3,128,128]{3,2,1,0:T(8,128)(2,1)} %ut_ref.1) | copy-start | bytes 294916
  32.0 11.3 %copy-start.7 = (f32[32,3072]{1,0:T(8,128)S(1)}, f32[32,3072]{1,0:T(8,128)}, u32[]{:S(2)}) copy-start(f32[32,3072]{1,0:T(8,128)} %x_ref.1) | copy-start | bytes 1179652

commit v8 on v7

--- a/solution.py
+++ b/solution.py
@@ -12,10 +12,8 @@
 BF16 = jnp.bfloat16
 TILE = 256
 FAR_AWAY = 32768.0
-LOG2E = 1.0 / math.log(2.0)
-POLY = math.log(2.0) ** 2 / 3.0
-LINEAR = 3.0 * LOG2E
-CONSTANT = 3.0 * LOG2E * LOG2E
+THIRD = 1.0 / 3.0
+DECAY = -3.0 / math.log(2.0)
 
 VMEM = pl.BlockSpec(memory_space=pltpu.VMEM)
 SMEM = pl.BlockSpec(memory_space=pltpu.SMEM)
@@ -49,6 +47,10 @@
             halves(x), generator, (((1,), (1,)), ((), ())), preferred_element_type=F32
         )
     )
+
+
+def lane_sums(x):
+    return sum(x[:, first : first + 128] for first in range(0, x.shape[1], 128))
 
 
 def leaf_ends(sizes_ref, leaf_count):
@@ -188,7 +190,7 @@
                 place = 128 * (8 * group + row)
                 ordered_ref[axis : axis + 1, place : place + 128] = found[row : row + 1, :]
     row8 = lax.broadcasted_iota(jnp.int32, (8, points), 0)
-    scale = (math.sqrt(5.0) * LOG2E) / scalars_ref[0:1, 0:1]
+    scale = (math.sqrt(5.0) / 3.0) / scalars_ref[0:1, 0:1]
     scaled = jnp.where(row8 < 3, (ordered_ref[...] - 0.5) * scale, 0.0)
     z1 = scaled.astype(BF16).astype(F32)
     z2 = (scaled - z1).astype(BF16).astype(F32)
@@ -313,7 +315,7 @@
             )
             squared = jnp.maximum(squared, 1e-12)
             root = squared * lax.rsqrt(squared)
-            kernel = (squared + LINEAR * root + CONSTANT) * jnp.exp2(-root)
+            kernel = (squared + root + THIRD) * jnp.exp2(root * DECAY)
             high_part = kernel.astype(BF16)
             low_part = (kernel - high_part.astype(F32)).astype(BF16)
             both = jnp.dot(
@@ -342,11 +344,40 @@
     )(plan, left, right, dd, *before, after)
 
 
+def assemble_kernel(scalars_ref, near_ref, d_ref, r_ref, after_ref, base_ref, old_ref):
+    probes, points = d_ref.shape
+    noise = scalars_ref[2:3, 0:1]
+    near_scale = scalars_ref[1:2, 0:1] * 3.0
+    old = jnp.zeros((probes, 128), F32)
+    for first in range(0, points, 512):
+        window = slice(first, first + 512)
+        near = folded(near_ref[window, :].T[: 2 * probes])
+        base_ref[:, window] = noise * d_ref[:, window] + near_scale * near
+        r = r_ref[:, window]
+        old = old + lane_sums(r * r)
+    old_ref[...] = old
+
+
+def assemble(scalars, near, direction, residual, after):
+    return pl.pallas_call(
+        assemble_kernel,
+        out_shape=(
+            jax.ShapeDtypeStruct(direction.shape, F32),
+            jax.ShapeDtypeStruct((direction.shape[0], 128), F32),
+        ),
+        in_specs=[VMEM] * 4 + [ANY],
+        out_specs=(VMEM, VMEM),
+        compiler_params=PARAMS,
+        name="assemble",
+    )(scalars, near, direction, residual, after)
+
+
 def down_kernel(
     leaf_count,
     levels,
     sizes_ref,
-    scalars_ref,
+    base_ref,
+    old_ref,
     d_ref,
     r_ref,
     basis_ref,
@@ -358,7 +389,7 @@
     *rest,
 ):
     side_refs = rest[:levels]
-    near_ref, a_ref, sums_ref = rest[levels:]
+    a_ref, sums_ref = rest[levels:]
     probes, points = d_ref.shape
     down = None
     for level in range(levels - 1, -1, -1):
@@ -388,15 +419,9 @@
         current = following
     stacked = jnp.concatenate([halves(term) for term in current], axis=0)
     ends = leaf_ends(sizes_ref, leaf_count)
-    noise = scalars_ref[2:3, 0:1]
-    near_scale = scalars_ref[1:2, 0:1] * POLY
     width = 512
     peak = jnp.zeros((probes, 128), F32)
-    old = jnp.zeros((probes, 128), F32)
     curve = jnp.zeros((probes, 128), F32)
-
-    def lanes(x):
-        return sum(x[:, 128 * i : 128 * i + 128] for i in range(width // 128))
 
     for first in range(0, points, width):
         far_all = jnp.dot(
@@ -408,24 +433,21 @@
             term = folded(far_all[2 * probes * index : 2 * probes * (index + 1)])
             far = jnp.where(leaf == index, term, far)
         d = d_ref[:, first : first + width]
-        r = r_ref[:, first : first + width]
-        near = folded(near_ref[first : first + width, :].T[: 2 * probes])
-        applied = noise * d + near_scale * near + far
+        applied = base_ref[:, first : first + width] + far
         a_ref[:, first : first + width] = applied
         size = jnp.abs(applied)
         for i in range(width // 128):
             peak = jnp.maximum(peak, size[:, 128 * i : 128 * i + 128])
-        old = old + lanes(r * r)
-        curve = curve + lanes(d * applied)
+        curve = curve + lane_sums(d * applied)
     top = jnp.maximum(jnp.max(peak, axis=1, keepdims=True), 1e-30)
     inverse = 1.0 / top
     cross = jnp.zeros((probes, 128), F32)
     square = jnp.zeros((probes, 128), F32)
     for first in range(0, points, width):
         unit = a_ref[:, first : first + width] * inverse
-        cross = cross + lanes(r_ref[:, first : first + width] * unit)
-        square = square + lanes(unit * unit)
-    columns = [jnp.sum(x, axis=1, keepdims=True) for x in (old, curve, cross, square)]
+        cross = cross + lane_sums(r_ref[:, first : first + width] * unit)
+        square = square + lane_sums(unit * unit)
+    columns = [jnp.sum(x, axis=1, keepdims=True) for x in (old_ref[...], curve, cross, square)]
     lane = lax.broadcasted_iota(jnp.int32, (probes, 128), 1)
     quantity = lax.div(lane, probes)
     own = lax.rem(lane, probes) == lax.broadcasted_iota(jnp.int32, (probes, 128), 0)
@@ -443,8 +465,8 @@
 
 
 def descend(
-    sizes, scalars, direction, residual, basis, node_transfer, node_coupling,
-    upper_transfer, upper_coupling, local, sides, near,
+    sizes, base, old, direction, residual, basis, node_transfer, node_coupling,
+    upper_transfer, upper_coupling, local, sides,
 ):
     leaf_count = sizes.shape[1]
     probes, points = direction.shape
@@ -459,8 +481,8 @@
         compiler_params=PARAMS,
         name="descend",
     )(
-        sizes, scalars, direction, residual, basis,
-        node_transfer, node_coupling, upper_transfer, upper_coupling, local, *sides, near,
+        sizes, base, old, direction, residual, basis,
+        node_transfer, node_coupling, upper_transfer, upper_coupling, local, *sides,
     )
 
 
@@ -548,22 +570,23 @@
             prepared = features(
                 leaf_sizes, scalars, coordinates, cluster_order, direction, current
             )
-        if 2 <= level < PARTS + 2:
-            near = (near_part(prepared, near, current, level - 2),)
+        if 1 <= level <= PARTS:
+            near = (near_part(prepared, near, current, level - 1),)
+        if level == PARTS + 1:
+            base, old = assemble(scalars, near[0], direction, residual, current)
         if level < levels:
             current = current + incoming
             sides.append(current[0])
             current = current[1:] if level + 1 < levels else current
             if level == 0:
                 current, scalars = lax.optimization_barrier((current, scalars))
-            elif level == 1:
-                current, *prepared = lax.optimization_barrier((current, *prepared))
-            elif near and level < PARTS + 2:
+            elif level <= PARTS:
                 current, *near = lax.optimization_barrier((current, *near))
-    near = near[0]
+            elif level == PARTS + 1:
+                current, base, old = lax.optimization_barrier((current, base, old))
     applied, sums = descend(
-        leaf_sizes, scalars, direction, residual, leaf_basis,
-        node_transfer, node_coupling, upper_transfer, upper_coupling, local, sides, near,
+        leaf_sizes, base, old, direction, residual, leaf_basis,
+        node_transfer, node_coupling, upper_transfer, upper_coupling, local, sides,
     )
     gathered = lax.all_to_all(sums, "leaf", 0, 0, tiled=True)
     return finish(gathered, solution, residual, direction, applied)

time: 44.8 us -> 45.5 us (1.016)
  Pallas kernels: 22 us -> 20.6 us
  blocking collectives: 8.95 us -> 10.3 us
  starting transfers between devices: 9.23 us -> 10.1 us
    pallas_call x3, Pallas kernels: 14 us -> 12.2 us  [near_part(): pl.pallas_call(functools.partial(near_kernel, part), out_shape=jax.ShapeD...]
    all_to_all x1, blocking collectives: 8.95 us -> 10.3 us  [shards(): gathered = lax.all_to_all(sums, 'leaf', 0, 0, tiled=True)]
    ppermute x5, starting transfers between devices: 9.23 us -> 10.1 us  [from_partner(): return lax.ppermute(array, 'leaf', [(i, i ^ stride) for i in range(count)])]
    pallas_call x0 -> x1, Pallas kernels: none -> 0.46 us  [assemble(): pl.pallas_call(assemble_kernel, out_shape=(jax.ShapeDtypeStruct(direction...]
  transfers between devices with their start and end apart: 5 -> 5, of which waited for: 1 -> 1; matrix products, arithmetic and copies ran while one was open for 0% -> 0% of each run, Pallas kernels for 34% -> 31%
where the time goes in v8:
time: 45.5 us; the launch traced here: 45.3 us
  Pallas kernels  20.6 us (45%)
  blocking collectives  10.3 us (23%)
  starting transfers between devices  10.1 us (22%)
  between operations  2.84 us (6%)
  waiting for transfers between devices  1.24 us (3%)
    pallas_call x3, Pallas kernels, near_part(): pl.pallas_call(functools.partial(near_kernel, part), out_shape=jax.ShapeD...  12.2 us
    all_to_all x1, blocking collectives, shards(): gathered = lax.all_to_all(sums, 'leaf', 0, 0, tiled=True)  10.3 us
    ppermute x5, starting transfers between devices, from_partner(): return lax.ppermute(array, 'leaf', [(i, i ^ stride) for i in range(count)])  10.1 us
    pallas_call x1, Pallas kernels, climb(): pl.pallas_call(functools.partial(up_kernel, leaf_count, levels), out_shap...  3.08 us
    pallas_call x1, Pallas kernels, descend(): pl.pallas_call(functools.partial(down_kernel, leaf_count, len(sides)), ou...  2.26 us
    pallas_call x1, Pallas kernels, features(): pl.pallas_call(functools.partial(features_kernel, leaf_count), out_shape=...  1.29 us
    pallas_call x1, Pallas kernels, finish(): pl.pallas_call(step_kernel, out_shape=(shape, shape, shape), in_specs=[VM...  1.27 us
    ppermute x5, waiting for transfers between devices, from_partner(): return lax.ppermute(array, 'leaf', [(i, i ^ stride) for i in range(count)])  1.24 us
  transfers between devices with their start and end apart: 5, of which 1 were waited for; matrix products, arithmetic and copies ran while one was open for 0% of the time, Pallas kernels for 31%

profile of v8, /device:TPU:0, one launch (start us, length us, event | category | flops | bytes accessed | tf_op | source)
XLA Modules:
  0.0 45.3 jit_solution(2086144462900427074)
XLA Ops:
  0.6 0.0 copy-start
  0.6 0.0 copy-start.10
  0.7 0.0 copy-start.9
  0.7 0.0 copy-start.8
  0.7 3.1 %climb.1 = (f32[5,32,128]{2,1,0:T(8,128)S(1)}, f32[3,32,128]{2,1,0:T(8,128)S(1)}) custom-call(s32[1,4]{1,0:T(1,128)} %sizes_ref.3, f32[32,3072]{1,0:T(8,128)} %d_ref.7, bf16[128,3072]{1,0:T(8,128)(2,1)} %basis_ref.1, bf16[1,7,128,128]{3,2,1,0:T(8,128)(2,1)} %nt_ref.1, bf16[1,7,128,128]{3,2,1,0:T(8,128)(2,1)} %nc_ref.1, bf16[1,3,128,128]{3,2,1,0:T(8,128)(2,1)} %ut_ref.1, ...), custom_call_target="tpu_custom_call" | custom-call | tf_op jit(solution)/shard_map/climb/pallas_call | solution.py:144
  3.8 0.5 %collective-permute-start = (f32[5,32,128]{2,1,0:T(8,128)S(1)}, f32[5,32,128]{2,1,0:T(8,128)S(1)}, u32[]{:S(2)}, u32[]{:S(2)}) collective-permute-start(f32[5,32,128]{2,1,0:T(8,128)S(1)} %get-tuple-element.23.after_ref), channel_id=1, source_target_pairs={{0,1},{1,0},{2,3},{3,2},{4,5},{5,4},{6,7},{7,6},{8,9},{9,8},{10,11... | collective-permute-start | bytes 245768 | tf_op jit(solution)/shard_map/ppermute | solution.py:535
  6.2 0.0 collective-permute-done
  6.3 2.6 %collective-permute-start.1 = (f32[4,32,128]{2,1,0:T(8,128)S(1)}, f32[4,32,128]{2,1,0:T(8,128)S(1)}, u32[]{:S(2)}, u32[]{:S(2)}) collective-permute-start(f32[4,32,128]{2,1,0:T(8,128)S(1)} %slice.32.after_ref.refs_0_), channel_id=1, source_target_pairs={{0,2},{1,3},{2,0},{3,1},{4,6},{5,7},{6,4},{7,5},{8,10},{9,11},{10,... | collective-permute-start | bytes 196616 | tf_op jit(solution)/shard_map/ppermute | solution.py:535
  8.8 0.0 copy-done
  8.8 0.0 copy-done.10
  8.8 0.0 copy-done.9
  8.8 0.0 copy-done.8
  8.9 1.3 %features.1 = (bf16[3456,128]{1,0:T(8,128)(2,1)S(1)}, bf16[48,3072]{1,0:T(8,128)(2,1)S(1)}, bf16[3328,128]{1,0:T(8,128)(2,1)S(1)}, s32[8,128]{1,0:T(8,128)S(1)}) custom-call(s32[1,4]{1,0:T(1,128)S(1)} %copy-done.10, f32[8,128]{1,0:T(8,128)S(1)} %spread_scalars.1.scalars_ref, f32[3,3072]{1,0:T(4,128)S(1)} %copy-done.8, s32[24,128]{1,0:T(8,128)S(1)} %bitcast.11, ...), custom_call_target="tpu_custom_call" | custom-call | tf_op jit(solution)/shard_map/features/pallas_call | solution.py:249
  10.2 4.1 %near_part.3.refs_0_ = f32[3456,128]{1,0:T(8,128)S(1)} custom-call(s32[8,128]{1,0:T(8,128)S(1)} %get-tuple-element.26.plan_ref, bf16[3456,128]{1,0:T(8,128)(2,1)S(1)} %get-tuple-element.27.left_ref, bf16[48,3072]{1,0:T(8,128)(2,1)S(1)} %get-tuple-element.28.right_ref, bf16[3328,128]{1,0:T(8,128)(2,1)S(1)} %get-tuple-element.29.dd_ref, ...), custom_call_target="tpu_custom_call" | custom-call | tf_op jit(solution)/shard_map/near_part/pallas_call | solution.py:336
  14.3 0.0 collective-permute-done.1
  14.3 1.6 %collective-permute-start.2 = (f32[3,32,128]{2,1,0:T(8,128)S(1)}, f32[3,32,128]{2,1,0:T(8,128)S(1)}, u32[]{:S(2)}, u32[]{:S(2)}) collective-permute-start(f32[3,32,128]{2,1,0:T(8,128)S(1)} %slice.33.refs_1_), channel_id=1, source_target_pairs={{0,4},{1,5},{2,6},{3,7},{4,0},{5,1},{6,2},{7,3},{8,12},{9,13},{10,... | collective-permute-start | bytes 147464 | tf_op jit(solution)/shard_map/ppermute | solution.py:535
  15.9 4.0 %near_part.4.refs_0_ = f32[3456,128]{1,0:T(8,128)S(1)} custom-call(s32[8,128]{1,0:T(8,128)S(1)} %get-tuple-element.26.plan_ref, bf16[3456,128]{1,0:T(8,128)(2,1)S(1)} %get-tuple-element.27.left_ref, bf16[48,3072]{1,0:T(8,128)(2,1)S(1)} %get-tuple-element.28.right_ref, ...), custom_call_target="tpu_custom_call", output_to_operand_aliasing={{}: (4, {})} | custom-call | tf_op jit(solution)/shard_map/near_part/pallas_call | solution.py:336
  20.0 0.0 collective-permute-done.2
  20.0 1.6 %collective-permute-start.3 = (f32[2,32,128]{2,1,0:T(8,128)S(1)}, f32[2,32,128]{2,1,0:T(8,128)S(1)}, u32[]{:S(2)}, u32[]{:S(2)}) collective-permute-start(f32[2,32,128]{2,1,0:T(8,128)S(1)} %slice.34.refs_1_), channel_id=1, source_target_pairs={{0,8},{1,9},{2,10},{3,11},{4,12},{5,13},{6,14},{7,15},{8,0},{9,1},... | collective-permute-start | bytes 98312 | tf_op jit(solution)/shard_map/ppermute | solution.py:535
  21.7 0.0 copy-start.1
  21.7 4.0 %near_part.5.near_ref = f32[3456,128]{1,0:T(8,128)S(1)} custom-call(s32[8,128]{1,0:T(8,128)S(1)} %get-tuple-element.26.plan_ref, bf16[3456,128]{1,0:T(8,128)(2,1)S(1)} %get-tuple-element.27.left_ref, bf16[48,3072]{1,0:T(8,128)(2,1)S(1)} %get-tuple-element.28.right_ref, ...), custom_call_target="tpu_custom_call", output_to_operand_aliasing={{}: (4, {})} | custom-call | tf_op jit(solution)/shard_map/near_part/pallas_call | solution.py:336
  25.7 0.0 copy-start.2
  25.7 0.0 copy-start.3
  25.7 0.0 copy-start.4
  25.8 0.0 copy-start.5
  25.8 0.0 copy-start.6
  25.8 0.0 collective-permute-done.3
  25.8 3.8 %collective-permute-start.4 = (f32[1,32,128]{2,1,0:T(8,128)S(1)}, f32[1,32,128]{2,1,0:T(8,128)S(1)}, u32[]{:S(2)}, u32[]{:S(2)}) collective-permute-start(f32[1,32,128]{2,1,0:T(8,128)S(1)} %get-tuple-element.34.after_ref), channel_id=1, source_target_pairs={{0,16},{1,17},{2,18},{3,19},{4,20},{5,21},{6,22},{7,23},{8,24},{9,... | collective-permute-start | bytes 49160 | tf_op jit(solution)/shard_map/ppermute | solution.py:535
  29.6 0.0 copy-done.1
  29.6 0.5 %assemble.1 = (f32[32,3072]{1,0:T(8,128)S(1)}, f32[32,128]{1,0:T(8,128)S(1)}) custom-call(f32[8,128]{1,0:T(8,128)S(1)} %spread_scalars.1.scalars_ref, f32[3456,128]{1,0:T(8,128)S(1)} %near_part.5.near_ref, f32[32,3072]{1,0:T(8,128)S(1)} %copy-done, f32[32,3072]{1,0:T(8,128)S(1)} %copy-done.1, f32[1,32,128]{2,1,0:T(8,128)S(1)} %get-tuple-element.34.after_ref), custom_call_target="tpu_custom_call" | custom-call | tf_op jit(solution)/shard_map/assemble/pallas_call | solution.py:362
  30.1 0.0 copy-start.7
  30.1 1.2 %collective-permute-done.4 = f32[1,32,128]{2,1,0:T(8,128)S(1)} collective-permute-done((f32[1,32,128]{2,1,0:T(8,128)S(1)}, f32[1,32,128]{2,1,0:T(8,128)S(1)}, u32[]{:S(2)}, u32[]{:S(2)}) %collective-permute-start.4) | collective-permute-done | bytes 16416 | tf_op jit(solution)/shard_map/ppermute | solution.py:535
  31.3 0.0 copy-done.2
  31.3 0.0 copy-done.3
  31.3 0.0 copy-done.4
  31.3 0.0 copy-done.5
  31.4 0.0 copy-done.6
  31.4 2.3 %descend.1 = (f32[32,3072]{1,0:T(8,128)S(1)}, f32[32,1,256]{2,1,0:T(1,128)S(1)}) custom-call(s32[1,4]{1,0:T(1,128)S(1)} %copy-done.10, f32[32,3072]{1,0:T(8,128)S(1)} %get-tuple-element.38.base_ref, f32[32,128]{1,0:T(8,128)S(1)} %get-tuple-element.39.old_ref, f32[32,3072]{1,0:T(8,128)S(1)} %copy-done, f32[32,3072]{1,0:T(8,128)S(1)} %copy-done.1, ...), custom_call_target="tpu_custom_call" | custom-call | tf_op jit(solution)/shard_map/descend/pallas_call | solution.py:473
  33.6 10.3 %all_to_all.5.sums_ref = f32[32,1,256]{2,1,0:T(1,128)S(1)} all-to-all(f32[32,1,256]{2,1,0:T(1,128)S(1)} %get-tuple-element.41), channel_id=1, replica_groups=mesh['leaf'=32] {'leaf'}, dimensions={0} | all-to-all | bytes 65536 | tf_op jit(solution)/shard_map/all_to_all | solution.py:591
  44.0 0.0 copy-done.7
  44.0 1.3 %finish.1 = (f32[32,3072]{1,0:T(8,128)}, f32[32,3072]{1,0:T(8,128)}, f32[32,3072]{1,0:T(8,128)}) custom-call(f32[32,1,256]{2,1,0:T(1,128)S(1)} %all_to_all.5.sums_ref, f32[32,3072]{1,0:T(8,128)S(1)} %copy-done.7, f32[32,3072]{1,0:T(8,128)S(1)} %copy-done.1, f32[32,3072]{1,0:T(8,128)S(1)} %copy-done, f32[32,3072]{1,0:T(8,128)S(1)} %get-tuple-element.42.a_ref), custom_call_target="tpu_custom_call" | custom-call | tf_op jit(solution)/shard_map/finish/pallas_call | solution.py:523
  (13 shorter events, 0.1 us)
Async XLA Ops:
  0.6 8.2 %copy-start = (f32[32,3072]{1,0:T(8,128)S(1)}, f32[32,3072]{1,0:T(8,128)}, u32[]{:S(2)}) copy-start(f32[32,3072]{1,0:T(8,128)} %d_ref.7) | copy-start | bytes 1179652
  0.6 8.2 %copy-start.10 = (s32[1,4]{1,0:T(1,128)S(1)}, s32[1,4]{1,0:T(1,128)}, u32[]{:S(2)}) copy-start(s32[1,4]{1,0:T(1,128)} %sizes_ref.3) | copy-start | bytes 52
  0.7 8.2 %copy-start.9 = (s32[3072]{0:T(1024)S(1)}, s32[3072]{0:T(1024)}, u32[]{:S(2)}) copy-start(s32[3072]{0:T(1024)} %param.18) | copy-start | bytes 36868
  0.7 8.2 %copy-start.8 = (f32[3,3072]{1,0:T(4,128)S(1)}, f32[3,3072]{1,0:T(4,128)}, u32[]{:S(2)}) copy-start(f32[3,3072]{1,0:T(4,128)} %coords_ref.1) | copy-start | bytes 110596
  3.8 2.5 %collective-permute-start = (f32[5,32,128]{2,1,0:T(8,128)S(1)}, f32[5,32,128]{2,1,0:T(8,128)S(1)}, u32[]{:S(2)}, u32[]{:S(2)}) collective-permute-start(f32[5,32,128]{2,1,0:T(8,128)S(1)} %get-tuple-element.23.after_ref), channel_id=1, source_target_pairs={{0,1},{1,0},{2,3},{3,2},{4,5},{5,4},{6,7},{7,6},{8,9},{9,8},{10,11... | collective-permute-start | bytes 245768 | tf_op jit(solution)/shard_map/ppermute | solution.py:535
  6.3 8.0 %collective-permute-start.1 = (f32[4,32,128]{2,1,0:T(8,128)S(1)}, f32[4,32,128]{2,1,0:T(8,128)S(1)}, u32[]{:S(2)}, u32[]{:S(2)}) collective-permute-start(f32[4,32,128]{2,1,0:T(8,128)S(1)} %slice.32.after_ref.refs_0_), channel_id=1, source_target_pairs={{0,2},{1,3},{2,0},{3,1},{4,6},{5,7},{6,4},{7,5},{8,10},{9,11},{10,... | collective-permute-start | bytes 196616 | tf_op jit(solution)/shard_map/ppermute | solution.py:535
  14.3 5.6 %collective-permute-start.2 = (f32[3,32,128]{2,1,0:T(8,128)S(1)}, f32[3,32,128]{2,1,0:T(8,128)S(1)}, u32[]{:S(2)}, u32[]{:S(2)}) collective-permute-start(f32[3,32,128]{2,1,0:T(8,128)S(1)} %slice.33.refs_1_), channel_id=1, source_target_pairs={{0,4},{1,5},{2,6},{3,7},{4,0},{5,1},{6,2},{7,3},{8,12},{9,13},{10,... | collective-permute-start | bytes 147464 | tf_op jit(solution)/shard_map/ppermute | solution.py:535
  20.0 5.7 %collective-permute-start.3 = (f32[2,32,128]{2,1,0:T(8,128)S(1)}, f32[2,32,128]{2,1,0:T(8,128)S(1)}, u32[]{:S(2)}, u32[]{:S(2)}) collective-permute-start(f32[2,32,128]{2,1,0:T(8,128)S(1)} %slice.34.refs_1_), channel_id=1, source_target_pairs={{0,8},{1,9},{2,10},{3,11},{4,12},{5,13},{6,14},{7,15},{8,0},{9,1},... | collective-permute-start | bytes 98312 | tf_op jit(solution)/shard_map/ppermute | solution.py:535
  21.7 7.9 %copy-start.1 = (f32[32,3072]{1,0:T(8,128)S(1)}, f32[32,3072]{1,0:T(8,128)}, u32[]{:S(2)}) copy-start(f32[32,3072]{1,0:T(8,128)} %r_ref.5) | copy-start | bytes 1179652
  25.7 5.6 %copy-start.2 = (bf16[128,3072]{1,0:T(8,128)(2,1)S(1)}, bf16[128,3072]{1,0:T(8,128)(2,1)}, u32[]{:S(2)}) copy-start(bf16[128,3072]{1,0:T(8,128)(2,1)} %basis_ref.1) | copy-start | bytes 2359300
  25.7 5.6 %copy-start.3 = (bf16[1,7,128,128]{3,2,1,0:T(8,128)(2,1)S(1)}, bf16[1,7,128,128]{3,2,1,0:T(8,128)(2,1)}, u32[]{:S(2)}) copy-start(bf16[1,7,128,128]{3,2,1,0:T(8,128)(2,1)} %nt_ref.1) | copy-start | bytes 688132
  25.7 5.6 %copy-start.4 = (bf16[1,7,128,128]{3,2,1,0:T(8,128)(2,1)S(1)}, bf16[1,7,128,128]{3,2,1,0:T(8,128)(2,1)}, u32[]{:S(2)}) copy-start(bf16[1,7,128,128]{3,2,1,0:T(8,128)(2,1)} %nc_ref.1) | copy-start | bytes 688132
  25.8 5.6 %copy-start.5 = (bf16[1,4,128,128]{3,2,1,0:T(8,128)(2,1)S(1)}, bf16[1,4,128,128]{3,2,1,0:T(8,128)(2,1)}, u32[]{:S(2)}) copy-start(bf16[1,4,128,128]{3,2,1,0:T(8,128)(2,1)} %uc_ref.1) | copy-start | bytes 393220
  25.8 5.6 %copy-start.6 = (bf16[1,3,128,128]{3,2,1,0:T(8,128)(2,1)S(1)}, bf16[1,3,128,128]{3,2,1,0:T(8,128)(2,1)}, u32[]{:S(2)}) copy-start(bf16[1,3,128,128]{3,2,1,0:T(8,128)(2,1)} %ut_ref.1) | copy-start | bytes 294916
  25.8 5.5 %collective-permute-start.4 = (f32[1,32,128]{2,1,0:T(8,128)S(1)}, f32[1,32,128]{2,1,0:T(8,128)S(1)}, u32[]{:S(2)}, u32[]{:S(2)}) collective-permute-start(f32[1,32,128]{2,1,0:T(8,128)S(1)} %get-tuple-element.34.after_ref), channel_id=1, source_target_pairs={{0,16},{1,17},{2,18},{3,19},{4,20},{5,21},{6,22},{7,23},{8,24},{9,... | collective-permute-start | bytes 49160 | tf_op jit(solution)/shard_map/ppermute | solution.py:535
  30.1 13.9 %copy-start.7 = (f32[32,3072]{1,0:T(8,128)S(1)}, f32[32,3072]{1,0:T(8,128)}, u32[]{:S(2)}) copy-start(f32[32,3072]{1,0:T(8,128)} %x_ref.1) | copy-start | bytes 1179652

commit v9 on v8

--- a/solution.py
+++ b/solution.py
@@ -21,7 +21,7 @@
 HBM = pl.BlockSpec(memory_space=pltpu.HBM)
 STRIP = 384
 GROUP = 4
-PARTS = 3
+PARTS = 4
 BLOCKS = 3
 PARAMS = pltpu.CompilerParams(vmem_limit_bytes=48 * 1024 * 1024)
 
@@ -71,8 +71,8 @@
 
 
 def up_kernel(leaf_count, levels, *refs):
-    sources, (up_ref, local_ref) = refs[:7], refs[7:9]
-    held, semaphores = refs[9:16], refs[16]
+    sources, (up_ref, local_ref, high_ref, low_ref) = refs[:7], refs[7:11]
+    held, semaphores = refs[11:18], refs[18]
     sizes_ref, d_ref, basis_ref, nt_ref, nc_ref, ut_ref, uc_ref = held
     probes, points = d_ref.shape
     block = points // BLOCKS
@@ -90,8 +90,26 @@
         for number, window in enumerate(windows)
     ]
     others = [copy(index, 2 * BLOCKS + index - 2) for index in range(3, 7)]
-    for pending in first + sum(blocks, []) + others:
+    for pending in others + first + sum(blocks, []):
         pending.start()
+    for pending in others:
+        pending.wait()
+    rank = basis_ref.shape[0]
+    images = [nc_ref[0, 0].astype(F32)]
+    path = nt_ref[0, 0].astype(F32)
+    for level in range(1, levels):
+        if level + 1 < levels:
+            both = jnp.concatenate([ut_ref[0, level - 1], uc_ref[0, level - 1]], axis=1)
+            image = times(path, both)
+            path = image[:, :rank]
+            images.append(image[:, rank:])
+        else:
+            images.append(times(path, uc_ref[0, level - 1]))
+    images = jnp.concatenate(images, axis=1)
+    high = images.astype(BF16)
+    low = (images - high.astype(F32)).astype(BF16)
+    high_ref[...] = high
+    low_ref[...] = low
     first[0].wait()
     ends = leaf_ends(sizes_ref, leaf_count)
     raw = jnp.zeros((2 * probes * leaf_count, basis_ref.shape[0]), F32)
@@ -107,12 +125,9 @@
         raw = raw + lax.dot_general(
             masked, basis_ref[:, window], (((1,), (1,)), ((), ())), preferred_element_type=F32
         )
-    for pending in others:
-        pending.wait()
     current = [
         folded(raw[2 * probes * index : 2 * probes * (index + 1)]) for index in range(leaf_count)
     ]
-    rank = basis_ref.shape[0]
     while len(current) > 1:
         count = len(current)
         raised, sided = [], []
@@ -125,16 +140,9 @@
         current = [raised[2 * i] + raised[2 * i + 1] for i in range(count // 2)]
         for i in range(count // 2):
             local_ref[count // 2 - 1 + i] = sided[2 * i] + sided[2 * i + 1]
-    coefficient = current[0]
+    image = times(current[0], high) + times(current[0], low)
     for level in range(levels):
-        coupling = nc_ref[0, 0] if level == 0 else uc_ref[0, level - 1]
-        if level + 1 < levels:
-            transfer = nt_ref[0, 0] if level == 0 else ut_ref[0, level - 1]
-            image = times(coefficient, jnp.concatenate([transfer, coupling], axis=1))
-            coefficient = image[:, :rank]
-            up_ref[level] = image[:, rank:]
-        else:
-            up_ref[level] = times(coefficient, coupling)
+        up_ref[level] = image[:, rank * level : rank * (level + 1)]
 
 
 def climb(sizes, vectors, levels):
@@ -146,9 +154,11 @@
         out_shape=(
             jax.ShapeDtypeStruct((levels, probes, rank), F32),
             jax.ShapeDtypeStruct((leaf_count - 1, probes, rank), F32),
+            jax.ShapeDtypeStruct((rank, rank * levels), BF16),
+            jax.ShapeDtypeStruct((rank, rank * levels), BF16),
         ),
         in_specs=[HBM] * len(arrays),
-        out_specs=(VMEM, VMEM),
+        out_specs=(VMEM,) * 4,
         scratch_shapes=[pltpu.SMEM(sizes.shape, sizes.dtype)]
         + [pltpu.VMEM(array.shape, array.dtype) for array in vectors]
         + [pltpu.SemaphoreType.DMA((2 * BLOCKS + 5,))],
@@ -170,6 +180,8 @@
     dd_ref,
     plan_ref,
     ordered_ref,
+    list_ref,
+    semaphore,
 ):
     points = coords_ref.shape[1]
     chunks = points // 128
@@ -200,7 +212,9 @@
     n2 = (norm - n1).astype(BF16).astype(F32)
     n3 = norm - n1 - n2
     ends = leaf_ends(sizes_ref, leaf_count)
-    plan_ref[...] = near_plan(ends, points // TILE)
+    list_ref[...] = near_plan(ends, points // TILE)
+    handed = pltpu.make_async_copy(list_ref, plan_ref, semaphore.at[0])
+    handed.start()
     leaf = leaf_row(ends, 0, (8, points))
     parts = jnp.where(row8 % 3 == 0, n1, jnp.where(row8 % 3 == 1, n2, n3))
     norm_left = jnp.where(row8 < 3, parts, jnp.where(row8 < 6, 1.0, 0.0))
@@ -223,6 +237,7 @@
     split = jnp.concatenate([split, jnp.zeros((128 - split.shape[0], points), F32)], axis=0)
     dd_ref[:points, :] = split.T.astype(BF16)
     dd_ref[points:, :] = jnp.zeros((TILE, 128), BF16)
+    handed.wait()
 
 
 def scalars_kernel(length_ref, scale_ref, noise_ref, after_ref, out_ref):
@@ -252,11 +267,15 @@
             jax.ShapeDtypeStruct((points + STRIP, 128), BF16),
             jax.ShapeDtypeStruct((48, points), BF16),
             jax.ShapeDtypeStruct((points + TILE, 128), BF16),
-            jax.ShapeDtypeStruct((8, 128), jnp.int32),
+            pltpu.SMEM((8, 128), jnp.int32),
         ),
         in_specs=[SMEM, VMEM, VMEM, VMEM, VMEM, ANY],
-        out_specs=(VMEM,) * 4,
-        scratch_shapes=[pltpu.VMEM((8, points), F32)],
+        out_specs=(VMEM, VMEM, VMEM, SMEM),
+        scratch_shapes=[
+            pltpu.VMEM((8, points), F32),
+            pltpu.VMEM((8, 128), jnp.int32),
+            pltpu.SemaphoreType.DMA((1,)),
+        ],
         compiler_params=PARAMS,
         name="features",
     )(sizes, scalars, coordinates, order.reshape(-1, 128), direction, after)
@@ -333,6 +352,7 @@
 
 def near_part(prepared, before, after, part):
     left, right, dd, plan = prepared
+    plan = pltpu.with_memory_space_constraint(plan, pltpu.SMEM)
     return pl.pallas_call(
         functools.partial(near_kernel, part),
         out_shape=jax.ShapeDtypeStruct(left.shape, F32),
@@ -383,26 +403,16 @@
     basis_ref,
     nt_ref,
     nc_ref,
-    ut_ref,
-    uc_ref,
+    high_ref,
+    low_ref,
     local_ref,
     *rest,
 ):
     side_refs = rest[:levels]
     a_ref, sums_ref = rest[levels:]
     probes, points = d_ref.shape
-    down = None
-    for level in range(levels - 1, -1, -1):
-        coupling = nc_ref[0, 0] if level == 0 else uc_ref[0, level - 1]
-        side = side_refs[level][...]
-        if down is None:
-            down = times_transposed(side, coupling)
-        else:
-            transfer = nt_ref[0, 0] if level == 0 else ut_ref[0, level - 1]
-            down = times_transposed(
-                jnp.concatenate([down, side], axis=1),
-                jnp.concatenate([transfer, coupling], axis=1),
-            )
+    wide = jnp.concatenate([side_ref[...] for side_ref in side_refs], axis=1)
+    down = times_transposed(wide, high_ref[...]) + times_transposed(wide, low_ref[...])
     current = [down]
     while len(current) < leaf_count:
         count = len(current)
@@ -466,7 +476,7 @@
 
 def descend(
     sizes, base, old, direction, residual, basis, node_transfer, node_coupling,
-    upper_transfer, upper_coupling, local, sides,
+    images, local, sides,
 ):
     leaf_count = sizes.shape[1]
     probes, points = direction.shape
@@ -482,7 +492,7 @@
         name="descend",
     )(
         sizes, base, old, direction, residual, basis,
-        node_transfer, node_coupling, upper_transfer, upper_coupling, local, *sides,
+        node_transfer, node_coupling, *images, local, *sides,
     )
 
 
@@ -553,7 +563,7 @@
 ):
     levels = lax.axis_size("leaf").bit_length() - 1
     probes, points = direction.shape
-    up, local = climb(
+    up, local, *images = climb(
         leaf_sizes,
         (direction, leaf_basis, node_transfer, node_coupling, upper_transfer, upper_coupling),
         levels,
@@ -561,7 +571,7 @@
     sides = []
     near = ()
     current = up
-    for level in range(max(levels, PARTS + 2)):
+    for level in range(max(levels, PARTS + 1)):
         if level < levels:
             incoming = from_partner(current, 2**level)
         if level == 0:
@@ -572,8 +582,6 @@
             )
         if 1 <= level <= PARTS:
             near = (near_part(prepared, near, current, level - 1),)
-        if level == PARTS + 1:
-            base, old = assemble(scalars, near[0], direction, residual, current)
         if level < levels:
             current = current + incoming
             sides.append(current[0])
@@ -582,11 +590,10 @@
                 current, scalars = lax.optimization_barrier((current, scalars))
             elif level <= PARTS:
                 current, *near = lax.optimization_barrier((current, *near))
-            elif level == PARTS + 1:
-                current, base, old = lax.optimization_barrier((current, base, old))
+    base, old = assemble(scalars, near[0], direction, residual, near[0])
     applied, sums = descend(
         leaf_sizes, base, old, direction, residual, leaf_basis,
-        node_transfer, node_coupling, upper_transfer, upper_coupling, local, sides,
+        node_transfer, node_coupling, images, local, sides,
     )
     gathered = lax.all_to_all(sums, "leaf", 0, 0, tiled=True)
     return finish(gathered, solution, residual, direction, applied)

time: 45.5 us -> 43 us (0.945)
  starting transfers between devices: 10.1 us -> 7.2 us
  local copies, waits for them, and re-layouts: 0.09 us -> 0.79 us
    ppermute x5, starting transfers between devices: 10.1 us -> 7.2 us  [from_partner(): return lax.ppermute(array, 'leaf', [(i, i ^ stride) for i in range(count)])]
    pallas_call x3 -> x4, Pallas kernels: 12.2 us -> 11.5 us  [near_part(): pl.pallas_call(functools.partial(near_kernel, part), out_shape=jax.ShapeD...]
    unnamed x22 -> x18, local copies, waits for them, and re-layouts: 0.06 us -> 0.77 us
    pallas_call x1, Pallas kernels: 1.29 us -> 1.96 us  [features(): pl.pallas_call(functools.partial(features_kernel, leaf_count), out_shape=...]
where the time goes in v9:
time: 43 us; the launch traced here: 42.8 us
  Pallas kernels  20.4 us (47%)
  blocking collectives  10.6 us (25%)
  starting transfers between devices  7.2 us (17%)
  between operations  2.81 us (7%)
  waiting for transfers between devices  0.94 us (2%)
  local copies, waits for them, and re-layouts  0.79 us (2%)
    pallas_call x4, Pallas kernels, near_part(): pl.pallas_call(functools.partial(near_kernel, part), out_shape=jax.ShapeD...  11.5 us
    all_to_all x1, blocking collectives, shards(): gathered = lax.all_to_all(sums, 'leaf', 0, 0, tiled=True)  10.6 us
    ppermute x5, starting transfers between devices, from_partner(): return lax.ppermute(array, 'leaf', [(i, i ^ stride) for i in range(count)])  7.2 us
    pallas_call x1, Pallas kernels, climb(): pl.pallas_call(functools.partial(up_kernel, leaf_count, levels), out_shap...  3.32 us
    pallas_call x1, Pallas kernels, features(): pl.pallas_call(functools.partial(features_kernel, leaf_count), out_shape=...  1.96 us
    pallas_call x1, Pallas kernels, descend(): pl.pallas_call(functools.partial(down_kernel, leaf_count, len(sides)), ou...  1.86 us
    pallas_call x1, Pallas kernels, finish(): pl.pallas_call(step_kernel, out_shape=(shape, shape, shape), in_specs=[VM...  1.28 us
    ppermute x5, waiting for transfers between devices, from_partner(): return lax.ppermute(array, 'leaf', [(i, i ^ stride) for i in range(count)])  0.94 us
  transfers between devices with their start and end apart: 5, of which 1 were waited for; matrix products, arithmetic and copies ran while one was open for 0% of the time, Pallas kernels for 31%

profile of v9, /device:TPU:0, one launch (start us, length us, event | category | flops | bytes accessed | tf_op | source)
XLA Modules:
  0.0 42.8 jit_solution(7837612510069400441)
XLA Ops:
  0.6 0.0 copy-start
  0.6 0.0 copy-start.8
  0.7 0.0 copy-start.7
  0.7 0.0 copy-start.6
  0.7 3.3 %climb.1 = (f32[5,32,128]{2,1,0:T(8,128)S(1)}, f32[3,32,128]{2,1,0:T(8,128)S(1)}, bf16[128,640]{1,0:T(8,128)(2,1)S(1)}, bf16[128,640]{1,0:T(8,128)(2,1)S(1)}) custom-call(s32[1,4]{1,0:T(1,128)} %sizes_ref.3, f32[32,3072]{1,0:T(8,128)} %d_ref.7, bf16[128,3072]{1,0:T(8,128)(2,1)} %basis_ref.1, bf16[1,7,128,128]{3,2,1,0:T(8,128)(2,1)} %nt_ref.1, ...), custom_call_target="tpu_custom_call" | custom-call | tf_op jit(solution)/shard_map/climb/pallas_call | solution.py:152
  4.0 0.5 %collective-permute-start = (f32[5,32,128]{2,1,0:T(8,128)S(1)}, f32[5,32,128]{2,1,0:T(8,128)S(1)}, u32[]{:S(2)}, u32[]{:S(2)}) collective-permute-start(f32[5,32,128]{2,1,0:T(8,128)S(1)} %get-tuple-element.24.after_ref), channel_id=1, source_target_pairs={{0,1},{1,0},{2,3},{3,2},{4,5},{5,4},{6,7},{7,6},{8,9},{9,8},{10,11... | collective-permute-start | bytes 245768 | tf_op jit(solution)/shard_map/ppermute | solution.py:545
  6.5 0.0 collective-permute-done
  6.5 2.6 %collective-permute-start.1 = (f32[4,32,128]{2,1,0:T(8,128)S(1)}, f32[4,32,128]{2,1,0:T(8,128)S(1)}, u32[]{:S(2)}, u32[]{:S(2)}) collective-permute-start(f32[4,32,128]{2,1,0:T(8,128)S(1)} %slice.32.after_ref.refs_0_), channel_id=1, source_target_pairs={{0,2},{1,3},{2,0},{3,1},{4,6},{5,7},{6,4},{7,5},{8,10},{9,11},{10,... | collective-permute-start | bytes 196616 | tf_op jit(solution)/shard_map/ppermute | solution.py:545
  9.1 0.0 copy-done
  9.1 0.0 copy-done.8
  9.1 0.0 copy-done.7
  9.1 0.0 copy-done.6
  9.1 2.0 %features.1 = (bf16[3456,128]{1,0:T(8,128)(2,1)S(1)}, bf16[48,3072]{1,0:T(8,128)(2,1)S(1)}, bf16[3328,128]{1,0:T(8,128)(2,1)S(1)}, s32[8,128]{1,0:T(8,128)S(4)}) custom-call(s32[1,4]{1,0:T(1,128)S(1)} %copy-done.8, f32[8,128]{1,0:T(8,128)S(1)} %spread_scalars.1.scalars_ref, f32[3,3072]{1,0:T(4,128)S(1)} %copy-done.6, s32[24,128]{1,0:T(8,128)S(1)} %bitcast.11, ...), custom_call_target="tpu_custom_call" | custom-call | tf_op jit(solution)/shard_map/features/pallas_call | solution.py:264
  11.1 2.4 %near_part.4.refs_0_ = f32[3456,128]{1,0:T(8,128)S(1)} custom-call(s32[8,128]{1,0:T(8,128)S(4)} %get-tuple-element.27.plan_ref, bf16[3456,128]{1,0:T(8,128)(2,1)S(1)} %get-tuple-element.28.left_ref, bf16[48,3072]{1,0:T(8,128)(2,1)S(1)} %get-tuple-element.29.right_ref, bf16[3328,128]{1,0:T(8,128)(2,1)S(1)} %get-tuple-element.30.dd_ref, ...), custom_call_target="tpu_custom_call" | custom-call | tf_op jit(solution)/shard_map/near_part/pallas_call | solution.py:356
  13.5 0.0 collective-permute-done.1
  13.5 1.6 %collective-permute-start.2 = (f32[3,32,128]{2,1,0:T(8,128)S(1)}, f32[3,32,128]{2,1,0:T(8,128)S(1)}, u32[]{:S(2)}, u32[]{:S(2)}) collective-permute-start(f32[3,32,128]{2,1,0:T(8,128)S(1)} %slice.33.refs_1_), channel_id=1, source_target_pairs={{0,4},{1,5},{2,6},{3,7},{4,0},{5,1},{6,2},{7,3},{8,12},{9,13},{10,... | collective-permute-start | bytes 147464 | tf_op jit(solution)/shard_map/ppermute | solution.py:545
  15.1 3.4 %near_part.5.refs_0_ = f32[3456,128]{1,0:T(8,128)S(1)} custom-call(s32[8,128]{1,0:T(8,128)S(4)} %get-tuple-element.27.plan_ref, bf16[3456,128]{1,0:T(8,128)(2,1)S(1)} %get-tuple-element.28.left_ref, bf16[48,3072]{1,0:T(8,128)(2,1)S(1)} %get-tuple-element.29.right_ref, ...), custom_call_target="tpu_custom_call", output_to_operand_aliasing={{}: (4, {})} | custom-call | tf_op jit(solution)/shard_map/near_part/pallas_call | solution.py:356
  18.5 0.0 collective-permute-done.2
  18.6 0.8 %collective-permute-start.3 = (f32[2,32,128]{2,1,0:T(8,128)S(1)}, f32[2,32,128]{2,1,0:T(8,128)S(1)}, u32[]{:S(2)}, u32[]{:S(2)}) collective-permute-start(f32[2,32,128]{2,1,0:T(8,128)S(1)} %slice.34.refs_1_), channel_id=1, source_target_pairs={{0,8},{1,9},{2,10},{3,11},{4,12},{5,13},{6,14},{7,15},{8,0},{9,1},... | collective-permute-start | bytes 98312 | tf_op jit(solution)/shard_map/ppermute | solution.py:545
  19.3 2.3 %near_part.6.refs_0_ = f32[3456,128]{1,0:T(8,128)S(1)} custom-call(s32[8,128]{1,0:T(8,128)S(4)} %get-tuple-element.27.plan_ref, bf16[3456,128]{1,0:T(8,128)(2,1)S(1)} %get-tuple-element.28.left_ref, bf16[48,3072]{1,0:T(8,128)(2,1)S(1)} %get-tuple-element.29.right_ref, ...), custom_call_target="tpu_custom_call", output_to_operand_aliasing={{}: (4, {})} | custom-call | tf_op jit(solution)/shard_map/near_part/pallas_call | solution.py:356
  21.6 0.9 %collective-permute-done.3 = f32[2,32,128]{2,1,0:T(8,128)S(1)} collective-permute-done((f32[2,32,128]{2,1,0:T(8,128)S(1)}, f32[2,32,128]{2,1,0:T(8,128)S(1)}, u32[]{:S(2)}, u32[]{:S(2)}) %collective-permute-start.3) | collective-permute-done | bytes 32800 | tf_op jit(solution)/shard_map/ppermute | solution.py:545
  22.6 1.8 %collective-permute-start.4 = (f32[1,32,128]{2,1,0:T(8,128)S(1)}, f32[1,32,128]{2,1,0:T(8,128)S(1)}, u32[]{:S(2)}, u32[]{:S(2)}) collective-permute-start(f32[1,32,128]{2,1,0:T(8,128)S(1)} %get-tuple-element.35.refs_1_), channel_id=1, source_target_pairs={{0,16},{1,17},{2,18},{3,19},{4,20},{5,21},{6,22},{7,23},{8,24},{9,... | collective-permute-start | bytes 49160 | tf_op jit(solution)/shard_map/ppermute | solution.py:545
  24.3 0.0 copy-start.1
  24.3 3.4 %near_part.7.near_ref.after_ref = f32[3456,128]{1,0:T(8,128)S(1)} custom-call(s32[8,128]{1,0:T(8,128)S(4)} %get-tuple-element.27.plan_ref, bf16[3456,128]{1,0:T(8,128)(2,1)S(1)} %get-tuple-element.28.left_ref, bf16[48,3072]{1,0:T(8,128)(2,1)S(1)} %get-tuple-element.29.right_ref, ...), custom_call_target="tpu_custom_call", output_to_operand_aliasing={{}: (4, {})} | custom-call | tf_op jit(solution)/shard_map/near_part/pallas_call | solution.py:356
  27.8 0.0 collective-permute-done.4
  27.8 0.0 copy-done.1
  27.8 0.0 copy-start.2
  27.8 0.0 copy-start.3
  27.8 0.0 copy-start.4
  27.8 0.5 %assemble.1 = (f32[32,3072]{1,0:T(8,128)S(1)}, f32[32,128]{1,0:T(8,128)S(1)}) custom-call(f32[8,128]{1,0:T(8,128)S(1)} %spread_scalars.1.scalars_ref, f32[3456,128]{1,0:T(8,128)S(1)} %near_part.7.near_ref.after_ref, f32[32,3072]{1,0:T(8,128)S(1)} %copy-done, f32[32,3072]{1,0:T(8,128)S(1)} %copy-done.1, f32[3456,128]{1,0:T(8,128)S(1)} %near_part.7.near_ref.after_ref), custom_call_target="tpu_custom_call" | custom-call | tf_op jit(solution)/shard_map/assemble/pallas_call | solution.py:382
  28.3 0.0 copy-start.5
  28.3 0.6 %copy-done.2 = bf16[128,3072]{1,0:T(8,128)(2,1)S(1)} copy-done((bf16[128,3072]{1,0:T(8,128)(2,1)S(1)}, bf16[128,3072]{1,0:T(8,128)(2,1)}, u32[]{:S(2)}) %copy-start.2) | copy-done | bytes 786456
  28.9 0.0 copy-done.3
  29.0 0.1 copy-done.4
  29.0 1.9 %descend.1 = (f32[32,3072]{1,0:T(8,128)S(1)}, f32[32,1,256]{2,1,0:T(1,128)S(1)}) custom-call(s32[1,4]{1,0:T(1,128)S(1)} %copy-done.8, f32[32,3072]{1,0:T(8,128)S(1)} %get-tuple-element.38.base_ref, f32[32,128]{1,0:T(8,128)S(1)} %get-tuple-element.39.old_ref, f32[32,3072]{1,0:T(8,128)S(1)} %copy-done, f32[32,3072]{1,0:T(8,128)S(1)} %copy-done.1, ...), custom_call_target="tpu_custom_call" | custom-call | tf_op jit(solution)/shard_map/descend/pallas_call | solution.py:483
  30.9 10.6 %all_to_all.5.sums_ref = f32[32,1,256]{2,1,0:T(1,128)S(1)} all-to-all(f32[32,1,256]{2,1,0:T(1,128)S(1)} %get-tuple-element.43), channel_id=1, replica_groups=mesh['leaf'=32] {'leaf'}, dimensions={0} | all-to-all | bytes 65536 | tf_op jit(solution)/shard_map/all_to_all | solution.py:598
  41.6 0.0 copy-done.5
  41.6 1.3 %finish.1 = (f32[32,3072]{1,0:T(8,128)}, f32[32,3072]{1,0:T(8,128)}, f32[32,3072]{1,0:T(8,128)}) custom-call(f32[32,1,256]{2,1,0:T(1,128)S(1)} %all_to_all.5.sums_ref, f32[32,3072]{1,0:T(8,128)S(1)} %copy-done.5, f32[32,3072]{1,0:T(8,128)S(1)} %copy-done.1, f32[32,3072]{1,0:T(8,128)S(1)} %copy-done, f32[32,3072]{1,0:T(8,128)S(1)} %get-tuple-element.44.a_ref), custom_call_target="tpu_custom_call" | custom-call | tf_op jit(solution)/shard_map/finish/pallas_call | solution.py:533
  (13 shorter events, 0.1 us)
Async XLA Ops:
  0.6 8.5 %copy-start = (f32[32,3072]{1,0:T(8,128)S(1)}, f32[32,3072]{1,0:T(8,128)}, u32[]{:S(2)}) copy-start(f32[32,3072]{1,0:T(8,128)} %d_ref.7) | copy-start | bytes 1179652
  0.6 8.5 %copy-start.8 = (s32[1,4]{1,0:T(1,128)S(1)}, s32[1,4]{1,0:T(1,128)}, u32[]{:S(2)}) copy-start(s32[1,4]{1,0:T(1,128)} %sizes_ref.3) | copy-start | bytes 52
  0.7 8.4 %copy-start.7 = (s32[3072]{0:T(1024)S(1)}, s32[3072]{0:T(1024)}, u32[]{:S(2)}) copy-start(s32[3072]{0:T(1024)} %param.18) | copy-start | bytes 36868
  0.7 8.4 %copy-start.6 = (f32[3,3072]{1,0:T(4,128)S(1)}, f32[3,3072]{1,0:T(4,128)}, u32[]{:S(2)}) copy-start(f32[3,3072]{1,0:T(4,128)} %coords_ref.1) | copy-start | bytes 110596
  4.0 2.5 %collective-permute-start = (f32[5,32,128]{2,1,0:T(8,128)S(1)}, f32[5,32,128]{2,1,0:T(8,128)S(1)}, u32[]{:S(2)}, u32[]{:S(2)}) collective-permute-start(f32[5,32,128]{2,1,0:T(8,128)S(1)} %get-tuple-element.24.after_ref), channel_id=1, source_target_pairs={{0,1},{1,0},{2,3},{3,2},{4,5},{5,4},{6,7},{7,6},{8,9},{9,8},{10,11... | collective-permute-start | bytes 245768 | tf_op jit(solution)/shard_map/ppermute | solution.py:545
  6.5 7.0 %collective-permute-start.1 = (f32[4,32,128]{2,1,0:T(8,128)S(1)}, f32[4,32,128]{2,1,0:T(8,128)S(1)}, u32[]{:S(2)}, u32[]{:S(2)}) collective-permute-start(f32[4,32,128]{2,1,0:T(8,128)S(1)} %slice.32.after_ref.refs_0_), channel_id=1, source_target_pairs={{0,2},{1,3},{2,0},{3,1},{4,6},{5,7},{6,4},{7,5},{8,10},{9,11},{10,... | collective-permute-start | bytes 196616 | tf_op jit(solution)/shard_map/ppermute | solution.py:545
  13.5 5.0 %collective-permute-start.2 = (f32[3,32,128]{2,1,0:T(8,128)S(1)}, f32[3,32,128]{2,1,0:T(8,128)S(1)}, u32[]{:S(2)}, u32[]{:S(2)}) collective-permute-start(f32[3,32,128]{2,1,0:T(8,128)S(1)} %slice.33.refs_1_), channel_id=1, source_target_pairs={{0,4},{1,5},{2,6},{3,7},{4,0},{5,1},{6,2},{7,3},{8,12},{9,13},{10,... | collective-permute-start | bytes 147464 | tf_op jit(solution)/shard_map/ppermute | solution.py:545
  18.6 4.0 %collective-permute-start.3 = (f32[2,32,128]{2,1,0:T(8,128)S(1)}, f32[2,32,128]{2,1,0:T(8,128)S(1)}, u32[]{:S(2)}, u32[]{:S(2)}) collective-permute-start(f32[2,32,128]{2,1,0:T(8,128)S(1)} %slice.34.refs_1_), channel_id=1, source_target_pairs={{0,8},{1,9},{2,10},{3,11},{4,12},{5,13},{6,14},{7,15},{8,0},{9,1},... | collective-permute-start | bytes 98312 | tf_op jit(solution)/shard_map/ppermute | solution.py:545
  22.6 5.2 %collective-permute-start.4 = (f32[1,32,128]{2,1,0:T(8,128)S(1)}, f32[1,32,128]{2,1,0:T(8,128)S(1)}, u32[]{:S(2)}, u32[]{:S(2)}) collective-permute-start(f32[1,32,128]{2,1,0:T(8,128)S(1)} %get-tuple-element.35.refs_1_), channel_id=1, source_target_pairs={{0,16},{1,17},{2,18},{3,19},{4,20},{5,21},{6,22},{7,23},{8,24},{9,... | collective-permute-start | bytes 49160 | tf_op jit(solution)/shard_map/ppermute | solution.py:545
  24.3 3.4 %copy-start.1 = (f32[32,3072]{1,0:T(8,128)S(1)}, f32[32,3072]{1,0:T(8,128)}, u32[]{:S(2)}) copy-start(f32[32,3072]{1,0:T(8,128)} %r_ref.5) | copy-start | bytes 1179652
  27.8 1.1 %copy-start.2 = (bf16[128,3072]{1,0:T(8,128)(2,1)S(1)}, bf16[128,3072]{1,0:T(8,128)(2,1)}, u32[]{:S(2)}) copy-start(bf16[128,3072]{1,0:T(8,128)(2,1)} %basis_ref.1) | copy-start | bytes 2359300
  27.8 1.2 %copy-start.3 = (bf16[1,7,128,128]{3,2,1,0:T(8,128)(2,1)S(1)}, bf16[1,7,128,128]{3,2,1,0:T(8,128)(2,1)}, u32[]{:S(2)}) copy-start(bf16[1,7,128,128]{3,2,1,0:T(8,128)(2,1)} %nt_ref.1) | copy-start | bytes 688132
  27.8 1.2 %copy-start.4 = (bf16[1,7,128,128]{3,2,1,0:T(8,128)(2,1)S(1)}, bf16[1,7,128,128]{3,2,1,0:T(8,128)(2,1)}, u32[]{:S(2)}) copy-start(bf16[1,7,128,128]{3,2,1,0:T(8,128)(2,1)} %nc_ref.1) | copy-start | bytes 688132
  28.3 13.3 %copy-start.5 = (f32[32,3072]{1,0:T(8,128)S(1)}, f32[32,3072]{1,0:T(8,128)}, u32[]{:S(2)}) copy-start(f32[32,3072]{1,0:T(8,128)} %x_ref.1) | copy-start | bytes 1179652

commit v10 on v9

--- a/solution.py
+++ b/solution.py
@@ -22,7 +22,7 @@
 STRIP = 384
 GROUP = 4
 PARTS = 4
-BLOCKS = 3
+SENDS = 6
 PARAMS = pltpu.CompilerParams(vmem_limit_bytes=48 * 1024 * 1024)
 
 
@@ -72,28 +72,19 @@
 
 def up_kernel(leaf_count, levels, *refs):
     sources, (up_ref, local_ref, high_ref, low_ref) = refs[:7], refs[7:11]
-    held, semaphores = refs[11:18], refs[18]
-    sizes_ref, d_ref, basis_ref, nt_ref, nc_ref, ut_ref, uc_ref = held
+    d_ref, basis_ref, nt_ref, nc_ref = refs[11:15]
+    sizes_ref, ut_ref, uc_ref, semaphores = refs[15:]
     probes, points = d_ref.shape
-    block = points // BLOCKS
-
-    def copy(index, place, window=None):
-        source, target = sources[index], held[index]
-        if window is not None:
-            source, target = source.at[:, window], target.at[:, window]
-        return pltpu.make_async_copy(source, target, semaphores.at[place])
-
-    windows = [pl.ds(block * number, block) for number in range(BLOCKS)]
-    first = [copy(0, 0)]
-    blocks = [
-        [copy(1, 1 + 2 * number, window), copy(2, 2 + 2 * number, window)]
-        for number, window in enumerate(windows)
+    copies = [
+        pltpu.make_async_copy(source, target, semaphores.at[index])
+        for index, (source, target) in enumerate(
+            zip(sources, (sizes_ref, d_ref, basis_ref, nt_ref, nc_ref, ut_ref, uc_ref))
+        )
     ]
-    others = [copy(index, 2 * BLOCKS + index - 2) for index in range(3, 7)]
-    for pending in others + first + sum(blocks, []):
-        pending.start()
-    for pending in others:
-        pending.wait()
+    for copy in copies:
+        copy.start()
+    for copy in copies:
+        copy.wait()
     rank = basis_ref.shape[0]
     images = [nc_ref[0, 0].astype(F32)]
     path = nt_ref[0, 0].astype(F32)
@@ -110,21 +101,16 @@
     low = (images - high.astype(F32)).astype(BF16)
     high_ref[...] = high
     low_ref[...] = low
-    first[0].wait()
     ends = leaf_ends(sizes_ref, leaf_count)
-    raw = jnp.zeros((2 * probes * leaf_count, basis_ref.shape[0]), F32)
-    for number, window in enumerate(windows):
-        for pending in blocks[number]:
-            pending.wait()
-        split = halves(d_ref[:, window])
-        leaf = leaf_row(ends, block * number, split.shape)
-        zero = jnp.zeros_like(split)
-        masked = jnp.concatenate(
-            [jnp.where(leaf == index, split, zero) for index in range(leaf_count)], axis=0
-        )
-        raw = raw + lax.dot_general(
-            masked, basis_ref[:, window], (((1,), (1,)), ((), ())), preferred_element_type=F32
-        )
+    split = halves(d_ref[...])
+    leaf = leaf_row(ends, 0, split.shape)
+    zero = jnp.zeros_like(split)
+    masked = jnp.concatenate(
+        [jnp.where(leaf == index, split, zero) for index in range(leaf_count)], axis=0
+    )
+    raw = lax.dot_general(
+        masked, basis_ref[...], (((1,), (1,)), ((), ())), preferred_element_type=F32
+    )
     current = [
         folded(raw[2 * probes * index : 2 * probes * (index + 1)]) for index in range(leaf_count)
     ]
@@ -156,12 +142,15 @@
             jax.ShapeDtypeStruct((leaf_count - 1, probes, rank), F32),
             jax.ShapeDtypeStruct((rank, rank * levels), BF16),
             jax.ShapeDtypeStruct((rank, rank * levels), BF16),
+            *(jax.ShapeDtypeStruct(array.shape, array.dtype) for array in vectors[:4]),
         ),
         in_specs=[HBM] * len(arrays),
-        out_specs=(VMEM,) * 4,
-        scratch_shapes=[pltpu.SMEM(sizes.shape, sizes.dtype)]
-        + [pltpu.VMEM(array.shape, array.dtype) for array in vectors]
-        + [pltpu.SemaphoreType.DMA((2 * BLOCKS + 5,))],
+        out_specs=(VMEM,) * 8,
+        scratch_shapes=[
+            pltpu.SMEM(sizes.shape, sizes.dtype),
+            *(pltpu.VMEM(array.shape, array.dtype) for array in vectors[4:]),
+            pltpu.SemaphoreType.DMA((len(arrays),)),
+        ],
         compiler_params=PARAMS,
         name="climb",
     )(*(pltpu.with_memory_space_constraint(array, pltpu.HBM) for array in arrays))
@@ -185,6 +174,10 @@
 ):
     points = coords_ref.shape[1]
     chunks = points // 128
+    ends = leaf_ends(sizes_ref, leaf_count)
+    list_ref[...] = near_plan(ends, points // TILE)
+    handed = pltpu.make_async_copy(list_ref, plan_ref, semaphore.at[0])
+    handed.start()
     ordered_ref[...] = jnp.zeros_like(ordered_ref)
     for group in range(chunks // 8):
         order = order_ref[8 * group : 8 * group + 8, :]
@@ -211,10 +204,6 @@
     n1 = norm.astype(BF16).astype(F32)
     n2 = (norm - n1).astype(BF16).astype(F32)
     n3 = norm - n1 - n2
-    ends = leaf_ends(sizes_ref, leaf_count)
-    list_ref[...] = near_plan(ends, points // TILE)
-    handed = pltpu.make_async_copy(list_ref, plan_ref, semaphore.at[0])
-    handed.start()
     leaf = leaf_row(ends, 0, (8, points))
     parts = jnp.where(row8 % 3 == 0, n1, jnp.where(row8 % 3 == 1, n2, n3))
     norm_left = jnp.where(row8 < 3, parts, jnp.where(row8 < 6, 1.0, 0.0))
@@ -505,7 +494,8 @@
     return jnp.sum(values * factor, axis=0), top
 
 
-def step_kernel(sums_ref, x_ref, r_ref, d_ref, a_ref, nx_ref, nr_ref, nd_ref):
+def step_kernel(sums_ref, x_ref, r_ref, d_ref, a_ref, *refs):
+    targets, held, semaphores = refs[:3], refs[3:6], refs[6]
     probes = d_ref.shape[0]
     total, top = merged(sums_ref[...], probes)
     lane = lax.broadcasted_iota(jnp.int32, (probes, 128), 1)
@@ -521,11 +511,26 @@
     reach = step * column(top, 0)
     fresh = old - 2.0 * (reach * cross) + (reach * reach) * square
     beta = fresh / old
-    d = d_ref[...]
-    nx_ref[...] = x_ref[...] + step * d
-    remaining = r_ref[...] - step * a_ref[...]
-    nr_ref[...] = remaining
-    nd_ref[...] = remaining + beta * d
+    points = d_ref.shape[1]
+    width = points // SENDS
+    copies = []
+    for number in range(SENDS):
+        window = pl.ds(width * number, width)
+        d = d_ref[:, window]
+        remaining = r_ref[:, window] - step * a_ref[:, window]
+        held[0][:, window] = x_ref[:, window] + step * d
+        held[1][:, window] = remaining
+        held[2][:, window] = remaining + beta * d
+        for index in range(3):
+            copy = pltpu.make_async_copy(
+                held[index].at[:, window],
+                targets[index].at[:, window],
+                semaphores.at[3 * number + index],
+            )
+            copy.start()
+            copies.append(copy)
+    for copy in copies:
+        copy.wait()
 
 
 def finish(sums, solution_block, residual, direction, applied):
@@ -534,7 +539,9 @@
         step_kernel,
         out_shape=(shape, shape, shape),
         in_specs=[VMEM] * 5,
-        out_specs=(VMEM, VMEM, VMEM),
+        out_specs=(HBM, HBM, HBM),
+        scratch_shapes=[pltpu.VMEM(direction.shape, F32)] * 3
+        + [pltpu.SemaphoreType.DMA((3 * SENDS,))],
         compiler_params=PARAMS,
         name="finish",
     )(sums, solution_block, residual, direction, applied)
@@ -563,7 +570,7 @@
 ):
     levels = lax.axis_size("leaf").bit_length() - 1
     probes, points = direction.shape
-    up, local, *images = climb(
+    up, local, high, low, direction, leaf_basis, node_transfer, node_coupling = climb(
         leaf_sizes,
         (direction, leaf_basis, node_transfer, node_coupling, upper_transfer, upper_coupling),
         levels,
@@ -582,18 +589,20 @@
             )
         if 1 <= level <= PARTS:
             near = (near_part(prepared, near, current, level - 1),)
+        if level == PARTS:
+            base, old = assemble(scalars, near[0], direction, residual, near[0])
+            current, base, old = lax.optimization_barrier((current, base, old))
         if level < levels:
             current = current + incoming
             sides.append(current[0])
             current = current[1:] if level + 1 < levels else current
             if level == 0:
                 current, scalars = lax.optimization_barrier((current, scalars))
-            elif level <= PARTS:
+            elif level < PARTS:
                 current, *near = lax.optimization_barrier((current, *near))
-    base, old = assemble(scalars, near[0], direction, residual, near[0])
     applied, sums = descend(
         leaf_sizes, base, old, direction, residual, leaf_basis,
-        node_transfer, node_coupling, images, local, sides,
+        node_transfer, node_coupling, (high, low), local, sides,
     )
     gathered = lax.all_to_all(sums, "leaf", 0, 0, tiled=True)
     return finish(gathered, solution, residual, direction, applied)

time: 43 us -> 41.8 us (0.972)
  starting transfers between devices: 7.2 us -> 9.83 us
  blocking collectives: 10.6 us -> 9.31 us
  Pallas kernels: 20.4 us -> 19.2 us
  local copies, waits for them, and re-layouts: 0.79 us -> 0.05 us
  waiting for transfers between devices: 0.94 us -> 0.29 us
    ppermute x5, starting transfers between devices: 7.2 us -> 9.83 us  [from_partner(): return lax.ppermute(array, 'leaf', [(i, i ^ stride) for i in range(count)])]
    all_to_all x1, blocking collectives: 10.6 us -> 9.31 us  [shards(): gathered = lax.all_to_all(sums, 'leaf', 0, 0, tiled=True)]
    pallas_call x4, Pallas kernels: 11.5 us -> 10.4 us  [near_part(): pl.pallas_call(functools.partial(near_kernel, part), out_shape=jax.ShapeD...]
    unnamed x18 -> x10, local copies, waits for them, and re-layouts: 0.77 us -> 0.02 us
    ppermute x5, waiting for transfers between devices: 0.94 us -> 0.29 us  [from_partner(): return lax.ppermute(array, 'leaf', [(i, i ^ stride) for i in range(count)])]
where the time goes in v10:
time: 41.8 us; the launch traced here: 41.6 us
  Pallas kernels  19.2 us (46%)
  starting transfers between devices  9.83 us (24%)
  blocking collectives  9.31 us (22%)
  between operations  2.79 us (7%)
    pallas_call x4, Pallas kernels, near_part(): pl.pallas_call(functools.partial(near_kernel, part), out_shape=jax.ShapeD...  10.4 us
    ppermute x5, starting transfers between devices, from_partner(): return lax.ppermute(array, 'leaf', [(i, i ^ stride) for i in range(count)])  9.83 us
    all_to_all x1, blocking collectives, shards(): gathered = lax.all_to_all(sums, 'leaf', 0, 0, tiled=True)  9.31 us
    pallas_call x1, Pallas kernels, climb(): pl.pallas_call(functools.partial(up_kernel, leaf_count, levels), out_shap...  3.23 us
    pallas_call x1, Pallas kernels, features(): pl.pallas_call(functools.partial(features_kernel, leaf_count), out_shape=...  1.96 us
    pallas_call x1, Pallas kernels, descend(): pl.pallas_call(functools.partial(down_kernel, leaf_count, len(sides)), ou...  1.87 us
    pallas_call x1, Pallas kernels, finish(): pl.pallas_call(step_kernel, out_shape=(shape, shape, shape), in_specs=[VM...  1.36 us
  transfers between devices with their start and end apart: 5, of which 1 were waited for; matrix products, arithmetic and copies ran while one was open for 0% of the time, Pallas kernels for 31%

profile of v10, /device:TPU:0, one launch (start us, length us, event | category | flops | bytes accessed | tf_op | source)
XLA Modules:
  0.0 41.6 jit_solution(5842802151087071276)
XLA Ops:
  0.6 0.0 copy-start.4
  0.6 0.0 copy-start.3
  0.7 0.0 copy-start.2
  0.7 3.2 %climb.1 = (f32[5,32,128]{2,1,0:T(8,128)S(1)}, f32[3,32,128]{2,1,0:T(8,128)S(1)}, bf16[128,640]{1,0:T(8,128)(2,1)S(1)}, bf16[128,640]{1,0:T(8,128)(2,1)S(1)}, f3...) custom-call(s32[1,4]{1,0:T(1,128)} %sizes_ref.3, ...), custom_call_target="tpu_custom_call" | custom-call | tf_op jit(solution)/shard_map/climb/pallas_call | solution.py:138
  3.9 0.5 %collective-permute-start = (f32[5,32,128]{2,1,0:T(8,128)S(1)}, f32[5,32,128]{2,1,0:T(8,128)S(1)}, u32[]{:S(2)}, u32[]{:S(2)}) collective-permute-start(f32[5,32,128]{2,1,0:T(8,128)S(1)} %get-tuple-element.30.after_ref), channel_id=1, source_target_pairs={{0,1},{1,0},{2,3},{3,2},{4,5},{5,4},{6,7},{7,6},{8,9},{9,8},{10,11... | collective-permute-start | bytes 245768 | tf_op jit(solution)/shard_map/ppermute | solution.py:552
  6.4 0.0 collective-permute-done
  6.4 2.6 %collective-permute-start.1 = (f32[4,32,128]{2,1,0:T(8,128)S(1)}, f32[4,32,128]{2,1,0:T(8,128)S(1)}, u32[]{:S(2)}, u32[]{:S(2)}) collective-permute-start(f32[4,32,128]{2,1,0:T(8,128)S(1)} %slice.32.after_ref.refs_0_), channel_id=1, source_target_pairs={{0,2},{1,3},{2,0},{3,1},{4,6},{5,7},{6,4},{7,5},{8,10},{9,11},{10,... | collective-permute-start | bytes 196616 | tf_op jit(solution)/shard_map/ppermute | solution.py:552
  9.0 0.0 copy-done.4
  9.0 0.0 copy-done.3
  9.0 0.0 copy-done.2
  9.0 2.0 %features.1 = (bf16[3456,128]{1,0:T(8,128)(2,1)S(1)}, bf16[48,3072]{1,0:T(8,128)(2,1)S(1)}, bf16[3328,128]{1,0:T(8,128)(2,1)S(1)}, s32[8,128]{1,0:T(8,128)S(4)}) custom-call(s32[1,4]{1,0:T(1,128)S(1)} %copy-done.4, f32[8,128]{1,0:T(8,128)S(1)} %spread_scalars.1.scalars_ref, f32[3,3072]{1,0:T(4,128)S(1)} %copy-done.2, s32[24,128]{1,0:T(8,128)S(1)} %bitcast.11, ...), custom_call_target="tpu_custom_call" | custom-call | tf_op jit(solution)/shard_map/features/pallas_call | solution.py:253
  11.0 2.4 %near_part.4.refs_0_ = f32[3456,128]{1,0:T(8,128)S(1)} custom-call(s32[8,128]{1,0:T(8,128)S(4)} %get-tuple-element.34.plan_ref, bf16[3456,128]{1,0:T(8,128)(2,1)S(1)} %get-tuple-element.35.left_ref, bf16[48,3072]{1,0:T(8,128)(2,1)S(1)} %get-tuple-element.36.right_ref, bf16[3328,128]{1,0:T(8,128)(2,1)S(1)} %get-tuple-element.37.dd_ref, ...), custom_call_target="tpu_custom_call" | custom-call | tf_op jit(solution)/shard_map/near_part/pallas_call | solution.py:345
  13.4 0.0 collective-permute-done.1
  13.4 1.6 %collective-permute-start.2 = (f32[3,32,128]{2,1,0:T(8,128)S(1)}, f32[3,32,128]{2,1,0:T(8,128)S(1)}, u32[]{:S(2)}, u32[]{:S(2)}) collective-permute-start(f32[3,32,128]{2,1,0:T(8,128)S(1)} %slice.33.refs_1_), channel_id=1, source_target_pairs={{0,4},{1,5},{2,6},{3,7},{4,0},{5,1},{6,2},{7,3},{8,12},{9,13},{10,... | collective-permute-start | bytes 147464 | tf_op jit(solution)/shard_map/ppermute | solution.py:552
  15.0 2.3 %near_part.5.refs_0_ = f32[3456,128]{1,0:T(8,128)S(1)} custom-call(s32[8,128]{1,0:T(8,128)S(4)} %get-tuple-element.34.plan_ref, bf16[3456,128]{1,0:T(8,128)(2,1)S(1)} %get-tuple-element.35.left_ref, bf16[48,3072]{1,0:T(8,128)(2,1)S(1)} %get-tuple-element.36.right_ref, ...), custom_call_target="tpu_custom_call", output_to_operand_aliasing={{}: (4, {})} | custom-call | tf_op jit(solution)/shard_map/near_part/pallas_call | solution.py:345
  17.3 0.3 collective-permute-done.2
  17.6 2.5 %collective-permute-start.3 = (f32[2,32,128]{2,1,0:T(8,128)S(1)}, f32[2,32,128]{2,1,0:T(8,128)S(1)}, u32[]{:S(2)}, u32[]{:S(2)}) collective-permute-start(f32[2,32,128]{2,1,0:T(8,128)S(1)} %slice.34.refs_1_), channel_id=1, source_target_pairs={{0,8},{1,9},{2,10},{3,11},{4,12},{5,13},{6,14},{7,15},{8,0},{9,1},... | collective-permute-start | bytes 98312 | tf_op jit(solution)/shard_map/ppermute | solution.py:552
  20.1 2.3 %near_part.6.refs_0_ = f32[3456,128]{1,0:T(8,128)S(1)} custom-call(s32[8,128]{1,0:T(8,128)S(4)} %get-tuple-element.34.plan_ref, bf16[3456,128]{1,0:T(8,128)(2,1)S(1)} %get-tuple-element.35.left_ref, bf16[48,3072]{1,0:T(8,128)(2,1)S(1)} %get-tuple-element.36.right_ref, ...), custom_call_target="tpu_custom_call", output_to_operand_aliasing={{}: (4, {})} | custom-call | tf_op jit(solution)/shard_map/near_part/pallas_call | solution.py:345
  22.4 0.0 collective-permute-done.3
  22.4 2.7 %collective-permute-start.4 = (f32[1,32,128]{2,1,0:T(8,128)S(1)}, f32[1,32,128]{2,1,0:T(8,128)S(1)}, u32[]{:S(2)}, u32[]{:S(2)}) collective-permute-start(f32[1,32,128]{2,1,0:T(8,128)S(1)} %get-tuple-element.54.refs_1_), channel_id=1, source_target_pairs={{0,16},{1,17},{2,18},{3,19},{4,20},{5,21},{6,22},{7,23},{8,24},{9,... | collective-permute-start | bytes 49160 | tf_op jit(solution)/shard_map/ppermute | solution.py:552
  25.1 0.0 copy-start
  25.1 3.4 %near_part.7.near_ref.after_ref = f32[3456,128]{1,0:T(8,128)S(1)} custom-call(s32[8,128]{1,0:T(8,128)S(4)} %get-tuple-element.34.plan_ref, bf16[3456,128]{1,0:T(8,128)(2,1)S(1)} %get-tuple-element.35.left_ref, bf16[48,3072]{1,0:T(8,128)(2,1)S(1)} %get-tuple-element.36.right_ref, ...), custom_call_target="tpu_custom_call", output_to_operand_aliasing={{}: (4, {})} | custom-call | tf_op jit(solution)/shard_map/near_part/pallas_call | solution.py:345
  28.5 0.0 copy-done
  28.5 0.5 %assemble.1 = (f32[32,3072]{1,0:T(8,128)S(1)}, f32[32,128]{1,0:T(8,128)S(1)}) custom-call(f32[8,128]{1,0:T(8,128)S(1)} %spread_scalars.1.scalars_ref, f32[3456,128]{1,0:T(8,128)S(1)} %near_part.7.near_ref.after_ref, f32[32,3072]{1,0:T(8,128)S(1)} %get-tuple-element.33.d_ref, f32[32,3072]{1,0:T(8,128)S(1)} %copy-done, f32[3456,128]{1,0:T(8,128)S(1)} %near_part.7.near_ref.after_ref), custom_call_target="tpu_custom_call" | custom-call | tf_op jit(solution)/shard_map/assemble/pallas_call | solution.py:371
  29.0 0.0 copy-start.1
  29.0 0.0 collective-permute-done.4
  29.0 1.9 %descend.1 = (f32[32,3072]{1,0:T(8,128)S(1)}, f32[32,1,256]{2,1,0:T(1,128)S(1)}) custom-call(s32[1,4]{1,0:T(1,128)S(1)} %copy-done.4, f32[32,3072]{1,0:T(8,128)S(1)} %get-tuple-element.46.base_ref, f32[32,128]{1,0:T(8,128)S(1)} %get-tuple-element.47.old_ref, f32[32,3072]{1,0:T(8,128)S(1)} %get-tuple-element.33.d_ref, f32[32,3072]{1,0:T(8,128)S(1)} %copy-done, ...), custom_call_target="tpu_custom_call" | custom-call | tf_op jit(solution)/shard_map/descend/pallas_call | solution.py:472
  30.9 9.3 %all_to_all.5.sums_ref = f32[32,1,256]{2,1,0:T(1,128)S(1)} all-to-all(f32[32,1,256]{2,1,0:T(1,128)S(1)} %get-tuple-element.55), channel_id=1, replica_groups=mesh['leaf'=32] {'leaf'}, dimensions={0} | all-to-all | bytes 65536 | tf_op jit(solution)/shard_map/all_to_all | solution.py:607
  40.2 0.0 copy-done.1
  40.2 1.4 %finish.1 = (f32[32,3072]{1,0:T(8,128)}, f32[32,3072]{1,0:T(8,128)}, f32[32,3072]{1,0:T(8,128)}) custom-call(f32[32,1,256]{2,1,0:T(1,128)S(1)} %all_to_all.5.sums_ref, f32[32,3072]{1,0:T(8,128)S(1)} %copy-done.1, f32[32,3072]{1,0:T(8,128)S(1)} %copy-done, f32[32,3072]{1,0:T(8,128)S(1)} %get-tuple-element.33.d_ref, f32[32,3072]{1,0:T(8,128)S(1)} %get-tuple-element.56.a_ref), custom_call_target="tpu_custom_call" | custom-call | tf_op jit(solution)/shard_map/finish/pallas_call | solution.py:538
  (13 shorter events, 0.1 us)
Async XLA Ops:
  0.6 8.4 %copy-start.4 = (s32[1,4]{1,0:T(1,128)S(1)}, s32[1,4]{1,0:T(1,128)}, u32[]{:S(2)}) copy-start(s32[1,4]{1,0:T(1,128)} %sizes_ref.3) | copy-start | bytes 52
  0.6 8.3 %copy-start.3 = (s32[3072]{0:T(1024)S(1)}, s32[3072]{0:T(1024)}, u32[]{:S(2)}) copy-start(s32[3072]{0:T(1024)} %param.18) | copy-start | bytes 36868
  0.7 8.3 %copy-start.2 = (f32[3,3072]{1,0:T(4,128)S(1)}, f32[3,3072]{1,0:T(4,128)}, u32[]{:S(2)}) copy-start(f32[3,3072]{1,0:T(4,128)} %coords_ref.1) | copy-start | bytes 110596
  3.9 2.5 %collective-permute-start = (f32[5,32,128]{2,1,0:T(8,128)S(1)}, f32[5,32,128]{2,1,0:T(8,128)S(1)}, u32[]{:S(2)}, u32[]{:S(2)}) collective-permute-start(f32[5,32,128]{2,1,0:T(8,128)S(1)} %get-tuple-element.30.after_ref), channel_id=1, source_target_pairs={{0,1},{1,0},{2,3},{3,2},{4,5},{5,4},{6,7},{7,6},{8,9},{9,8},{10,11... | collective-permute-start | bytes 245768 | tf_op jit(solution)/shard_map/ppermute | solution.py:552
  6.4 6.9 %collective-permute-start.1 = (f32[4,32,128]{2,1,0:T(8,128)S(1)}, f32[4,32,128]{2,1,0:T(8,128)S(1)}, u32[]{:S(2)}, u32[]{:S(2)}) collective-permute-start(f32[4,32,128]{2,1,0:T(8,128)S(1)} %slice.32.after_ref.refs_0_), channel_id=1, source_target_pairs={{0,2},{1,3},{2,0},{3,1},{4,6},{5,7},{6,4},{7,5},{8,10},{9,11},{10,... | collective-permute-start | bytes 196616 | tf_op jit(solution)/shard_map/ppermute | solution.py:552
  13.4 4.2 %collective-permute-start.2 = (f32[3,32,128]{2,1,0:T(8,128)S(1)}, f32[3,32,128]{2,1,0:T(8,128)S(1)}, u32[]{:S(2)}, u32[]{:S(2)}) collective-permute-start(f32[3,32,128]{2,1,0:T(8,128)S(1)} %slice.33.refs_1_), channel_id=1, source_target_pairs={{0,4},{1,5},{2,6},{3,7},{4,0},{5,1},{6,2},{7,3},{8,12},{9,13},{10,... | collective-permute-start | bytes 147464 | tf_op jit(solution)/shard_map/ppermute | solution.py:552
  17.6 4.8 %collective-permute-start.3 = (f32[2,32,128]{2,1,0:T(8,128)S(1)}, f32[2,32,128]{2,1,0:T(8,128)S(1)}, u32[]{:S(2)}, u32[]{:S(2)}) collective-permute-start(f32[2,32,128]{2,1,0:T(8,128)S(1)} %slice.34.refs_1_), channel_id=1, source_target_pairs={{0,8},{1,9},{2,10},{3,11},{4,12},{5,13},{6,14},{7,15},{8,0},{9,1},... | collective-permute-start | bytes 98312 | tf_op jit(solution)/shard_map/ppermute | solution.py:552
  22.4 6.6 %collective-permute-start.4 = (f32[1,32,128]{2,1,0:T(8,128)S(1)}, f32[1,32,128]{2,1,0:T(8,128)S(1)}, u32[]{:S(2)}, u32[]{:S(2)}) collective-permute-start(f32[1,32,128]{2,1,0:T(8,128)S(1)} %get-tuple-element.54.refs_1_), channel_id=1, source_target_pairs={{0,16},{1,17},{2,18},{3,19},{4,20},{5,21},{6,22},{7,23},{8,24},{9,... | collective-permute-start | bytes 49160 | tf_op jit(solution)/shard_map/ppermute | solution.py:552
  25.1 3.4 %copy-start = (f32[32,3072]{1,0:T(8,128)S(1)}, f32[32,3072]{1,0:T(8,128)}, u32[]{:S(2)}) copy-start(f32[32,3072]{1,0:T(8,128)} %r_ref.5) | copy-start | bytes 1179652
  29.0 11.2 %copy-start.1 = (f32[32,3072]{1,0:T(8,128)S(1)}, f32[32,3072]{1,0:T(8,128)}, u32[]{:S(2)}) copy-start(f32[32,3072]{1,0:T(8,128)} %x_ref.1) | copy-start | bytes 1179652

commit v11 on v10

--- a/solution.py
+++ b/solution.py
@@ -72,8 +72,8 @@
 
 def up_kernel(leaf_count, levels, *refs):
     sources, (up_ref, local_ref, high_ref, low_ref) = refs[:7], refs[7:11]
-    d_ref, basis_ref, nt_ref, nc_ref = refs[11:15]
-    sizes_ref, ut_ref, uc_ref, semaphores = refs[15:]
+    d_ref, basis_ref, nt_ref, nc_ref, plan_ref = refs[11:16]
+    sizes_ref, ut_ref, uc_ref, list_ref, semaphores = refs[16:]
     probes, points = d_ref.shape
     copies = [
         pltpu.make_async_copy(source, target, semaphores.at[index])
@@ -83,7 +83,12 @@
     ]
     for copy in copies:
         copy.start()
-    for copy in copies:
+    copies[0].wait()
+    ends = leaf_ends(sizes_ref, leaf_count)
+    list_ref[...] = near_plan(ends, points // TILE)
+    handed = pltpu.make_async_copy(list_ref, plan_ref, semaphores.at[len(copies)])
+    handed.start()
+    for copy in copies[1:]:
         copy.wait()
     rank = basis_ref.shape[0]
     images = [nc_ref[0, 0].astype(F32)]
@@ -101,7 +106,6 @@
     low = (images - high.astype(F32)).astype(BF16)
     high_ref[...] = high
     low_ref[...] = low
-    ends = leaf_ends(sizes_ref, leaf_count)
     split = halves(d_ref[...])
     leaf = leaf_row(ends, 0, split.shape)
     zero = jnp.zeros_like(split)
@@ -129,6 +133,7 @@
     image = times(current[0], high) + times(current[0], low)
     for level in range(levels):
         up_ref[level] = image[:, rank * level : rank * (level + 1)]
+    handed.wait()
 
 
 def climb(sizes, vectors, levels):
@@ -143,13 +148,15 @@
             jax.ShapeDtypeStruct((rank, rank * levels), BF16),
             jax.ShapeDtypeStruct((rank, rank * levels), BF16),
             *(jax.ShapeDtypeStruct(array.shape, array.dtype) for array in vectors[:4]),
+            pltpu.SMEM((8, 128), jnp.int32),
         ),
         in_specs=[HBM] * len(arrays),
-        out_specs=(VMEM,) * 8,
+        out_specs=(VMEM,) * 8 + (SMEM,),
         scratch_shapes=[
             pltpu.SMEM(sizes.shape, sizes.dtype),
             *(pltpu.VMEM(array.shape, array.dtype) for array in vectors[4:]),
-            pltpu.SemaphoreType.DMA((len(arrays),)),
+            pltpu.VMEM((8, 128), jnp.int32),
+            pltpu.SemaphoreType.DMA((len(arrays) + 1,)),
         ],
         compiler_params=PARAMS,
         name="climb",
@@ -167,17 +174,11 @@
     left_ref,
     right_ref,
     dd_ref,
-    plan_ref,
     ordered_ref,
-    list_ref,
-    semaphore,
 ):
     points = coords_ref.shape[1]
     chunks = points // 128
     ends = leaf_ends(sizes_ref, leaf_count)
-    list_ref[...] = near_plan(ends, points // TILE)
-    handed = pltpu.make_async_copy(list_ref, plan_ref, semaphore.at[0])
-    handed.start()
     ordered_ref[...] = jnp.zeros_like(ordered_ref)
     for group in range(chunks // 8):
         order = order_ref[8 * group : 8 * group + 8, :]
@@ -226,25 +227,26 @@
     split = jnp.concatenate([split, jnp.zeros((128 - split.shape[0], points), F32)], axis=0)
     dd_ref[:points, :] = split.T.astype(BF16)
     dd_ref[points:, :] = jnp.zeros((TILE, 128), BF16)
-    handed.wait()
-
-
-def scalars_kernel(length_ref, scale_ref, noise_ref, after_ref, out_ref):
+
+
+def scalars_kernel(*refs):
+    out_ref = refs[-1]
     row = lax.broadcasted_iota(jnp.int32, out_ref.shape, 0)
-    out_ref[...] = jnp.where(
-        row == 0, length_ref[0], jnp.where(row == 1, scale_ref[0], noise_ref[0])
-    )
-
-
-def spread_scalars(lengthscale, outputscale, noise_variance, after):
+    spread = jnp.full(out_ref.shape, refs[0][0])
+    for index, ref in enumerate(refs[1:-2]):
+        spread = jnp.where(row == index + 1, ref[0], spread)
+    out_ref[...] = spread
+
+
+def spread_scalars(scalars, after):
     return pl.pallas_call(
         scalars_kernel,
         out_shape=jax.ShapeDtypeStruct((8, 128), F32),
-        in_specs=[SMEM, SMEM, SMEM, ANY],
+        in_specs=[SMEM] * len(scalars) + [ANY],
         out_specs=VMEM,
         compiler_params=PARAMS,
         name="spread_scalars",
-    )(lengthscale, outputscale, noise_variance, after)
+    )(*scalars, after)
 
 
 def features(sizes, scalars, coordinates, order, direction, after):
@@ -256,15 +258,10 @@
             jax.ShapeDtypeStruct((points + STRIP, 128), BF16),
             jax.ShapeDtypeStruct((48, points), BF16),
             jax.ShapeDtypeStruct((points + TILE, 128), BF16),
-            pltpu.SMEM((8, 128), jnp.int32),
         ),
         in_specs=[SMEM, VMEM, VMEM, VMEM, VMEM, ANY],
-        out_specs=(VMEM, VMEM, VMEM, SMEM),
-        scratch_shapes=[
-            pltpu.VMEM((8, points), F32),
-            pltpu.VMEM((8, 128), jnp.int32),
-            pltpu.SemaphoreType.DMA((1,)),
-        ],
+        out_specs=(VMEM, VMEM, VMEM),
+        scratch_shapes=[pltpu.VMEM((8, points), F32)],
         compiler_params=PARAMS,
         name="features",
     )(sizes, scalars, coordinates, order.reshape(-1, 128), direction, after)
@@ -339,8 +336,8 @@
     )
 
 
-def near_part(prepared, before, after, part):
-    left, right, dd, plan = prepared
+def near_part(plan, prepared, before, after, part):
+    left, right, dd = prepared
     plan = pltpu.with_memory_space_constraint(plan, pltpu.SMEM)
     return pl.pallas_call(
         functools.partial(near_kernel, part),
@@ -353,9 +350,9 @@
     )(plan, left, right, dd, *before, after)
 
 
-def assemble_kernel(scalars_ref, near_ref, d_ref, r_ref, after_ref, base_ref, old_ref):
+def assemble_kernel(scalars_ref, noise_ref, near_ref, d_ref, r_ref, after_ref, base_ref, old_ref):
     probes, points = d_ref.shape
-    noise = scalars_ref[2:3, 0:1]
+    noise = noise_ref[0:1, 0:1]
     near_scale = scalars_ref[1:2, 0:1] * 3.0
     old = jnp.zeros((probes, 128), F32)
     for first in range(0, points, 512):
@@ -367,18 +364,18 @@
     old_ref[...] = old
 
 
-def assemble(scalars, near, direction, residual, after):
+def assemble(scalars, noise, near, direction, residual, after):
     return pl.pallas_call(
         assemble_kernel,
         out_shape=(
             jax.ShapeDtypeStruct(direction.shape, F32),
             jax.ShapeDtypeStruct((direction.shape[0], 128), F32),
         ),
-        in_specs=[VMEM] * 4 + [ANY],
+        in_specs=[VMEM] * 5 + [ANY],
         out_specs=(VMEM, VMEM),
         compiler_params=PARAMS,
         name="assemble",
-    )(scalars, near, direction, residual, after)
+    )(scalars, noise, near, direction, residual, after)
 
 
 def down_kernel(
@@ -570,7 +567,7 @@
 ):
     levels = lax.axis_size("leaf").bit_length() - 1
     probes, points = direction.shape
-    up, local, high, low, direction, leaf_basis, node_transfer, node_coupling = climb(
+    up, local, high, low, direction, leaf_basis, node_transfer, node_coupling, plan = climb(
         leaf_sizes,
         (direction, leaf_basis, node_transfer, node_coupling, upper_transfer, upper_coupling),
         levels,
@@ -582,15 +579,16 @@
         if level < levels:
             incoming = from_partner(current, 2**level)
         if level == 0:
-            scalars = spread_scalars(lengthscale, outputscale, noise_variance, current)
+            scalars = spread_scalars((lengthscale, outputscale), current)
         if level == 1:
+            noise = spread_scalars((noise_variance,), current)
             prepared = features(
                 leaf_sizes, scalars, coordinates, cluster_order, direction, current
             )
         if 1 <= level <= PARTS:
-            near = (near_part(prepared, near, current, level - 1),)
+            near = (near_part(plan, prepared, near, current, level - 1),)
         if level == PARTS:
-            base, old = assemble(scalars, near[0], direction, residual, near[0])
+            base, old = assemble(scalars, noise, near[0], direction, residual, near[0])
             current, base, old = lax.optimization_barrier((current, base, old))
         if level < levels:
             current = current + incoming
@@ -598,6 +596,8 @@
             current = current[1:] if level + 1 < levels else current
             if level == 0:
                 current, scalars = lax.optimization_barrier((current, scalars))
+            elif level == 1:
+                current, noise, *near = lax.optimization_barrier((current, noise, *near))
             elif level < PARTS:
                 current, *near = lax.optimization_barrier((current, *near))
     applied, sums = descend(

time: 41.8 us -> 41.1 us (0.983)
  Pallas kernels: 19.2 us -> 18.6 us
    pallas_call x1, Pallas kernels: 1.96 us -> 1.29 us  [features(): pl.pallas_call(functools.partial(features_kernel, leaf_count), out_shape=...]
  transfers between devices with their start and end apart: 5 -> 5, of which waited for: 1 -> 1; matrix products, arithmetic and copies ran while one was open for 0% -> 0% of each run, Pallas kernels for 31% -> 30%
where the time goes in v11:
time: 41.1 us; the launch traced here: 41 us
  Pallas kernels  18.6 us (45%)
  starting transfers between devices  9.85 us (24%)
  blocking collectives  9.26 us (23%)
  between operations  2.82 us (7%)
    pallas_call x4, Pallas kernels, near_part(): pl.pallas_call(functools.partial(near_kernel, part), out_shape=jax.ShapeD...  10.4 us
    ppermute x5, starting transfers between devices, from_partner(): return lax.ppermute(array, 'leaf', [(i, i ^ stride) for i in range(count)])  9.85 us
    all_to_all x1, blocking collectives, shards(): gathered = lax.all_to_all(sums, 'leaf', 0, 0, tiled=True)  9.26 us
    pallas_call x1, Pallas kernels, climb(): pl.pallas_call(functools.partial(up_kernel, leaf_count, levels), out_shap...  3.25 us
    pallas_call x1, Pallas kernels, descend(): pl.pallas_call(functools.partial(down_kernel, leaf_count, len(sides)), ou...  1.88 us
    pallas_call x1, Pallas kernels, finish(): pl.pallas_call(step_kernel, out_shape=(shape, shape, shape), in_specs=[VM...  1.36 us
    pallas_call x1, Pallas kernels, features(): pl.pallas_call(functools.partial(features_kernel, leaf_count), out_shape=...  1.29 us
  transfers between devices with their start and end apart: 5, of which 1 were waited for; matrix products, arithmetic and copies ran while one was open for 0% of the time, Pallas kernels for 30%

profile of v11, /device:TPU:0, one launch (start us, length us, event | category | flops | bytes accessed | tf_op | source)
XLA Modules:
  0.0 41.0 jit_solution(12465401738732099989)
XLA Ops:
  0.6 0.0 copy-start.4
  0.6 0.0 copy-start.3
  0.7 0.0 copy-start.2
  0.7 3.2 %climb.1 = (f32[5,32,128]{2,1,0:T(8,128)S(1)}, f32[3,32,128]{2,1,0:T(8,128)S(1)}, bf16[128,640]{1,0:T(8,128)(2,1)S(1)}, bf16[128,640]{1,0:T(8,128)(2,1)S(1)}, f3...) custom-call(s32[1,4]{1,0:T(1,128)} %sizes_ref.3, ...), custom_call_target="tpu_custom_call" | custom-call | tf_op jit(solution)/shard_map/climb/pallas_call | solution.py:143
  3.9 0.5 %collective-permute-start = (f32[5,32,128]{2,1,0:T(8,128)S(1)}, f32[5,32,128]{2,1,0:T(8,128)S(1)}, u32[]{:S(2)}, u32[]{:S(2)}) collective-permute-start(f32[5,32,128]{2,1,0:T(8,128)S(1)} %get-tuple-element.31.refs_2_), channel_id=1, source_target_pairs={{0,1},{1,0},{2,3},{3,2},{4,5},{5,4},{6,7},{7,6},{8,9},{9,8},{10,11... | collective-permute-start | bytes 245768 | tf_op jit(solution)/shard_map/ppermute | solution.py:549
  5.7 0.0 collective-permute-done
  5.8 2.6 %collective-permute-start.1 = (f32[4,32,128]{2,1,0:T(8,128)S(1)}, f32[4,32,128]{2,1,0:T(8,128)S(1)}, u32[]{:S(2)}, u32[]{:S(2)}) collective-permute-start(f32[4,32,128]{2,1,0:T(8,128)S(1)} %slice.32.refs_1_.after_ref.refs_0_), channel_id=1, source_target_pairs={{0,2},{1,3},{2,0},{3,1},{4,6},{5,7},{6,4},{7,5},{8,10},{9,11},{10,... | collective-permute-start | bytes 196616 | tf_op jit(solution)/shard_map/ppermute | solution.py:549
  9.0 0.0 copy-done.4
  9.0 0.0 copy-done.3
  9.0 0.0 copy-done.2
  9.0 1.3 %features.1 = (bf16[3456,128]{1,0:T(8,128)(2,1)S(1)}, bf16[48,3072]{1,0:T(8,128)(2,1)S(1)}, bf16[3328,128]{1,0:T(8,128)(2,1)S(1)}) custom-call(s32[1,4]{1,0:T(1,128)S(1)} %copy-done.4, f32[8,128]{1,0:T(8,128)S(1)} %spread_scalars.2.scalars_ref, f32[3,3072]{1,0:T(4,128)S(1)} %copy-done.2, s32[24,128]{1,0:T(8,128)S(1)} %bitcast.11, ...), custom_call_target="tpu_custom_call" | custom-call | tf_op jit(solution)/shard_map/features/pallas_call | solution.py:255
  10.3 2.4 %near_part.4.refs_0_ = f32[3456,128]{1,0:T(8,128)S(1)} custom-call(s32[8,128]{1,0:T(8,128)S(4)} %get-tuple-element.33.plan_ref, bf16[3456,128]{1,0:T(8,128)(2,1)S(1)} %get-tuple-element.36.left_ref, bf16[48,3072]{1,0:T(8,128)(2,1)S(1)} %get-tuple-element.37.right_ref, bf16[3328,128]{1,0:T(8,128)(2,1)S(1)} %get-tuple-element.38.dd_ref, ...), custom_call_target="tpu_custom_call" | custom-call | tf_op jit(solution)/shard_map/near_part/pallas_call | solution.py:342
  12.7 0.0 collective-permute-done.1
  12.8 1.6 %collective-permute-start.2 = (f32[3,32,128]{2,1,0:T(8,128)S(1)}, f32[3,32,128]{2,1,0:T(8,128)S(1)}, u32[]{:S(2)}, u32[]{:S(2)}) collective-permute-start(f32[3,32,128]{2,1,0:T(8,128)S(1)} %slice.33.refs_1_), channel_id=1, source_target_pairs={{0,4},{1,5},{2,6},{3,7},{4,0},{5,1},{6,2},{7,3},{8,12},{9,13},{10,... | collective-permute-start | bytes 147464 | tf_op jit(solution)/shard_map/ppermute | solution.py:549
  14.4 2.3 %near_part.5.refs_0_ = f32[3456,128]{1,0:T(8,128)S(1)} custom-call(s32[8,128]{1,0:T(8,128)S(4)} %get-tuple-element.33.plan_ref, bf16[3456,128]{1,0:T(8,128)(2,1)S(1)} %get-tuple-element.36.left_ref, bf16[48,3072]{1,0:T(8,128)(2,1)S(1)} %get-tuple-element.37.right_ref, ...), custom_call_target="tpu_custom_call", output_to_operand_aliasing={{}: (4, {})} | custom-call | tf_op jit(solution)/shard_map/near_part/pallas_call | solution.py:342
  16.6 0.3 collective-permute-done.2
  17.0 2.5 %collective-permute-start.3 = (f32[2,32,128]{2,1,0:T(8,128)S(1)}, f32[2,32,128]{2,1,0:T(8,128)S(1)}, u32[]{:S(2)}, u32[]{:S(2)}) collective-permute-start(f32[2,32,128]{2,1,0:T(8,128)S(1)} %slice.34.refs_1_), channel_id=1, source_target_pairs={{0,8},{1,9},{2,10},{3,11},{4,12},{5,13},{6,14},{7,15},{8,0},{9,1},... | collective-permute-start | bytes 98312 | tf_op jit(solution)/shard_map/ppermute | solution.py:549
  19.5 2.3 %near_part.6.refs_0_ = f32[3456,128]{1,0:T(8,128)S(1)} custom-call(s32[8,128]{1,0:T(8,128)S(4)} %get-tuple-element.33.plan_ref, bf16[3456,128]{1,0:T(8,128)(2,1)S(1)} %get-tuple-element.36.left_ref, bf16[48,3072]{1,0:T(8,128)(2,1)S(1)} %get-tuple-element.37.right_ref, ...), custom_call_target="tpu_custom_call", output_to_operand_aliasing={{}: (4, {})} | custom-call | tf_op jit(solution)/shard_map/near_part/pallas_call | solution.py:342
  21.8 0.0 collective-permute-done.3
  21.8 2.7 %collective-permute-start.4 = (f32[1,32,128]{2,1,0:T(8,128)S(1)}, f32[1,32,128]{2,1,0:T(8,128)S(1)}, u32[]{:S(2)}, u32[]{:S(2)}) collective-permute-start(f32[1,32,128]{2,1,0:T(8,128)S(1)} %get-tuple-element.56.refs_1_), channel_id=1, source_target_pairs={{0,16},{1,17},{2,18},{3,19},{4,20},{5,21},{6,22},{7,23},{8,24},{9,... | collective-permute-start | bytes 49160 | tf_op jit(solution)/shard_map/ppermute | solution.py:549
  24.5 0.0 copy-start
  24.5 3.4 %near_part.7.near_ref.after_ref = f32[3456,128]{1,0:T(8,128)S(1)} custom-call(s32[8,128]{1,0:T(8,128)S(4)} %get-tuple-element.33.plan_ref, bf16[3456,128]{1,0:T(8,128)(2,1)S(1)} %get-tuple-element.36.left_ref, bf16[48,3072]{1,0:T(8,128)(2,1)S(1)} %get-tuple-element.37.right_ref, ...), custom_call_target="tpu_custom_call", output_to_operand_aliasing={{}: (4, {})} | custom-call | tf_op jit(solution)/shard_map/near_part/pallas_call | solution.py:342
  27.9 0.0 copy-done
  27.9 0.5 %assemble.1 = (f32[32,3072]{1,0:T(8,128)S(1)}, f32[32,128]{1,0:T(8,128)S(1)}) custom-call(f32[8,128]{1,0:T(8,128)S(1)} %spread_scalars.2.scalars_ref, f32[8,128]{1,0:T(8,128)S(1)} %spread_scalars.3.noise_ref, f32[3456,128]{1,0:T(8,128)S(1)} %near_part.7.near_ref.after_ref, f32[32,3072]{1,0:T(8,128)S(1)} %get-tuple-element.35.d_ref, f32[32,3072]{1,0:T(8,128)S(1)} %copy-done, ...), custom_call_target="tpu_custom_call" | custom-call | tf_op jit(solution)/shard_map/assemble/pallas_call | solution.py:368
  28.4 0.0 copy-start.1
  28.4 0.0 collective-permute-done.4
  28.4 1.9 %descend.1 = (f32[32,3072]{1,0:T(8,128)S(1)}, f32[32,1,256]{2,1,0:T(1,128)S(1)}) custom-call(s32[1,4]{1,0:T(1,128)S(1)} %copy-done.4, f32[32,3072]{1,0:T(8,128)S(1)} %get-tuple-element.48.base_ref, f32[32,128]{1,0:T(8,128)S(1)} %get-tuple-element.49.old_ref, f32[32,3072]{1,0:T(8,128)S(1)} %get-tuple-element.35.d_ref, f32[32,3072]{1,0:T(8,128)S(1)} %copy-done, ...), custom_call_target="tpu_custom_call" | custom-call | tf_op jit(solution)/shard_map/descend/pallas_call | solution.py:469
  30.3 9.3 %all_to_all.5.sums_ref = f32[32,1,256]{2,1,0:T(1,128)S(1)} all-to-all(f32[32,1,256]{2,1,0:T(1,128)S(1)} %get-tuple-element.57), channel_id=1, replica_groups=mesh['leaf'=32] {'leaf'}, dimensions={0} | all-to-all | bytes 65536 | tf_op jit(solution)/shard_map/all_to_all | solution.py:607
  39.6 0.0 copy-done.1
  39.6 1.4 %finish.1 = (f32[32,3072]{1,0:T(8,128)}, f32[32,3072]{1,0:T(8,128)}, f32[32,3072]{1,0:T(8,128)}) custom-call(f32[32,1,256]{2,1,0:T(1,128)S(1)} %all_to_all.5.sums_ref, f32[32,3072]{1,0:T(8,128)S(1)} %copy-done.1, f32[32,3072]{1,0:T(8,128)S(1)} %copy-done, f32[32,3072]{1,0:T(8,128)S(1)} %get-tuple-element.35.d_ref, f32[32,3072]{1,0:T(8,128)S(1)} %get-tuple-element.58.a_ref), custom_call_target="tpu_custom_call" | custom-call | tf_op jit(solution)/shard_map/finish/pallas_call | solution.py:535
  (14 shorter events, 0.1 us)
Async XLA Ops:
  0.6 8.4 %copy-start.4 = (s32[1,4]{1,0:T(1,128)S(1)}, s32[1,4]{1,0:T(1,128)}, u32[]{:S(2)}) copy-start(s32[1,4]{1,0:T(1,128)} %sizes_ref.3) | copy-start | bytes 52
  0.6 8.4 %copy-start.3 = (s32[3072]{0:T(1024)S(1)}, s32[3072]{0:T(1024)}, u32[]{:S(2)}) copy-start(s32[3072]{0:T(1024)} %param.18) | copy-start | bytes 36868
  0.7 8.4 %copy-start.2 = (f32[3,3072]{1,0:T(4,128)S(1)}, f32[3,3072]{1,0:T(4,128)}, u32[]{:S(2)}) copy-start(f32[3,3072]{1,0:T(4,128)} %coords_ref.1) | copy-start | bytes 110596
  3.9 1.8 %collective-permute-start = (f32[5,32,128]{2,1,0:T(8,128)S(1)}, f32[5,32,128]{2,1,0:T(8,128)S(1)}, u32[]{:S(2)}, u32[]{:S(2)}) collective-permute-start(f32[5,32,128]{2,1,0:T(8,128)S(1)} %get-tuple-element.31.refs_2_), channel_id=1, source_target_pairs={{0,1},{1,0},{2,3},{3,2},{4,5},{5,4},{6,7},{7,6},{8,9},{9,8},{10,11... | collective-permute-start | bytes 245768 | tf_op jit(solution)/shard_map/ppermute | solution.py:549
  5.8 7.0 %collective-permute-start.1 = (f32[4,32,128]{2,1,0:T(8,128)S(1)}, f32[4,32,128]{2,1,0:T(8,128)S(1)}, u32[]{:S(2)}, u32[]{:S(2)}) collective-permute-start(f32[4,32,128]{2,1,0:T(8,128)S(1)} %slice.32.refs_1_.after_ref.refs_0_), channel_id=1, source_target_pairs={{0,2},{1,3},{2,0},{3,1},{4,6},{5,7},{6,4},{7,5},{8,10},{9,11},{10,... | collective-permute-start | bytes 196616 | tf_op jit(solution)/shard_map/ppermute | solution.py:549
  12.8 4.2 %collective-permute-start.2 = (f32[3,32,128]{2,1,0:T(8,128)S(1)}, f32[3,32,128]{2,1,0:T(8,128)S(1)}, u32[]{:S(2)}, u32[]{:S(2)}) collective-permute-start(f32[3,32,128]{2,1,0:T(8,128)S(1)} %slice.33.refs_1_), channel_id=1, source_target_pairs={{0,4},{1,5},{2,6},{3,7},{4,0},{5,1},{6,2},{7,3},{8,12},{9,13},{10,... | collective-permute-start | bytes 147464 | tf_op jit(solution)/shard_map/ppermute | solution.py:549
  17.0 4.8 %collective-permute-start.3 = (f32[2,32,128]{2,1,0:T(8,128)S(1)}, f32[2,32,128]{2,1,0:T(8,128)S(1)}, u32[]{:S(2)}, u32[]{:S(2)}) collective-permute-start(f32[2,32,128]{2,1,0:T(8,128)S(1)} %slice.34.refs_1_), channel_id=1, source_target_pairs={{0,8},{1,9},{2,10},{3,11},{4,12},{5,13},{6,14},{7,15},{8,0},{9,1},... | collective-permute-start | bytes 98312 | tf_op jit(solution)/shard_map/ppermute | solution.py:549
  21.8 6.6 %collective-permute-start.4 = (f32[1,32,128]{2,1,0:T(8,128)S(1)}, f32[1,32,128]{2,1,0:T(8,128)S(1)}, u32[]{:S(2)}, u32[]{:S(2)}) collective-permute-start(f32[1,32,128]{2,1,0:T(8,128)S(1)} %get-tuple-element.56.refs_1_), channel_id=1, source_target_pairs={{0,16},{1,17},{2,18},{3,19},{4,20},{5,21},{6,22},{7,23},{8,24},{9,... | collective-permute-start | bytes 49160 | tf_op jit(solution)/shard_map/ppermute | solution.py:549
  24.5 3.4 %copy-start = (f32[32,3072]{1,0:T(8,128)S(1)}, f32[32,3072]{1,0:T(8,128)}, u32[]{:S(2)}) copy-start(f32[32,3072]{1,0:T(8,128)} %r_ref.5) | copy-start | bytes 1179652
  28.4 11.2 %copy-start.1 = (f32[32,3072]{1,0:T(8,128)S(1)}, f32[32,3072]{1,0:T(8,128)}, u32[]{:S(2)}) copy-start(f32[32,3072]{1,0:T(8,128)} %x_ref.1) | copy-start | bytes 1179652
